TPU v7x, 32 devices: a whole 2x2x4 slice. The times are simulated.
32 devices in a mesh: replica: 8 (over z, y), tensor: 4 (over x, core).
Axes of the slice: x: 2, y: 2, z: 4, core: 2. Of those that a mesh axis runs over, the one named last changes fastest.
Arguments:
- residual: bfloat16 [1024, 4, 5120], P('replica', None, 'tensor'), may hold values from -3 to 3
- queries: bfloat16 [1024, 4, 2560], P('replica', None, 'tensor'), may hold values from -144 to 144
- new_keys: bfloat16 [1024, 4, 512], P('replica', None, 'tensor'), may hold values from -6 to 6
- new_values: bfloat16 [1024, 4, 512], P('replica', None, 'tensor'), may hold values from -6 to 6
- cache_keys: bfloat16 [1024, 64, 512], P('replica', None, 'tensor'), may hold values from -7 to 7
- cache_values: bfloat16 [1024, 64, 512], P('replica', None, 'tensor'), may hold values from -6 to 6
- cache_lengths: int32 [1024], replicated, may hold values from 2 to 64
- finished: int32 [1024], replicated, may hold values 0 or 1
- partner: int32 [1024], P('replica'), may hold values from 0 to 1023, as said below
- row_slot: int32 [1024], replicated, may hold values from 0 to 3
- fork_table: int32 [8, 4], replicated, may hold values from 0 to 31, as said below
- prompt_keys: bfloat16 [32, 128, 512], P('replica', None, 'tensor'), may hold values from -6 to 6
- prompt_values: bfloat16 [32, 128, 512], P('replica', None, 'tensor'), may hold values from -6 to 6
- prompt_lengths: int32 [32], replicated, may hold values from 32 to 128
- out_proj: bfloat16 [2560, 5120], P('tensor'), may hold values from -0.125 to 0.125
Outputs:
- layer_out: bfloat16 [1024, 4, 5120], P('replica', None, 'tensor')
Inputs may be any that keep to these rules, and one draw needn't show every extreme that they name: partner is an involution; each replica has exactly 4 rows paired with rows of 4 different other replicas, one of them the replica 8 / 2 away, and every other row is paired with itself. `fork_table`: the 4 entries of a replica name prompts of 4 different owners, prompt p being held by replica p // 4.
All inputs are finite; a program needn't handle non-finite values.
Results may differ from a plain program's by a relative error of at most 0.0034.
Values may be sent and summed in bfloat16 or wider, within the bound.
No kernel may reach another device: no remote copies, remote signals or barrier semaphores. Data moves between devices by JAX's collectives and lax.ppermute only.
A program may use at most 128 MiB of HBM per device.

v0:
```python
import math

import jax
import jax.numpy as jnp
from jax import lax
from jax.sharding import PartitionSpec as P

HEAD_DIM = 128


def split_heads(block, kv_heads):
    return block.reshape(block.shape[0], block.shape[1], kv_heads, HEAD_DIM)


def attend(
    queries, new_keys, new_values, pre_keys, pre_values, pre_len, old_keys, old_values, old_len
):
    row_count, step_count = (queries.shape[0], queries.shape[1])
    kv_heads = new_keys.shape[2] // HEAD_DIM
    groups = queries.shape[2] // HEAD_DIM // kv_heads
    query_split = queries.reshape(row_count, step_count, kv_heads, groups, HEAD_DIM)
    score_scale = 1.0 / math.sqrt(HEAD_DIM)
    part_pre = (
        jnp.einsum(
            "bskgd,bpkd->bkgsp",
            query_split,
            split_heads(pre_keys, kv_heads),
            preferred_element_type=jnp.float32,
        )
        * score_scale
    )
    part_old = (
        jnp.einsum(
            "bskgd,bpkd->bkgsp",
            query_split,
            split_heads(old_keys, kv_heads),
            preferred_element_type=jnp.float32,
        )
        * score_scale
    )
    part_new = (
        jnp.einsum(
            "bskgd,btkd->bkgst",
            query_split,
            split_heads(new_keys, kv_heads),
            preferred_element_type=jnp.float32,
        )
        * score_scale
    )
    mask_pre = jnp.arange(pre_keys.shape[1], dtype=jnp.int32)[None, :] < pre_len[:, None]
    mask_old = jnp.arange(old_keys.shape[1], dtype=jnp.int32)[None, :] < old_len[:, None]
    steps_idx = jnp.arange(step_count, dtype=jnp.int32)
    mask_new = steps_idx[None, :] <= steps_idx[:, None]
    part_pre = jnp.where(mask_pre[:, None, None, None, :], part_pre, -jnp.inf)
    part_old = jnp.where(mask_old[:, None, None, None, :], part_old, -jnp.inf)
    part_new = jnp.where(mask_new[None, None, None, :, :], part_new, -jnp.inf)
    scores = jnp.concatenate([part_pre, part_old, part_new], axis=-1)
    row_top = jnp.max(scores, axis=-1, keepdims=True)
    exp_scores = jnp.exp(scores - row_top)
    weights = (exp_scores / jnp.sum(exp_scores, axis=-1, keepdims=True)).astype(jnp.bfloat16)
    len_pre = pre_keys.shape[1]
    len_old = old_keys.shape[1]
    mixed = jnp.einsum(
        "bkgsp,bpkd->bskgd",
        weights[..., :len_pre],
        split_heads(pre_values, kv_heads),
        preferred_element_type=jnp.float32,
    )
    mixed = mixed + jnp.einsum(
        "bkgsp,bpkd->bskgd",
        weights[..., len_pre : len_pre + len_old],
        split_heads(old_values, kv_heads),
        preferred_element_type=jnp.float32,
    )
    mixed = mixed + jnp.einsum(
        "bkgst,btkd->bskgd",
        weights[..., len_pre + len_old :],
        split_heads(new_values, kv_heads),
        preferred_element_type=jnp.float32,
    )
    return mixed.reshape(row_count, step_count, -1)


def body(
    residual,
    queries,
    new_keys,
    new_values,
    cache_keys,
    cache_values,
    cache_lengths,
    finished,
    partner,
    row_slot,
    fork_table,
    prompt_keys,
    prompt_values,
    prompt_lengths,
    out_proj,
):
    local_rows = queries.shape[0]
    peer_count = lax.axis_size("replica")
    where_am = lax.axis_index("replica")
    first_id = where_am * local_rows
    held_count = prompt_keys.shape[0]
    owners = fork_table // held_count
    chosen = owners == where_am
    offsets = jnp.sum(jnp.where(chosen, fork_table % held_count, 0), axis=1)
    has_block = jnp.any(chosen, axis=1)[:, None, None]
    zero_value = jnp.zeros((), prompt_keys.dtype)
    out_keys = jnp.where(has_block, prompt_keys[offsets], zero_value)
    out_values = jnp.where(has_block, prompt_values[offsets], zero_value)
    got_keys, got_values = (
        lax.all_to_all(out_keys, "replica", split_axis=0, concat_axis=0, tiled=True),
        lax.all_to_all(out_values, "replica", split_axis=0, concat_axis=0, tiled=True),
    )
    slot_keys = got_keys[owners[where_am]]
    slot_values = got_values[owners[where_am]]
    my_slots = lax.dynamic_slice_in_dim(row_slot, first_id, local_rows)
    pre_keys = slot_keys[my_slots]
    pre_values = slot_values[my_slots]
    peer_of = partner // local_rows
    moved_row = peer_of != where_am
    pairing = (peer_of[None, :] == jnp.arange(peer_count, dtype=jnp.int32)[:, None]) & moved_row[
        None, :
    ]
    peer_row = jnp.sum(
        jnp.where(pairing, jnp.arange(local_rows, dtype=jnp.int32)[None, :], 0), axis=1
    )
    has_row = jnp.any(pairing, axis=1)[:, None, None]
    from_peer = jnp.where(moved_row, peer_of, 0)
    keep_mask = moved_row[:, None, None]
    zero_value = jnp.zeros((), cache_keys.dtype)
    outgoing = (
        jnp.where(has_row, pre_keys[peer_row], zero_value),
        jnp.where(has_row, pre_values[peer_row], zero_value),
        jnp.where(has_row, cache_keys[peer_row], zero_value),
        jnp.where(has_row, cache_values[peer_row], zero_value),
    )
    received = (
        lax.all_to_all(outgoing[0], "replica", split_axis=0, concat_axis=0, tiled=True),
        lax.all_to_all(outgoing[1], "replica", split_axis=0, concat_axis=0, tiled=True),
        lax.all_to_all(outgoing[2], "replica", split_axis=0, concat_axis=0, tiled=True),
        lax.all_to_all(outgoing[3], "replica", split_axis=0, concat_axis=0, tiled=True),
    )
    use_pre_keys = jnp.where(keep_mask, received[0][from_peer], pre_keys)
    use_pre_values = jnp.where(keep_mask, received[1][from_peer], pre_values)
    use_old_keys = jnp.where(keep_mask, received[2][from_peer], cache_keys)
    use_old_values = jnp.where(keep_mask, received[3][from_peer], cache_values)
    problem = fork_table[partner // local_rows, row_slot[partner]]
    alive = (1 - finished[partner]).astype(jnp.float32)
    pre_len, old_len, alive = (prompt_lengths[problem], cache_lengths[partner], alive)
    result = attend(
        queries,
        new_keys,
        new_values,
        use_pre_keys,
        use_pre_values,
        pre_len,
        use_old_keys,
        use_old_values,
        old_len,
    )
    heads_out = (result * alive[:, None, None]).astype(jnp.bfloat16)
    terms = jnp.einsum("bsh,hd->bsd", heads_out, out_proj, preferred_element_type=jnp.float32)
    summed = lax.psum_scatter(terms, "tensor", scatter_dimension=2, tiled=True)
    return (residual.astype(jnp.float32) + summed).astype(jnp.bfloat16)


def solution(mesh):
    in_specs = (
        P("replica", None, "tensor"),
        P("replica", None, "tensor"),
        P("replica", None, "tensor"),
        P("replica", None, "tensor"),
        P("replica", None, "tensor"),
        P("replica", None, "tensor"),
        P(),
        P(),
        P("replica"),
        P(),
        P(),
        P("replica", None, "tensor"),
        P("replica", None, "tensor"),
        P(),
        P("tensor", None),
    )
    out_specs = P("replica", None, "tensor")
    return jax.shard_map(body, mesh=mesh, in_specs=in_specs, out_specs=out_specs, check_vma=False)
```

profile of v0, /device:TPU:0, one launch (start us, length us, event | category | flops | bytes accessed | tf_op | source)
XLA Modules:
  0.0 232.9 jit_solution(12322986213736866939)
XLA Ops:
  12.0 7.4 %all-to-all-start.2 = ((bf16[8,128,128]{2,1,0:T(8,128)(2,1)}), bf16[8,128,128]{2,1,0:T(8,128)(2,1)S(1)}, u32[]{:S(2)}, u32[]{:S(2)}) async-start(bf16[8,128,128]{2,1,0:T(8,128)(2,1)} %get-tuple-element.15), calls=%async_computation.2 | async-start | bytes 524288 | tf_op jit(solution)/shard_map/all_to_all | solution.py:114
  23.8 2.2 gather_fusion.14
  26.0 2.2 gather_fusion.16
  30.0 6.0 %all-to-all-start = ((bf16[8,128,128]{2,1,0:T(8,128)(2,1)}), bf16[8,128,128]{2,1,0:T(8,128)(2,1)}, u32[]{:S(2)}, u32[]{:S(2)}) async-start(bf16[8,128,128]{2,1,0:T(8,128)(2,1)} %get-tuple-element.14), calls=%async_computation | async-start | bytes 524288 | tf_op jit(solution)/shard_map/all_to_all | solution.py:115
  37.9 1.7 fusion.50
  39.6 5.1 %all-to-all-done = bf16[8,128,128]{2,1,0:T(8,128)(2,1)} async-done(((bf16[8,128,128]{2,1,0:T(8,128)(2,1)}), bf16[8,128,128]{2,1,0:T(8,128)(2,1)}, u32[]{:S(2)}, u32[]{:S(2)}) %all-to-all-start) | async-done | bytes 262176 | tf_op jit(solution)/shard_map/all_to_all | solution.py:115
  44.6 3.4 %all-to-all-start.4 = ((bf16[8,64,128]{2,1,0:T(8,128)(2,1)}), bf16[8,64,128]{2,1,0:T(8,128)(2,1)S(1)}, u32[]{:S(2)}, u32[]{:S(2)}) async-start(bf16[8,64,128]{2,1,0:T(8,128)(2,1)} %get-tuple-element.11), calls=%async_computation.4 | async-start | bytes 262144 | tf_op jit(solution)/shard_map/all_to_all | solution.py:143
  49.1 1.5 gather_fusion.9
  50.7 3.1 %gather_fusion.10 = bf16[128,128,128]{2,1,0:T(8,128)(2,1)} fusion(bf16[4,128,128]{2,1,0:T(8,128)(2,1)S(1)} %gather_fusion.9, s32[1024]{0:T(1024)S(1)} %pad_clamp_fusion.4), kind=kCustom, calls=%fused_computation.10 | custom fusion | bytes 8389120 | tf_op jit(solution)/shard_map/gather | solution.py:120
  53.7 2.8 %gather_fusion.11 = bf16[8,128,128]{2,1,0:T(8,128)(2,1)S(1)} fusion(bf16[128,128,128]{2,1,0:T(8,128)(2,1)} %gather_fusion.10, s32[1024]{0:T(1024)S(1)} %pad_clamp_fusion.3), kind=kCustom, calls=%fused_computation.11 | custom fusion | bytes 524320 | tf_op jit(solution)/shard_map/gather | solution.py:135
  56.5 1.5 gather_fusion.1
  58.1 3.0 %gather_fusion.2 = bf16[128,128,128]{2,1,0:T(8,128)(2,1)} fusion(bf16[4,128,128]{2,1,0:T(8,128)(2,1)S(1)} %gather_fusion.1, s32[1024]{0:T(1024)S(1)} %pad_clamp_fusion.4), kind=kCustom, calls=%fused_computation.2 | custom fusion | bytes 8389120 | tf_op jit(solution)/shard_map/gather | solution.py:121
  61.1 2.8 %gather_fusion.3 = bf16[8,128,128]{2,1,0:T(8,128)(2,1)S(1)} fusion(bf16[128,128,128]{2,1,0:T(8,128)(2,1)} %gather_fusion.2, s32[1024]{0:T(1024)S(1)} %pad_clamp_fusion.3), kind=kCustom, calls=%fused_computation.3 | custom fusion | bytes 524320 | tf_op jit(solution)/shard_map/gather | solution.py:136
  63.9 6.0 %all-to-all-start.5 = ((bf16[8,64,128]{2,1,0:T(8,128)(2,1)}), bf16[8,64,128]{2,1,0:T(8,128)(2,1)S(1)}, u32[]{:S(2)}, u32[]{:S(2)}) async-start(bf16[8,64,128]{2,1,0:T(8,128)(2,1)} %get-tuple-element.10), calls=%async_computation.5 | async-start | bytes 262144 | tf_op jit(solution)/shard_map/all_to_all | solution.py:144
  70.8 6.4 %all-to-all-done.5 = bf16[8,64,128]{2,1,0:T(8,128)(2,1)S(1)} async-done(((bf16[8,64,128]{2,1,0:T(8,128)(2,1)}), bf16[8,64,128]{2,1,0:T(8,128)(2,1)S(1)}, u32[]{:S(2)}, u32[]{:S(2)}) %all-to-all-start.5) | async-done | bytes 131104 | tf_op jit(solution)/shard_map/all_to_all | solution.py:144
  77.2 3.4 %all-to-all-start.3 = ((bf16[8,128,128]{2,1,0:T(8,128)(2,1)}), bf16[8,128,128]{2,1,0:T(8,128)(2,1)S(1)}, u32[]{:S(2)}, u32[]{:S(2)}) async-start(bf16[8,128,128]{2,1,0:T(8,128)(2,1)} %get-tuple-element.13), calls=%async_computation.3 | async-start | bytes 524288 | tf_op jit(solution)/shard_map/all_to_all | solution.py:141
  80.7 2.2 gather_fusion.15
  82.9 2.1 gather_fusion.17
  85.0 5.1 %fusion.52 = (f32[128,5,4]{1,2,0:T(4,128)S(1)}, f32[128,1,5,4,64]{4,2,3,0,1:T(8,128)}) fusion(bf16[128,4,5,128]{3,2,1,0:T(8,128)(2,1)} %copy-done.8, bf16[128,64,128]{2,1,0:T(8,128)(2,1)} %gather_fusion.15, bf16[128,64,128]{2,1,0:T(8,128)(2,1)} %param.19, pred[128]{0:T(512)(128)(4,1)S(1)} %broadcast_compare_fusion.2, pred[128,64]{1,0:T(8,128)(4,1)S(1)} %iota_compare_fusion), kind=kOutput, calls=%fused_computation.119 | convolution fusion | flops 43480576 | bytes 5523584 | tf_op jit(solution)/shard_map/bskgd,bpkd->bkgsp/dot_general | solution.py:33
  90.1 5.9 %all-to-all-start.1 = ((bf16[8,128,128]{2,1,0:T(8,128)(2,1)}), bf16[8,128,128]{2,1,0:T(8,128)(2,1)S(1)}, u32[]{:S(2)}, u32[]{:S(2)}) async-start(bf16[8,128,128]{2,1,0:T(8,128)(2,1)} %get-tuple-element.12), calls=%async_computation.1 | async-start | bytes 524288 | tf_op jit(solution)/shard_map/all_to_all | solution.py:142
  96.3 3.1 %gather_fusion.12 = bf16[128,128,128]{2,1,0:T(8,128)(2,1)} fusion(bf16[8,128,128]{2,1,0:T(8,128)(2,1)S(1)} %all-to-all-done.3, s32[1024]{0:T(1024)S(1)} %pad_clamp_fusion.2), kind=kCustom, calls=%fused_computation.12 | custom fusion | bytes 8389120 | tf_op jit(solution)/shard_map/gather | solution.py:146
  99.4 6.3 %fusion.51 = (f32[128,5,4]{1,2,0:T(4,128)S(1)}, f32[128,1,5,4,128]{4,2,3,0,1:T(8,128)S(1)}) fusion(bf16[128,4,5,128]{3,2,1,0:T(8,128)(2,1)} %copy-done.8, bf16[128,128,128]{2,1,0:T(8,128)(2,1)} %gather_fusion.12, bf16[128,128,128]{2,1,0:T(8,128)(2,1)} %gather_fusion.10, pred[128]{0:T(512)(128)(4,1)S(1)} %broadcast_compare_fusion.2, ...), kind=kOutput, calls=%fused_computation.118 | convolution fusion | flops 86963712 | bytes 10381440 | tf_op jit(solution)/shard_map/bskgd,bpkd->bkgsp/dot_general | solution.py:24
  105.8 2.5 %fusion.28 = f32[128,5,4]{1,2,0:T(4,128)S(1)} fusion(f32[128,5,4]{1,2,0:T(4,128)S(1)} %bitcast.117, f32[128,1,5,4,4]{4,2,3,0,1:T(8,128)S(1)} %get-tuple-element.17, f32[128,1,5,4,64]{4,2,3,0,1:T(8,128)S(1)} %copy-done.6, f32[128,1,5,4,128]{4,2,3,0,1:T(8,128)S(1)} %get-tuple-element.19), kind=kLoop, calls=%fused_computation.49 | loop fusion | flops 2004480 | bytes 2027520 | tf_op jit(solution)/shard_map/reduce_sum | solution.py:60
  108.3 3.5 %divide_convert_fusion = bf16[128,1,5,4,196]{4,2,3,0,1:T(8,128)(2,1)} fusion(f32[128,5,4]{1,2,0:T(4,128)S(1)} %fusion.28, f32[128,5,4]{1,2,0:T(4,128)S(1)} %bitcast.118, f32[128,1,5,4,4]{4,2,3,0,1:T(8,128)S(1)} %get-tuple-element.17, f32[128,1,5,4,64]{4,2,3,0,1:T(8,128)S(1)} %copy-done.6, f32[128,1,5,4,128]{4,2,3,0,1:T(8,128)S(1)} %get-tuple-element.19), kind=kLoop, calls=%fused_computation.27 | loop fusion | flops 2508800 | bytes 3031040 | tf_op jit(solution)/shard_map/convert_element_type | solution.py:60
  111.8 3.1 %gather_fusion.4 = bf16[128,128,128]{2,1,0:T(8,128)(2,1)} fusion(bf16[8,128,128]{2,1,0:T(8,128)(2,1)S(1)} %all-to-all-done.1, s32[1024]{0:T(1024)S(1)} %pad_clamp_fusion.2), kind=kCustom, calls=%fused_computation.4 | custom fusion | bytes 8389120 | tf_op jit(solution)/shard_map/gather | solution.py:147
  114.9 4.9 %fusion.5 = f32[128,128,5,4]{1,2,3,0:T(8,128)S(1)} fusion(bf16[128,128,128]{2,1,0:T(8,128)(2,1)} %gather_fusion.4, bf16[128,128,128]{2,1,0:T(8,128)(2,1)} %gather_fusion.2, pred[128]{0:T(512)(128)(4,1)S(1)} %broadcast_compare_fusion.2, bf16[128,1,5,4,196]{4,2,3,0,1:T(8,128)(2,1)S(1)} %copy-done.7), kind=kOutput, calls=%fused_computation.25 | convolution fusion | flops 85983232 | bytes 10748416 | tf_op jit(solution)/shard_map/bkgsp,bpkd->bskgd/dot_general | solution.py:63
  121.4 2.3 fusion.15
  123.7 1.8 copy.51
  125.5 9.7 %fusion = f32[128,4,5120]{2,0,1:T(8,128)} fusion(bf16[640,5120]{1,0:T(8,128)(2,1)} %param.29, f32[128,4,640]{0,2,1:T(8,128)S(1)} %bitcast.115, f32[128]{0:T(128)S(1)} %subtract_convert_fusion), kind=kOutput, calls=%fused_computation.19 | convolution fusion | flops 3356098560 | bytes 18350592 | tf_op jit(solution)/shard_map/bsh,hd->bsd/dot_general | solution.py:165
  135.2 86.7 %reduce-scatter.2.cloned.1.call-done = f32[128,4,1280]{2,0,1:T(8,128)} async-done(((f32[128,4,5120]{2,0,1:T(8,128)}), f32[128,4,1280]{2,0,1:T(8,128)}) %reduce-scatter.2.cloned.1.call-update) | async-done | bytes 2621456 | tf_op jit(solution)/shard_map/reduce_scatter | solution.py:166
  221.9 2.0 add_convert_fusion
  223.9 2.1 copy.53
  (79 shorter events, 17.2 us)
Async XLA Ops:
  6.5 113.2 %copy-start = (bf16[128,4,128]{2,1,0:T(4,128)(2,1)S(1)}, bf16[128,4,128]{2,1,0:T(4,128)(2,1)}, u32[]{:S(2)}) copy-start(bf16[128,4,128]{2,1,0:T(4,128)(2,1)} %param.18) | copy-start | bytes 393220
  6.5 14.4 %copy-start.2 = (s32[8,4]{0,1:T(4,128)S(1)}, s32[8,4]{0,1:T(4,128)}, u32[]{:S(2)}) copy-start(s32[8,4]{0,1:T(4,128)} %param.25) | copy-start | bytes 388
  6.5 12.9 %copy-start.16 = (s32[128]{0:T(128)S(1)}, s32[128]{0:T(128)}, u32[]{:S(2)}) copy-start(s32[128]{0:T(128)} %param.23) | copy-start | bytes 1540
  6.5 12.9 %copy-start.4 = (s32[1024]{0:T(1024)S(1)}, s32[1024]{0:T(1024)}, u32[]{:S(2)}) copy-start(s32[1024]{0:T(1024)} %param.24) | copy-start | bytes 12292
  6.5 15.9 %copy-start.1 = (s32[32]{0:T(128)S(1)}, s32[32]{0:T(128)}, u32[]{:S(2)}) copy-start(s32[32]{0:T(128)} %param.28) | copy-start | bytes 388
  9.6 18.6 %copy-start.3 = (s32[1024]{0:T(1024)S(1)}, s32[1024]{0:T(1024)}, u32[]{:S(2)}) copy-start(s32[1024]{0:T(1024)} %param.22) | copy-start | bytes 12292
  12.0 24.1 %copy-start.13 = (bf16[128,4,640]{2,1,0:T(4,128)(2,1)S(1)}, bf16[128,4,640]{2,1,0:T(4,128)(2,1)}, u32[]{:S(2)}) copy-start(bf16[128,4,640]{2,1,0:T(4,128)(2,1)} %param.16) | copy-start | bytes 1966084
  12.0 18.0 %all-to-all-start.2 = ((bf16[8,128,128]{2,1,0:T(8,128)(2,1)}), bf16[8,128,128]{2,1,0:T(8,128)(2,1)S(1)}, u32[]{:S(2)}, u32[]{:S(2)}) async-start(bf16[8,128,128]{2,1,0:T(8,128)(2,1)} %get-tuple-element.15), calls=%async_computation.2 | async-start | bytes 524288 | tf_op jit(solution)/shard_map/all_to_all | solution.py:114
  29.1 8.7 %copy-start.15 = (bf16[128,4,128]{2,1,0:T(4,128)(2,1)S(1)}, bf16[128,4,128]{2,1,0:T(4,128)(2,1)}, u32[]{:S(2)}) copy-start(bf16[128,4,128]{2,1,0:T(4,128)(2,1)} %param.17) | copy-start | bytes 393220
  30.0 6.0 %copy-start.14 = (bf16[8,128,128]{2,1,0:T(8,128)(2,1)}, bf16[8,128,128]{2,1,0:T(8,128)(2,1)S(1)}, u32[]{:S(2)}) copy-start(bf16[8,128,128]{2,1,0:T(8,128)(2,1)S(1)} %all-to-all-done.2) | copy-start | bytes 786436
  30.0 14.6 %all-to-all-start = ((bf16[8,128,128]{2,1,0:T(8,128)(2,1)}), bf16[8,128,128]{2,1,0:T(8,128)(2,1)}, u32[]{:S(2)}, u32[]{:S(2)}) async-start(bf16[8,128,128]{2,1,0:T(8,128)(2,1)} %get-tuple-element.14), calls=%async_computation | async-start | bytes 524288 | tf_op jit(solution)/shard_map/all_to_all | solution.py:115
  37.8 11.2 %copy-start.8 = (bf16[128,4,5,128]{3,2,1,0:T(8,128)(2,1)}, bf16[128,4,5,128]{3,2,1,0:T(8,128)(2,1)S(1)}, u32[]{:S(2)}) copy-start(bf16[128,4,5,128]{3,2,1,0:T(8,128)(2,1)S(1)} %copy.46) | copy-start | bytes 1966084
  37.8 10.2 %copy-start.5 = (s32[1024]{0:T(1024)S(1)}, s32[1024]{0:T(1024)}, u32[]{:S(2)}) copy-start(s32[1024]{0:T(1024)} %param.21) | copy-start | bytes 12292
  44.6 19.3 %all-to-all-start.4 = ((bf16[8,64,128]{2,1,0:T(8,128)(2,1)}), bf16[8,64,128]{2,1,0:T(8,128)(2,1)S(1)}, u32[]{:S(2)}, u32[]{:S(2)}) async-start(bf16[8,64,128]{2,1,0:T(8,128)(2,1)} %get-tuple-element.11), calls=%async_computation.4 | async-start | bytes 262144 | tf_op jit(solution)/shard_map/all_to_all | solution.py:143
  63.9 13.4 %all-to-all-start.5 = ((bf16[8,64,128]{2,1,0:T(8,128)(2,1)}), bf16[8,64,128]{2,1,0:T(8,128)(2,1)S(1)}, u32[]{:S(2)}, u32[]{:S(2)}) async-start(bf16[8,64,128]{2,1,0:T(8,128)(2,1)} %get-tuple-element.10), calls=%async_computation.5 | async-start | bytes 262144 | tf_op jit(solution)/shard_map/all_to_all | solution.py:144
  77.2 12.9 %all-to-all-start.3 = ((bf16[8,128,128]{2,1,0:T(8,128)(2,1)}), bf16[8,128,128]{2,1,0:T(8,128)(2,1)S(1)}, u32[]{:S(2)}, u32[]{:S(2)}) async-start(bf16[8,128,128]{2,1,0:T(8,128)(2,1)} %get-tuple-element.13), calls=%async_computation.3 | async-start | bytes 524288 | tf_op jit(solution)/shard_map/all_to_all | solution.py:141
  90.1 21.7 %all-to-all-start.1 = ((bf16[8,128,128]{2,1,0:T(8,128)(2,1)}), bf16[8,128,128]{2,1,0:T(8,128)(2,1)S(1)}, u32[]{:S(2)}, u32[]{:S(2)}) async-start(bf16[8,128,128]{2,1,0:T(8,128)(2,1)} %get-tuple-element.12), calls=%async_computation.1 | async-start | bytes 524288 | tf_op jit(solution)/shard_map/all_to_all | solution.py:142
  96.1 125.8 %reduce-scatter.2.cloned.1.call-start = ((), (), s32[]{:S(2)}) async-start(), calls=%async_computation.7 | async-start | bytes 13107200 | tf_op jit(solution)/shard_map/reduce_scatter | solution.py:166
  99.4 6.3 %copy-start.12 = (f32[128,5,4]{1,2,0:T(4,128)S(1)}, f32[128,5,4]{1,2,0:T(4,128)}, u32[]{:S(2)}) copy-start(f32[128,5,4]{1,2,0:T(4,128)} %get-tuple-element.16) | copy-start | bytes 30724
  99.4 6.4 %copy-start.6 = (f32[128,1,5,4,64]{4,2,3,0,1:T(8,128)S(1)}, f32[128,1,5,4,64]{4,2,3,0,1:T(8,128)}, u32[]{:S(2)}) copy-start(f32[128,1,5,4,64]{4,2,3,0,1:T(8,128)} %get-tuple-element.21) | copy-start | bytes 1966084
  111.8 3.1 %copy-start.7 = (bf16[128,1,5,4,196]{4,2,3,0,1:T(8,128)(2,1)S(1)}, bf16[128,1,5,4,196]{4,2,3,0,1:T(8,128)(2,1)}, u32[]{:S(2)}) copy-start(bf16[128,1,5,4,196]{4,2,3,0,1:T(8,128)(2,1)} %divide_convert_fusion) | copy-start | bytes 3010564
  114.9 5.5 %copy-start.10 = (bf16[128,64,128]{2,1,0:T(8,128)(2,1)S(1)}, bf16[128,64,128]{2,1,0:T(8,128)(2,1)}, u32[]{:S(2)}) copy-start(bf16[128,64,128]{2,1,0:T(8,128)(2,1)} %param.20) | copy-start | bytes 6291460
  119.8 1.6 copy-start.9
  135.2 86.7 %copy-start.11 = (bf16[128,4,1280]{2,1,0:T(4,128)(2,1)S(1)}, bf16[128,4,1280]{2,1,0:T(4,128)(2,1)}, u32[]{:S(2)}) copy-start(bf16[128,4,1280]{2,1,0:T(4,128)(2,1)} %param.15) | copy-start | bytes 3932164
Sparse Core Ops, SparseCore 0:
  135.4 86.5 reduce-scatter.1
where the time goes:
time: 234 us; the launch traced here: 233 us
  waiting for transfers between devices  98.2 us (42%)
  local copies, waits for them, and re-layouts  44.9 us (19%)
  starting transfers between devices  32.4 us (14%)
  matrix products  30.7 us (13%)
  between operations  13.8 us (6%)
  other arithmetic  12.8 us (5%)
    reduce_scatter x1, waiting for transfers between devices, body(): summed = lax.psum_scatter(terms, 'tensor', scatter_dimension=2, tiled=True)  86.7 us
    dot_general x1, matrix products, body(): jnp.einsum('bsh,hd->bsd', heads_out, out_proj, preferred_element_type=jnp...  9.71 us
    all_to_all x1, starting transfers between devices, body(): lax.all_to_all(out_keys, 'replica', split_axis=0, concat_axis=0, tiled=True)  7.41 us
    all_to_all x1, waiting for transfers between devices, body(): lax.all_to_all(outgoing[3], 'replica', split_axis=0, concat_axis=0, tiled...  6.4 us
    dot_general x1, matrix products, attend(): jnp.einsum('bskgd,bpkd->bkgsp', query_split, split_heads(pre_keys, kv_hea...  6.34 us
    all_to_all x1, starting transfers between devices, body(): lax.all_to_all(outgoing[3], 'replica', split_axis=0, concat_axis=0, tiled...  6.01 us
    all_to_all x1, starting transfers between devices, body(): lax.all_to_all(out_values, 'replica', split_axis=0, concat_axis=0, tiled=...  5.99 us
    all_to_all x1, starting transfers between devices, body(): lax.all_to_all(outgoing[1], 'replica', split_axis=0, concat_axis=0, tiled...  5.94 us
  transfers between devices with their start and end apart: 7, of which 3 were waited for; matrix products, arithmetic and copies ran while one was open for 24% of the time, Pallas kernels for 0%

commit v1 on v0

v1 whole, which is shorter than its diff:
```python
import functools
import math

import jax
import jax.numpy as jnp
from jax import lax
from jax.experimental import pallas as pl
from jax.experimental.pallas import tpu as pltpu
from jax.sharding import PartitionSpec as P

HEAD_DIM = 128
LOWEST = -1e30
EXP2_SCALE = math.log2(math.e) / math.sqrt(HEAD_DIM)
VMEM_BYTES = 40 * 1024 * 1024
NT = (((1,), (1,)), ((), ()))
NN = (((1,), (0,)), ((), ()))

ANY = pl.BlockSpec(memory_space=pl.ANY)
SMEM = pl.BlockSpec(memory_space=pltpu.SMEM)
VMEM = pl.BlockSpec(memory_space=pltpu.VMEM)


def params(side_effects=False):
    return pltpu.CompilerParams(vmem_limit_bytes=VMEM_BYTES, has_side_effects=side_effects)


def matmul(a, b, dims):
    return lax.dot_general(a, b, dims, preferred_element_type=jnp.float32)


def iota(shape, dim):
    return lax.broadcasted_iota(jnp.int32, shape, dim)


def pack_kernel(
    fork, partner, queries, new_keys, new_values, keys, values, *rest, replicas, slots
):
    outs, (piece, row_of, sems) = rest[: replicas - 1], rest[replicas - 1 :]
    me = lax.axis_index("replica")
    held, prefix = keys.shape[0], keys.shape[1]
    local_rows = queries.shape[0]
    groups = queries.shape[2] // HEAD_DIM
    copies = []
    for k in range(1, replicas):
        peer = lax.rem(me + k, replicas)
        offset = jnp.int32(0)
        for s in range(slots):
            prompt = fork[peer * slots + s]
            offset = jnp.where(lax.div(prompt, held) == me, lax.rem(prompt, held), offset)
        for n, source in enumerate((keys, values)):
            copy = pltpu.make_async_copy(
                source.at[offset],
                outs[k - 1].at[pl.ds(n * prefix, prefix)],
                sems.at[k - 1, n],
            )
            copy.start()
            copies.append(copy)

    for j in range(replicas):
        row_of[j] = 0

    def note(r, carry):
        row_of[lax.div(partner[r], local_rows)] = r
        return carry

    lax.fori_loop(0, local_rows, note, 0, unroll=8)
    for k in range(1, replicas):
        r = row_of[lax.rem(me + k, replicas)]
        q = queries[r].astype(jnp.float32)
        parts = [q[:, h * HEAD_DIM : (h + 1) * HEAD_DIM] for h in range(groups)]
        parts += [new_keys[r].astype(jnp.float32), new_values[r].astype(jnp.float32)]
        pad = piece.shape[1] - sum(p.shape[0] for p in parts)
        parts += [jnp.zeros((pad, HEAD_DIM), jnp.float32)]
        piece[k - 1] = jnp.concatenate(parts, axis=0).astype(piece.dtype)
        copy = pltpu.make_async_copy(
            piece.at[k - 1],
            outs[k - 1].at[pl.ds(2 * prefix, piece.shape[1])],
            sems.at[k - 1, 2],
        )
        copy.start()
        copies.append(copy)
    for copy in copies:
        copy.wait()


def meta_kernel(
    fork, partner, row_slot, prompt_lengths, cache_lengths, finished, out, *, slots, local_rows, moved
):
    me = lax.axis_index("replica")
    rows = local_rows

    def note(r, count):
        g = me * rows + r
        slot = row_slot[g]
        out[r] = slot
        out[rows + r] = prompt_lengths[fork[me * slots + slot]]
        out[2 * rows + r] = cache_lengths[g]
        out[3 * rows + r] = 1 - finished[g]
        peer = lax.div(partner[r], rows)
        out[4 * rows + count] = r
        out[4 * rows + (moved + 8) + count] = peer
        return jnp.minimum(count + jnp.where(peer != me, 1, 0), moved)

    lax.fori_loop(0, rows, note, jnp.int32(0), unroll=4)


def softmax_weights(prompt, new, cache, prompt_mask, new_mask, cache_mask):
    prompt = jnp.where(prompt_mask, prompt, LOWEST)
    new = jnp.where(new_mask, new, LOWEST)
    cache = jnp.where(cache_mask, cache, LOWEST)
    top = jnp.max(jnp.maximum(jnp.maximum(prompt, new), cache), axis=1, keepdims=True)
    prompt = jnp.exp2((prompt - top) * EXP2_SCALE)
    new = jnp.exp2((new - top) * EXP2_SCALE)
    cache = jnp.exp2((cache - top) * EXP2_SCALE)
    inverse = 1.0 / jnp.sum(prompt + new + cache, axis=1, keepdims=True)
    return prompt * inverse, new * inverse, cache * inverse


def pick_slot(scores, slot, slots, prefix):
    picked = scores[:, :prefix]
    for s in range(1, slots):
        picked = jnp.where(slot == s, scores[:, s * prefix : (s + 1) * prefix], picked)
    return picked


def spread_slot(weights, slot, slots):
    return jnp.concatenate(
        [jnp.where(slot == s, weights, 0.0).astype(jnp.bfloat16) for s in range(slots)], axis=1
    )


def attend_block(
    first_row, meta, q, nk, nv, ck, cv, pk, pv, heads, row_meta, alive_rows, cache_scores, cache_weights, mixed,
    *, local_rows, steps, slots, suffix
):
    n = q.shape[0]
    rows = n // steps
    groups = q.shape[1] // HEAD_DIM
    prefix = pk.shape[0] // slots
    for b in range(rows):
        span = pl.ds(b * steps, steps)
        for i in range(3):
            row_meta[i, span, :] = jnp.full(
                (steps, HEAD_DIM), meta[i * local_rows + first_row + b], jnp.int32
            )
        alive = meta[3 * local_rows + first_row + b].astype(jnp.float32)
        alive_rows[span, :] = jnp.full((steps, HEAD_DIM), alive, jnp.float32)

    subs = n // 16
    keys_sub = 4 * suffix
    half = 2 * suffix
    for sub in range(subs):
        r0 = sub * 16
        qs = jnp.concatenate(
            [q[r0 : r0 + 16, h * HEAD_DIM : (h + 1) * HEAD_DIM] for h in range(groups)], axis=0
        )
        s = matmul(qs, ck[sub * keys_sub : (sub + 1) * keys_sub, :], NT)
        for h in range(groups):
            cache_scores[h, r0 : r0 + 8, :] = s[16 * h : 16 * h + 8, :half]
            cache_scores[h, r0 + 8 : r0 + 16, :] = s[16 * h + 8 : 16 * h + 16, half:]

    shape = (n, HEAD_DIM)
    lane, row = iota(shape, 1), iota(shape, 0)
    cache_own = (lane // suffix) == ((row % 8) // steps)
    cache_lane = jnp.where(cache_own, lane % suffix, suffix)
    new_mask = ((lane // steps) == (row // steps)) & ((lane % steps) <= (row % steps))
    first_half = (row % 16) < 8
    slot = row_meta[0]
    prompt_mask = lane < row_meta[1]
    cache_mask = cache_lane < row_meta[2]
    for h in range(groups):
        qh = q[:, h * HEAD_DIM : (h + 1) * HEAD_DIM]
        prompt = pick_slot(matmul(qh, pk[...], NT), slot, slots, prefix)
        wp, wn, wc = softmax_weights(
            prompt, matmul(qh, nk[...], NT), cache_scores[h], prompt_mask, new_mask, cache_mask
        )
        cache_weights[h, :, :half] = jnp.where(first_half, wc, 0.0).astype(jnp.bfloat16)
        cache_weights[h, :, half:] = jnp.where(first_half, 0.0, wc).astype(jnp.bfloat16)
        mixed[h] = matmul(spread_slot(wp, slot, slots), pv[...], NN) + matmul(
            wn.astype(jnp.bfloat16), nv[...], NN
        )
    for sub in range(subs):
        r0 = sub * 16
        w = jnp.concatenate([cache_weights[h, r0 : r0 + 16, :] for h in range(groups)], axis=0)
        o = matmul(w, cv[sub * keys_sub : (sub + 1) * keys_sub, :], NN)
        for h in range(groups):
            total = mixed[h, r0 : r0 + 16, :] + o[16 * h : 16 * h + 16, :]
            heads[r0 : r0 + 16, h * HEAD_DIM : (h + 1) * HEAD_DIM] = (
                total * alive_rows[r0 : r0 + 16, :]
            ).astype(heads.dtype)


def first_kernel(
    fork, meta, q, nk, nv, ck, cv, own_keys, own_values, *rest, replicas, slots, moved, local_rows, steps, suffix
):
    recvs, rest = rest[: replicas - 1], rest[replicas - 1 :]
    heads, pk, pv, moved_q = rest[:4]
    row_meta, alive_rows, cache_scores, cache_weights, mixed, sems, moved_sems = rest[4:]
    me = lax.axis_index("replica")
    held, prefix = own_keys.shape[0], own_keys.shape[1]
    extra = moved_q.shape[1]
    for s in range(slots):
        prompt = fork[me * slots + s]
        k = lax.rem(me - lax.div(prompt, held) + replicas, replicas)
        offset = lax.rem(prompt, held)
        targets = (pk.at[pl.ds(s * prefix, prefix)], pv.at[pl.ds(s * prefix, prefix)])

        @pl.when(k == 0)
        def _():
            pltpu.make_async_copy(own_keys.at[offset], targets[0], sems.at[s, 0]).start()
            pltpu.make_async_copy(own_values.at[offset], targets[1], sems.at[s, 1]).start()

        for kk in range(1, replicas):

            @pl.when(k == kk)
            def _():
                for n in range(2):
                    pltpu.make_async_copy(
                        recvs[kk - 1].at[pl.ds(n * prefix, prefix)], targets[n], sems.at[s, n]
                    ).start()

    for i in range(moved):
        k = lax.rem(me - meta[4 * local_rows + moved + 8 + i] + replicas, replicas)
        for kk in range(1, replicas):

            @pl.when(k == kk)
            def _():
                pltpu.make_async_copy(
                    recvs[kk - 1].at[pl.ds(2 * prefix, extra)], moved_q.at[i], moved_sems.at[i]
                ).start()

    for s in range(slots):
        pltpu.make_async_copy(own_keys.at[0], pk.at[pl.ds(s * prefix, prefix)], sems.at[s, 0]).wait()
        pltpu.make_async_copy(own_values.at[0], pv.at[pl.ds(s * prefix, prefix)], sems.at[s, 1]).wait()
    attend_block(
        0, meta, q, nk, nv, ck, cv, pk, pv, heads, row_meta, alive_rows, cache_scores, cache_weights, mixed,
        local_rows=local_rows, steps=steps, slots=slots, suffix=suffix,
    )
    for i in range(moved):
        pltpu.make_async_copy(
            recvs[0].at[pl.ds(2 * prefix, extra)], moved_q.at[i], moved_sems.at[i]
        ).wait()


def later_kernel(meta, *refs, start, local_rows, steps, slots, suffix):
    first_row = (start + pl.program_id(0)) * (refs[0].shape[0] // steps)
    attend_block(
        first_row, meta, *refs, local_rows=local_rows, steps=steps, slots=slots, suffix=suffix
    )


def moved_kernel(
    meta, x, pk, pv, ck, cv, out, keys, values, row_meta, alive_rows, sems,
    *, local_rows, moved, steps, slots, groups
):
    span = x.shape[1]
    suffix = ck.shape[1]
    prefix = pk.shape[0] // slots
    step = pl.program_id(0)

    @pl.when(step == 0)
    def _():
        out[...] = jnp.zeros_like(out)

    copies = []
    for i in range(4):
        r = meta[4 * local_rows + step * 4 + i]
        for n, (source, target) in enumerate(((ck, keys), (cv, values))):
            copy = pltpu.make_async_copy(
                source.at[r], target.at[pl.ds(i * suffix, suffix)], sems.at[i, n]
            )
            copy.start()
            copies.append(copy)
        for n in range(3):
            row_meta[n, i * span : (i + 1) * span, :] = jnp.full(
                (span, HEAD_DIM), meta[n * local_rows + r], jnp.int32
            )
        alive_rows[i * span : (i + 1) * span, :] = jnp.full(
            (span, HEAD_DIM), meta[3 * local_rows + r].astype(jnp.float32), jnp.float32
        )
    q = x[...].reshape(4 * span, HEAD_DIM)
    shape = (4 * span, HEAD_DIM)
    lane, row = iota(shape, 1), iota(shape, 0)
    slot = row_meta[0]
    prompt_mask = lane < row_meta[1]
    cache_mask = ((lane // suffix) == ((row // span) % 2)) & ((lane % suffix) < row_meta[2])
    past = (lane % span) - groups * steps
    new_mask = ((lane // span) == (row // span)) & (past >= 0) & (past <= row % steps)
    prompt = pick_slot(matmul(q, pk[...], NT), slot, slots, prefix)
    new = matmul(q, q, NT)
    for copy in copies:
        copy.wait()
    cache = matmul(q, keys[...], NT)
    half = 2 * suffix
    top_half = row < 2 * span
    cache = jnp.where(top_half, cache[:, :half], cache[:, half:])
    wp, wn, wc = softmax_weights(prompt, new, cache, prompt_mask, new_mask, cache_mask)
    wc = jnp.concatenate(
        [jnp.where(top_half, wc, 0.0), jnp.where(top_half, 0.0, wc)], axis=1
    ).astype(jnp.bfloat16)
    wn = pltpu.roll(wn, steps, 1).astype(jnp.bfloat16)
    mixed = (
        matmul(spread_slot(wp, slot, slots), pv[...], NN)
        + matmul(wn, q, NN)
        + matmul(wc, values[...], NN)
    )
    mixed = (mixed * alive_rows[...]).astype(out.dtype)
    for i in range(4):
        out[meta[4 * local_rows + moved + 8 + step * 4 + i]] = mixed[i * span : (i + 1) * span]


def cross_kernel(cols, h_own, h_sib, w_own, w_sib, out):
    total = matmul(h_own[...], w_own[...], NN) + matmul(h_sib[...], w_sib[0], NN)
    out[...] = total.astype(out.dtype)


def base_kernel(cols, residual, h_own, h_sib, w_own, w_sib, out):
    total = matmul(h_own[...], w_own[...], NN) + matmul(h_sib[...], w_sib[0], NN)
    out[...] = total + residual[...].astype(jnp.float32)


def moved_heads(meta, ret, *, local_rows, moved, steps, groups):
    span = ret.shape[1]
    parts = []
    for first in range(0, moved, 4):
        x = jnp.concatenate(
            [ret[meta[4 * local_rows + moved + 8 + first + i]] for i in range(4)], axis=0
        )
        shape = (4 * steps, 4 * span)
        row, col = iota(shape, 0), iota(shape, 1)
        cols = []
        for h in range(groups):
            take = ((row // steps) == (col // span)) & ((col % span) == h * steps + row % steps)
            cols.append(matmul(take.astype(jnp.bfloat16), x, NN).astype(jnp.bfloat16))
        parts.append(jnp.concatenate(cols, axis=1))
    return jnp.concatenate(parts, axis=0) if len(parts) > 1 else parts[0]


def moved_cross_kernel(
    cols, meta, ret_own, ret_sib, w_here, w_there, w_sib, out, base, *, local_rows, moved, steps, groups
):
    options = dict(local_rows=local_rows, moved=moved, steps=steps, groups=groups)
    own = moved_heads(meta, ret_own, **options)
    sib = moved_heads(meta, ret_sib, **options)
    base[...] = matmul(own, w_here[...], NN) + matmul(sib, w_sib[0], NN)
    out[...] = (matmul(own, w_there[...], NN) + matmul(sib, w_sib[1], NN)).astype(out.dtype)


def write_rows(total, out, steps):
    for b in range(out.shape[0]):
        out[b] = total[b * steps : (b + 1) * steps].astype(out.dtype)


def first_final_kernel(base, recv, out):
    write_rows(base[...] + recv[...].astype(jnp.float32), out, out.shape[1])


def later_final_kernel(earlier, base, recv, out):
    write_rows(base[...] + recv[...].astype(jnp.float32), out, out.shape[1])


def moved_final_kernel(meta, earlier, residual, base, recv, out, before, after, sems, *, local_rows, moved, steps):
    rows = [meta[4 * local_rows + i] for i in range(moved)]
    copies = [
        pltpu.make_async_copy(residual.at[r], before.at[i], sems.at[i, 0]) for i, r in enumerate(rows)
    ]
    for copy in copies:
        copy.start()
    total = base[...] + recv[...].astype(jnp.float32)
    for copy in copies:
        copy.wait()
    for i in range(moved):
        after[i] = (
            total[i * steps : (i + 1) * steps] + before[i].astype(jnp.float32)
        ).astype(after.dtype)
    copies = [
        pltpu.make_async_copy(after.at[i], out.at[r], sems.at[i, 1]) for i, r in enumerate(rows)
    ]
    for copy in copies:
        copy.start()
    for copy in copies:
        copy.wait()


def body(
    residual,
    queries,
    new_keys,
    new_values,
    cache_keys,
    cache_values,
    cache_lengths,
    finished,
    partner,
    row_slot,
    fork_table,
    prompt_keys,
    prompt_values,
    prompt_lengths,
    out_proj,
):
    replicas = lax.axis_size("replica")
    tensors = lax.axis_size("tensor")
    me = lax.axis_index("replica")
    place = lax.axis_index("tensor")
    local_rows, steps, width = queries.shape
    groups = width // HEAD_DIM
    suffix = cache_keys.shape[1]
    held, prefix = prompt_keys.shape[:2]
    slots = fork_table.shape[1]
    moved = replicas // 2
    model = residual.shape[2]
    n = local_rows * steps
    span = 32
    dtype = queries.dtype
    fork = fork_table.reshape(-1)
    chunks = 4
    rows_chunk = local_rows // chunks
    nc = rows_chunk * steps

    if replicas <= 8:
        packed = pl.pallas_call(
            functools.partial(pack_kernel, replicas=replicas, slots=slots),
            out_shape=[jax.ShapeDtypeStruct((2 * prefix + span, HEAD_DIM), dtype)] * (replicas - 1),
            in_specs=[SMEM, SMEM, VMEM, VMEM, VMEM, ANY, ANY],
            out_specs=[ANY] * (replicas - 1),
            scratch_shapes=[
                pltpu.VMEM((replicas - 1, span, HEAD_DIM), dtype),
                pltpu.SMEM((replicas,), jnp.int32),
                pltpu.SemaphoreType.DMA((replicas - 1, 3)),
            ],
            compiler_params=params(),
            name="pack",
        )(fork, partner, queries, new_keys, new_values, prompt_keys, prompt_values)
        received = [
            lax.ppermute(packed[k - 1], "replica", [(i, (i + k) % replicas) for i in range(replicas)])
            for k in range(1, replicas)
        ]
    else:
        chosen = (fork_table // held) == me
        offsets = jnp.sum(jnp.where(chosen, fork_table % held, 0), axis=1)
        peer_of = partner // local_rows
        pairing = (peer_of[None, :] == jnp.arange(replicas, dtype=jnp.int32)[:, None]) & (
            peer_of[None, :] != me
        )
        row_of = jnp.sum(
            jnp.where(pairing, jnp.arange(local_rows, dtype=jnp.int32)[None, :], 0), axis=1
        )
        q = queries[row_of].reshape(replicas, steps, groups, HEAD_DIM).transpose(0, 2, 1, 3)
        q = q.reshape(replicas, groups * steps, HEAD_DIM)
        pad = jnp.zeros((replicas, span - (groups + 2) * steps, HEAD_DIM), dtype)
        block = jnp.concatenate(
            [prompt_keys[offsets], prompt_values[offsets], q, new_keys[row_of], new_values[row_of], pad],
            axis=1,
        )
        stacked = lax.all_to_all(block, "replica", split_axis=0, concat_axis=0, tiled=True)

    meta = pl.pallas_call(
        functools.partial(meta_kernel, slots=slots, local_rows=local_rows, moved=moved),
        out_shape=jax.ShapeDtypeStruct((4 * local_rows + 2 * (moved + 8),), jnp.int32),
        in_specs=[SMEM] * 6,
        out_specs=SMEM,
        name="meta",
    )(fork, partner, row_slot, prompt_lengths, cache_lengths, finished)

    def columns(index):
        return lax.dynamic_slice_in_dim(out_proj, index * model, model, axis=1)

    sibling = [(i, i ^ 1) for i in range(tensors)]
    across = [(i, i ^ 2) for i in range(tensors)]
    w_sib = lax.ppermute(jnp.stack([columns(place ^ 1), columns(place ^ 3)]), "tensor", sibling)

    q2 = queries.reshape(n, width)
    nk2 = new_keys.reshape(n, HEAD_DIM)
    nv2 = new_values.reshape(n, HEAD_DIM)
    ck2 = cache_keys.reshape(local_rows * suffix, HEAD_DIM)
    cv2 = cache_values.reshape(local_rows * suffix, HEAD_DIM)
    res2 = residual.reshape(n, model)

    scratch = [
        pltpu.VMEM((3, nc, HEAD_DIM), jnp.int32),
        pltpu.VMEM((nc, HEAD_DIM), jnp.float32),
        pltpu.VMEM((groups, nc, HEAD_DIM), jnp.float32),
        pltpu.VMEM((groups, nc, 2 * HEAD_DIM), jnp.bfloat16),
        pltpu.VMEM((groups, nc, HEAD_DIM), jnp.float32),
    ]
    sizes = dict(local_rows=local_rows, steps=steps, slots=slots, suffix=suffix)

    def block_specs(start):
        return [
            pl.BlockSpec((nc, width), lambda i: (i + start, 0)),
            pl.BlockSpec((nc, HEAD_DIM), lambda i: (i + start, 0)),
            pl.BlockSpec((nc, HEAD_DIM), lambda i: (i + start, 0)),
            pl.BlockSpec((rows_chunk * suffix, HEAD_DIM), lambda i: (i + start, 0)),
            pl.BlockSpec((rows_chunk * suffix, HEAD_DIM), lambda i: (i + start, 0)),
        ]

    def later(start, count, pk, pv):
        return pl.pallas_call(
            functools.partial(later_kernel, start=start, **sizes),
            grid=(count,),
            out_shape=jax.ShapeDtypeStruct((count * nc, width), dtype),
            in_specs=[SMEM] + block_specs(start) + [VMEM, VMEM],
            out_specs=pl.BlockSpec((nc, width), lambda i: (i, 0)),
            scratch_shapes=scratch,
            compiler_params=params(),
            name="attend",
        )(meta, q2, nk2, nv2, ck2, cv2, pk, pv)

    if replicas <= 8:
        h_first, pk, pv, moved_q = pl.pallas_call(
            functools.partial(first_kernel, replicas=replicas, moved=moved, **sizes),
            grid=(1,),
            out_shape=[
                jax.ShapeDtypeStruct((nc, width), dtype),
                jax.ShapeDtypeStruct((slots * prefix, HEAD_DIM), dtype),
                jax.ShapeDtypeStruct((slots * prefix, HEAD_DIM), dtype),
                jax.ShapeDtypeStruct((moved, span, HEAD_DIM), dtype),
            ],
            in_specs=[SMEM, SMEM] + block_specs(0) + [ANY] * (replicas + 1),
            out_specs=[VMEM] * 4,
            scratch_shapes=scratch
            + [pltpu.SemaphoreType.DMA((slots, 2)), pltpu.SemaphoreType.DMA((moved,))],
            compiler_params=params(),
            name="attend_first",
        )(fork, meta, q2, nk2, nv2, ck2, cv2, prompt_keys, prompt_values, *received)
    else:
        mine = stacked[fork_table[me] // held]
        pk = mine[:, :prefix].reshape(slots * prefix, HEAD_DIM)
        pv = mine[:, prefix : 2 * prefix].reshape(slots * prefix, HEAD_DIM)
        peers = lax.dynamic_slice_in_dim(meta, 4 * local_rows + moved + 8, moved)
        moved_q = stacked[peers][:, 2 * prefix :]
        h_first = later(0, 1, pk, pv)

    h_later = later(1, chunks - 1, pk, pv)
    back = pl.pallas_call(
        functools.partial(
            moved_kernel, local_rows=local_rows, moved=moved, steps=steps, slots=slots, groups=groups
        ),
        grid=(moved // 4,),
        out_shape=jax.ShapeDtypeStruct((replicas, span, HEAD_DIM), dtype),
        in_specs=[SMEM, pl.BlockSpec((4, span, HEAD_DIM), lambda i: (i, 0, 0)), VMEM, VMEM, ANY, ANY],
        out_specs=VMEM,
        scratch_shapes=[
            pltpu.VMEM((4 * suffix, HEAD_DIM), dtype),
            pltpu.VMEM((4 * suffix, HEAD_DIM), dtype),
            pltpu.VMEM((3, 4 * span, HEAD_DIM), jnp.int32),
            pltpu.VMEM((4 * span, HEAD_DIM), jnp.float32),
            pltpu.SemaphoreType.DMA((4, 2)),
        ],
        compiler_params=params(),
        name="attend_moved",
    )(meta, moved_q, pk, pv, cache_keys, cache_values)
    ret = lax.all_to_all(back, "replica", split_axis=0, concat_axis=0, tiled=True)

    cols = jnp.stack([place, place ^ 2]).astype(jnp.int32)

    def project(kernel, which, count, outs, extra=()):
        def call(h_own, h_sib, *more):
            rows = h_own.shape[0] // count
            grid_spec = pltpu.PrefetchScalarGridSpec(
                num_scalar_prefetch=1,
                grid=(count,),
                in_specs=list(extra)
                + [
                    pl.BlockSpec((rows, width), lambda i, c: (i, 0)),
                    pl.BlockSpec((rows, width), lambda i, c: (i, 0)),
                    pl.BlockSpec((width, model), lambda i, c: (0, c[which])),
                    pl.BlockSpec((1, width, model), lambda i, c: (which, 0, 0)),
                ],
                out_specs=pl.BlockSpec((rows, model), lambda i, c: (i, 0)),
            )
            return pl.pallas_call(
                kernel,
                grid_spec=grid_spec,
                out_shape=jax.ShapeDtypeStruct((h_own.shape[0], model), outs),
                compiler_params=params(),
                name="project",
            )(cols, *more, h_own, h_sib, out_proj, w_sib)

        return call

    cross = project(cross_kernel, 1, 1, dtype)
    s_first = lax.ppermute(h_first, "tensor", sibling)
    got = [lax.ppermute(cross(h_first, s_first), "tensor", across)]
    s_later = lax.ppermute(h_later, "tensor", sibling)
    for c in range(1, chunks):
        part = slice((c - 1) * nc, c * nc)
        got.append(lax.ppermute(cross(h_later[part], s_later[part]), "tensor", across))

    def base_of(first, h_own, h_sib, count):
        spec = pl.BlockSpec((nc, model), lambda i, c: (i + first, 0))
        return project(base_kernel, 0, count, jnp.float32, (spec,))(h_own, h_sib, res2)

    base_first = base_of(0, h_first, s_first, 1)
    base_later = base_of(1, h_later, s_later, chunks - 1)

    ret_sib = lax.ppermute(ret, "tensor", sibling)
    whole = lambda shape: pl.BlockSpec(shape, lambda i, c, m: (0,) * len(shape))
    cross_moved, base_moved = pl.pallas_call(
        functools.partial(
            moved_cross_kernel, local_rows=local_rows, moved=moved, steps=steps, groups=groups
        ),
        grid_spec=pltpu.PrefetchScalarGridSpec(
            num_scalar_prefetch=2,
            grid=(1,),
            in_specs=[
                whole(ret.shape),
                whole(ret.shape),
                pl.BlockSpec((width, model), lambda i, c, m: (0, c[0])),
                pl.BlockSpec((width, model), lambda i, c, m: (0, c[1])),
                whole(w_sib.shape),
            ],
            out_specs=[whole((moved * steps, model))] * 2,
        ),
        out_shape=[
            jax.ShapeDtypeStruct((moved * steps, model), dtype),
            jax.ShapeDtypeStruct((moved * steps, model), jnp.float32),
        ],
        compiler_params=params(),
        name="project_moved",
    )(cols, meta, ret, ret_sib, out_proj, out_proj, w_sib)
    got_moved = lax.ppermute(cross_moved, "tensor", across)

    shape = jax.ShapeDtypeStruct(residual.shape, residual.dtype)
    out = None
    for c in range(chunks):
        base, index = (base_first, 0) if c == 0 else (base_later, c - 1)
        specs = [
            pl.BlockSpec((nc, model), lambda i, index=index: (index, 0)),
            pl.BlockSpec((nc, model), lambda i: (0, 0)),
        ]
        out_spec = pl.BlockSpec((rows_chunk, steps, model), lambda i, c=c: (c, 0, 0))
        if out is None:
            out = pl.pallas_call(
                first_final_kernel,
                grid=(1,),
                in_specs=specs,
                out_specs=out_spec,
                out_shape=shape,
                compiler_params=params(),
                name="finish",
            )(base, got[c])
        else:
            out = pl.pallas_call(
                later_final_kernel,
                grid=(1,),
                in_specs=[ANY] + specs,
                out_specs=out_spec,
                out_shape=shape,
                input_output_aliases={0: 0},
                compiler_params=params(),
                name="finish",
            )(out, base, got[c])
    return pl.pallas_call(
        functools.partial(moved_final_kernel, local_rows=local_rows, moved=moved, steps=steps),
        in_specs=[SMEM, ANY, ANY, VMEM, VMEM],
        out_specs=ANY,
        out_shape=shape,
        input_output_aliases={1: 0},
        scratch_shapes=[
            pltpu.VMEM((moved, steps, model), dtype),
            pltpu.VMEM((moved, steps, model), dtype),
            pltpu.SemaphoreType.DMA((moved, 2)),
        ],
        compiler_params=params(),
        name="finish_moved",
    )(meta, out, residual, base_moved, got_moved)


def solution(mesh):
    rows = P("replica", None, "tensor")
    in_specs = (rows,) * 6 + (P(), P(), P("replica"), P(), P(), rows, rows, P(), P("tensor", None))
    return jax.shard_map(body, mesh=mesh, in_specs=in_specs, out_specs=rows, check_vma=False)
```

time: 234 us -> 116 us (0.50)
  waiting for transfers between devices: 98.2 us -> 4.5 us
  Pallas kernels: 0 us -> 43.3 us
  matrix products: 30.7 us -> 0 us
  starting transfers between devices: 32.4 us -> 19 us
  between operations: 13.8 us -> 0.46 us
  blocking collectives: 0 us -> 12.9 us
  local copies, waits for them, and re-layouts: 44.9 us -> 32.7 us
  other arithmetic: 12.8 us -> 2.02 us
    reduce_scatter x1 -> x0, waiting for transfers between devices: 86.7 us -> none  [body(): summed = lax.psum_scatter(terms, 'tensor', scatter_dimension=2, tiled=True)]
    pallas_call x0 -> x17, Pallas kernels: none -> 43.3 us  [the longest x6 12.9 us: call(): pl.pallas_call(kernel, grid_spec=grid_spec, out_shape=jax.ShapeDtypeStruc...]
    gather x19 -> x0, local copies, waits for them, and re-layouts: 38.1 us -> none  [the longest x1 3.06 us: body(): pre_keys = slot_keys[my_slots]]
    all_to_all x6 -> x0, starting transfers between devices: 32.2 us -> none  [the longest x1 7.41 us: body(): lax.all_to_all(out_keys, 'replica', split_axis=0, concat_axis=0, tiled=True)]
    dot_general x7 -> x0, matrix products: 30.7 us -> none  [the longest x1 9.71 us: body(): jnp.einsum('bsh,hd->bsd', heads_out, out_proj, preferred_element_type=jnp...]
    unnamed x35 -> x81, local copies, waits for them, and re-layouts: 1.77 us -> 22.7 us
    ppermute x0 -> x16, starting transfers between devices: none -> 19 us  [the longest x7 12.5 us: body(): lax.ppermute(packed[k - 1], 'replica', [(i, (i + k) % replicas) for i in...]
    all_to_all x0 -> x1, blocking collectives: none -> 12.9 us  [body(): lax.all_to_all(back, 'replica', split_axis=0, concat_axis=0, tiled=True)]
  transfers between devices with their start and end apart: 7 -> 16, of which waited for: 3 -> 4; matrix products, arithmetic and copies ran while one was open for 24% -> 7% of each run, Pallas kernels for 0% -> 36%
where the time goes in v1:
time: 116 us; the launch traced here: 115 us
  Pallas kernels  43.3 us (37%)
  local copies, waits for them, and re-layouts  32.7 us (28%)
  starting transfers between devices  19 us (16%)
  blocking collectives  12.9 us (11%)
  waiting for transfers between devices  4.5 us (4%)
  other arithmetic  2.02 us (2%)
    unnamed x81, local copies, waits for them, and re-layouts  22.7 us
    all_to_all x1, blocking collectives, body(): lax.all_to_all(back, 'replica', split_axis=0, concat_axis=0, tiled=True)  12.9 us
    pallas_call x6, Pallas kernels, call(): pl.pallas_call(kernel, grid_spec=grid_spec, out_shape=jax.ShapeDtypeStruc...  12.9 us
    ppermute x7, starting transfers between devices, body(): lax.ppermute(packed[k - 1], 'replica', [(i, (i + k) % replicas) for i in...  12.5 us
    pallas_call x1, Pallas kernels, later(): pl.pallas_call(functools.partial(later_kernel, start=start, **sizes), gri...  8.44 us
    pallas_call x3, Pallas kernels, body(): pl.pallas_call(later_final_kernel, grid=(1,), in_specs=[ANY] + specs, out...  5.43 us
    pallas_call x1, Pallas kernels, body(): pl.pallas_call(functools.partial(first_kernel, replicas=replicas, moved=m...  4.23 us
    ppermute x3, starting transfers between devices, body(): lax.ppermute(cross(h_later[part], s_later[part]), 'tensor', across)  3.52 us
  transfers between devices with their start and end apart: 16, of which 4 were waited for; matrix products, arithmetic and copies ran while one was open for 7% of the time, Pallas kernels for 36%

profile of v1, /device:TPU:0, one launch (start us, length us, event | category | flops | bytes accessed | tf_op | source)
XLA Modules:
  0.0 115.0 jit_solution(4904171131981127702)
XLA Ops:
  0.0 2.1 %dynamic-slice_bitcast_fusion.1 = (bf16[1,640,1280]{2,1,0:T(8,128)(2,1)S(1)}, bf16[1,640,1280]{2,1,0:T(8,128)(2,1)S(1)}) fusion(bf16[640,5120]{1,0:T(8,128)(2,1)} %w_there.1, s32[]{:T(128)S(6)} %select_n.6, s32[]{:T(128)S(6)} %select_n.7), kind=kLoop, calls=%fused_computation.2 | loop fusion | bytes 6553608 | tf_op jit(solution)/shard_map/stack | solution.py:471
  2.2 1.9 %pad_maximum_fusion = bf16[2,640,1280]{2,1,0:T(8,128)(2,1)} fusion(bf16[1,640,1280]{2,1,0:T(8,128)(2,1)S(1)} %get-tuple-element.32, bf16[1,640,1280]{2,1,0:T(8,128)(2,1)S(1)} %get-tuple-element.31), kind=kLoop, calls=%fused_computation | loop fusion | flops 1638400 | bytes 6553600 | tf_op jit(solution)/shard_map/stack | solution.py:471
  7.7 2.2 %pack.1 = (bf16[288,128]{1,0:T(8,128)(2,1)S(1)}, bf16[288,128]{1,0:T(8,128)(2,1)S(1)}, bf16[288,128]{1,0:T(8,128)(2,1)S(1)}, bf16[288,128]{1,0:T(8,128)(2,1)}, b...) custom-call(s32[32]{0:T(128)S(1)} %reshape.21.fork, s32[128]{0:T(128)S(1)} %copy-done.36, ...), custom_call_target="tpu_custom_call" | custom-call | tf_op jit(solution)/shard_map/pack/pallas_call | solution.py:422
  9.9 2.6 %collective-permute-start = (bf16[288,128]{1,0:T(8,128)(2,1)S(1)}, bf16[288,128]{1,0:T(8,128)(2,1)S(1)}, u32[]{:S(2)}, u32[]{:S(2)}) collective-permute-start(bf16[288,128]{1,0:T(8,128)(2,1)S(1)} %get-tuple-element.18), channel_id=1, source_target_pairs={{0,4},{4,8},{8,12},{12,16},{16,20},{20,24},{24,28},{28,0},{1,5},{5... | collective-permute-start | bytes 221192 | tf_op jit(solution)/shard_map/ppermute | solution.py:436
  12.5 1.6 %collective-permute-start.1 = (bf16[288,128]{1,0:T(8,128)(2,1)S(1)}, bf16[288,128]{1,0:T(8,128)(2,1)S(1)}, u32[]{:S(2)}, u32[]{:S(2)}) collective-permute-start(bf16[288,128]{1,0:T(8,128)(2,1)S(1)} %get-tuple-element.19), channel_id=1, source_target_pairs={{0,8},{4,12},{8,16},{12,20},{16,24},{20,28},{24,0},{28,4},{1,9},{5... | collective-permute-start | bytes 221192 | tf_op jit(solution)/shard_map/ppermute | solution.py:436
  14.1 2.5 %collective-permute-start.2 = (bf16[288,128]{1,0:T(8,128)(2,1)S(1)}, bf16[288,128]{1,0:T(8,128)(2,1)S(1)}, u32[]{:S(2)}, u32[]{:S(2)}) collective-permute-start(bf16[288,128]{1,0:T(8,128)(2,1)S(1)} %get-tuple-element.20), channel_id=1, source_target_pairs={{0,12},{4,16},{8,20},{12,24},{16,28},{20,0},{24,4},{28,8},{1,13},{... | collective-permute-start | bytes 221192 | tf_op jit(solution)/shard_map/ppermute | solution.py:436
  19.3 1.8 %collective-permute-start.4 = (bf16[288,128]{1,0:T(8,128)(2,1)}, bf16[288,128]{1,0:T(8,128)(2,1)}, u32[]{:S(2)}, u32[]{:S(2)}) collective-permute-start(bf16[288,128]{1,0:T(8,128)(2,1)} %get-tuple-element.22), channel_id=1, source_target_pairs={{0,20},{4,24},{8,28},{12,0},{16,4},{20,8},{24,12},{28,16},{1,21},{... | collective-permute-start | bytes 221192 | tf_op jit(solution)/shard_map/ppermute | solution.py:436
  23.1 1.9 %collective-permute-done.2.rest_2_ = bf16[288,128]{1,0:T(8,128)(2,1)S(1)} collective-permute-done((bf16[288,128]{1,0:T(8,128)(2,1)S(1)}, bf16[288,128]{1,0:T(8,128)(2,1)S(1)}, u32[]{:S(2)}, u32[]{:S(2)}) %collective-permute-start.2) | collective-permute-done | bytes 73760 | tf_op jit(solution)/shard_map/ppermute | solution.py:436
  27.0 2.2 %reshape.23.q.refs_0_ = bf16[512,640]{1,0:T(8,128)(2,1)} reshape(bf16[128,4,640]{2,1,0:T(4,128)(2,1)} %queries.1) | data formatting | bytes 1310720 | tf_op jit(solution)/shard_map/reshape | solution.py:473
  29.2 2.8 %meta.1 = s32[536]{0:T(1024)} custom-call(s32[32]{0:T(128)} %copy-done.34, s32[128]{0:T(128)} %partner.3, s32[1024]{0:T(1024)} %row_slot.1, s32[32]{0:T(128)} %prompt_lengths.1, s32[1024]{0:T(1024)} %cache_lengths.1, s32[1024]{0:T(1024)} %finished.1), custom_call_target="tpu_custom_call" | custom-call | tf_op jit(solution)/shard_map/meta/pallas_call | solution.py:458
  32.1 1.6 %copy-done.2 = bf16[128,64,128]{2,1,0:T(8,128)(2,1)S(1)} copy-done((bf16[128,64,128]{2,1,0:T(8,128)(2,1)S(1)}, bf16[128,64,128]{2,1,0:T(8,128)(2,1)}, u32[]{:S(2)}) %copy-start.2) | copy-done | bytes 2097176
  33.7 1.6 %copy-done.4 = bf16[128,64,128]{2,1,0:T(8,128)(2,1)S(1)} copy-done((bf16[128,64,128]{2,1,0:T(8,128)(2,1)S(1)}, bf16[128,64,128]{2,1,0:T(8,128)(2,1)}, u32[]{:S(2)}) %copy-start.4) | copy-done | bytes 2097176
  42.1 4.2 %attend_first.1 = (bf16[128,640]{1,0:T(8,128)(2,1)S(1)}, bf16[512,128]{1,0:T(8,128)(2,1)S(1)}, bf16[512,128]{1,0:T(8,128)(2,1)S(1)}, bf16[4,32,128]{2,1,0:T(8,128)(2,1)S(1)}) custom-call(s32[32]{0:T(128)S(1)} %copy-done.35, s32[536]{0:T(1024)S(1)} %copy-done.24, bf16[512,640]{1,0:T(8,128)(2,1)S(1)} %copy-done.7, bf16[512,128]{1,0:T(8,128)(2,1)S(1)} %bitcast.16, ...), custom_call_target="tpu_custom_call" | custom-call | tf_op jit(solution)/shard_map/attend_first/pallas_call | solution.py:511
  47.0 8.4 %attend.1.h_own = bf16[384,640]{1,0:T(8,128)(2,1)} custom-call(s32[536]{0:T(1024)S(1)} %copy-done.24, bf16[512,640]{1,0:T(8,128)(2,1)S(1)} %copy-done.7, bf16[512,128]{1,0:T(8,128)(2,1)S(1)} %bitcast.17, bf16[512,128]{1,0:T(8,128)(2,1)S(1)} %bitcast.19, bf16[8192,128]{1,0:T(8,128)(2,1)S(1)} %bitcast.13, bf16[8192,128]{1,0:T(8,128)(2,1)S(1)} %bitcast.15, ...), custom_call_target="tpu_custom_call" | custom-call | tf_op jit(solution)/shard_map/attend/pallas_call | solution.py:499
  58.9 2.9 %copy-done = bf16[640,5120]{1,0:T(8,128)(2,1)S(1)} copy-done((bf16[640,5120]{1,0:T(8,128)(2,1)S(1)}, bf16[640,5120]{1,0:T(8,128)(2,1)}, u32[]{:S(2)}) %copy-start) | copy-done | bytes 6553624
  61.8 2.0 %project.10 = bf16[128,1280]{1,0:T(8,128)(2,1)} custom-call(s32[2]{0:T(128)S(1)} %pad_add_fusion.cols, bf16[128,640]{1,0:T(8,128)(2,1)S(1)} %get-tuple-element.37.h_own, bf16[128,640]{1,0:T(8,128)(2,1)S(1)} %get-tuple-element.34.h_sib, bf16[640,5120]{1,0:T(8,128)(2,1)S(1)} %copy-done, bf16[2,640,1280]{2,1,0:T(8,128)(2,1)S(1)} %collective-permute-done.8.w_sib), custom_call_target="tpu_custom_call" | custom-call | tf_op jit(solution)/shard_map/project/pallas_call | solution.py:573
  63.7 1.5 %collective-permute-start.12 = (bf16[128,1280]{1,0:T(8,128)(2,1)}, bf16[128,1280]{1,0:T(8,128)(2,1)}, u32[]{:S(2)}, u32[]{:S(2)}) collective-permute-start(bf16[128,1280]{1,0:T(8,128)(2,1)} %project.10), channel_id=1, source_target_pairs={{0,2},{1,3},{2,0},{3,1},{4,6},{5,7},{6,4},{7,5},{8,10},{9,11},{10,... | collective-permute-start | bytes 983048 | tf_op jit(solution)/shard_map/ppermute | solution.py:589
  65.2 1.9 %project.7 = bf16[128,1280]{1,0:T(8,128)(2,1)} custom-call(s32[2]{0:T(128)S(1)} %pad_add_fusion.cols, bf16[128,640]{1,0:T(8,128)(2,1)S(1)} %copy-done.13, bf16[128,640]{1,0:T(8,128)(2,1)S(1)} %collective-permute-done.7.h_sib, bf16[640,5120]{1,0:T(8,128)(2,1)S(1)} %copy-done, bf16[2,640,1280]{2,1,0:T(8,128)(2,1)S(1)} %collective-permute-done.8.w_sib), custom_call_target="tpu_custom_call" | custom-call | tf_op jit(solution)/shard_map/project/pallas_call | solution.py:573
  67.7 2.0 %project.9 = bf16[128,1280]{1,0:T(8,128)(2,1)} custom-call(s32[2]{0:T(128)S(1)} %pad_add_fusion.cols, bf16[128,640]{1,0:T(8,128)(2,1)S(1)} %get-tuple-element.38.h_own, bf16[128,640]{1,0:T(8,128)(2,1)S(1)} %get-tuple-element.35.h_sib, bf16[640,5120]{1,0:T(8,128)(2,1)S(1)} %copy-done, bf16[2,640,1280]{2,1,0:T(8,128)(2,1)S(1)} %collective-permute-done.8.w_sib), custom_call_target="tpu_custom_call" | custom-call | tf_op jit(solution)/shard_map/project/pallas_call | solution.py:573
  69.6 1.5 %collective-permute-start.11 = (bf16[128,1280]{1,0:T(8,128)(2,1)}, bf16[128,1280]{1,0:T(8,128)(2,1)}, u32[]{:S(2)}, u32[]{:S(2)}) collective-permute-start(bf16[128,1280]{1,0:T(8,128)(2,1)} %project.9), channel_id=1, source_target_pairs={{0,2},{1,3},{2,0},{3,1},{4,6},{5,7},{6,4},{7,5},{8,10},{9,11},{10,... | collective-permute-start | bytes 983048 | tf_op jit(solution)/shard_map/ppermute | solution.py:589
  71.2 1.9 %project.11 = bf16[128,1280]{1,0:T(8,128)(2,1)} custom-call(s32[2]{0:T(128)S(1)} %pad_add_fusion.cols, bf16[128,640]{1,0:T(8,128)(2,1)S(1)} %get-tuple-element.36.h_own, bf16[128,640]{1,0:T(8,128)(2,1)S(1)} %get-tuple-element.33.h_sib, bf16[640,5120]{1,0:T(8,128)(2,1)S(1)} %copy-done, bf16[2,640,1280]{2,1,0:T(8,128)(2,1)S(1)} %collective-permute-done.8.w_sib), custom_call_target="tpu_custom_call" | custom-call | tf_op jit(solution)/shard_map/project/pallas_call | solution.py:573
  73.7 1.7 %attend_moved.1 = bf16[8,32,128]{2,1,0:T(8,128)(2,1)S(1)} custom-call(s32[536]{0:T(1024)S(1)} %copy-done.25, bf16[4,32,128]{2,1,0:T(8,128)(2,1)S(1)} %copy-done.33, bf16[512,128]{1,0:T(8,128)(2,1)S(1)} %copy-done.17, bf16[512,128]{1,0:T(8,128)(2,1)S(1)} %copy-done.19, bf16[128,64,128]{2,1,0:T(8,128)(2,1)S(1)} %copy-done.3, bf16[128,64,128]{2,1,0:T(8,128)(2,1)S(1)} %copy-done.5), custom_call_target="tpu_custom_call" | custom-call | tf_op jit(solution)/shard_map/attend_moved/pallas_call | solution.py:536
  75.3 12.9 %all_to_all.5.ret_own = bf16[8,32,128]{2,1,0:T(8,128)(2,1)S(1)} all-to-all(bf16[8,32,128]{2,1,0:T(8,128)(2,1)S(1)} %attend_moved.1), channel_id=1, replica_groups=mesh['replica'=8,'tensor'=4] {'replica'}, dimensions={0} | all-to-all | bytes 131072 | tf_op jit(solution)/shard_map/all_to_all | solution.py:554
  89.5 2.3 %project_moved.1 = (bf16[16,1280]{1,0:T(8,128)(2,1)}, f32[16,1280]{1,0:T(8,128)S(1)}) custom-call(s32[2]{0:T(128)S(1)} %pad_add_fusion.cols, s32[536]{0:T(1024)S(1)} %copy-done.25, bf16[8,32,128]{2,1,0:T(8,128)(2,1)S(1)} %all_to_all.5.ret_own, bf16[8,32,128]{2,1,0:T(8,128)(2,1)S(1)} %collective-permute-done.14.ret_sib, bf16[640,5120]{1,0:T(8,128)(2,1)S(1)} %bitcast.11, ...), custom_call_target="tpu_custom_call" | custom-call | tf_op jit(solution)/shard_map/project_moved/pallas_call | solution.py:600
  93.4 3.4 %reshape.22.residual = bf16[512,1280]{1,0:T(8,128)(2,1)} reshape(bf16[128,4,1280]{2,1,0:T(4,128)(2,1)} %residual.1) | data formatting | bytes 2621440 | tf_op jit(solution)/shard_map/reshape | solution.py:478
  96.7 2.9 %copy-done.1 = bf16[640,5120]{1,0:T(8,128)(2,1)S(1)} copy-done((bf16[640,5120]{1,0:T(8,128)(2,1)S(1)}, bf16[640,5120]{1,0:T(8,128)(2,1)}, u32[]{:S(2)}) %copy-start.1) | copy-done | bytes 6553624
  100.9 3.9 %project.8.base = f32[384,1280]{1,0:T(8,128)S(1)} custom-call(s32[2]{0:T(128)S(1)} %pad_add_fusion.cols, bf16[512,1280]{1,0:T(8,128)(2,1)S(1)} %copy-done.6, bf16[384,640]{1,0:T(8,128)(2,1)} %attend.1.h_own, bf16[384,640]{1,0:T(8,128)(2,1)} %collective-permute-done.10.h_sib, bf16[640,5120]{1,0:T(8,128)(2,1)S(1)} %copy-done.1, ...), custom_call_target="tpu_custom_call" | custom-call | tf_op jit(solution)/shard_map/project/pallas_call | solution.py:573
  106.1 1.8 %finish.4.earlier = bf16[128,4,1280]{2,1,0:T(4,128)(2,1)} custom-call(f32[128,1280]{1,0:T(8,128)S(1)} %project.6.base, bf16[128,1280]{1,0:T(8,128)(2,1)} %collective-permute-done.9.recv), custom_call_target="tpu_custom_call" | custom-call | tf_op jit(solution)/shard_map/finish/pallas_call | solution.py:635
  107.8 1.8 %finish.5.earlier = bf16[128,4,1280]{2,1,0:T(4,128)(2,1)} custom-call(bf16[128,4,1280]{2,1,0:T(4,128)(2,1)} %finish.4.earlier, f32[384,1280]{1,0:T(8,128)S(1)} %project.8.base, bf16[128,1280]{1,0:T(8,128)(2,1)} %collective-permute-done.11.recv), custom_call_target="tpu_custom_call", output_to_operand_aliasing={{}: (0, {})} | custom-call | tf_op jit(solution)/shard_map/finish/pallas_call | solution.py:645
  109.6 1.8 %finish.6.earlier = bf16[128,4,1280]{2,1,0:T(4,128)(2,1)} custom-call(bf16[128,4,1280]{2,1,0:T(4,128)(2,1)} %finish.5.earlier, f32[384,1280]{1,0:T(8,128)S(1)} %project.8.base, bf16[128,1280]{1,0:T(8,128)(2,1)} %collective-permute-done.12.recv), custom_call_target="tpu_custom_call", output_to_operand_aliasing={{}: (0, {})} | custom-call | tf_op jit(solution)/shard_map/finish/pallas_call | solution.py:645
  111.4 1.9 %finish.7.earlier = bf16[128,4,1280]{2,1,0:T(4,128)(2,1)} custom-call(bf16[128,4,1280]{2,1,0:T(4,128)(2,1)} %finish.6.earlier, f32[384,1280]{1,0:T(8,128)S(1)} %project.8.base, bf16[128,1280]{1,0:T(8,128)(2,1)} %collective-permute-done.13.recv), custom_call_target="tpu_custom_call", output_to_operand_aliasing={{}: (0, {})} | custom-call | tf_op jit(solution)/shard_map/finish/pallas_call | solution.py:645
  113.3 1.6 %finish_moved.1 = bf16[128,4,1280]{2,1,0:T(4,128)(2,1)} custom-call(s32[536]{0:T(1024)S(1)} %copy-done.25, bf16[128,4,1280]{2,1,0:T(4,128)(2,1)} %finish.7.earlier, bf16[128,4,1280]{2,1,0:T(4,128)(2,1)S(1)} %copy-done.8, f32[16,1280]{1,0:T(8,128)S(1)} %get-tuple-element.29.base, ...), custom_call_target="tpu_custom_call", output_to_operand_aliasing={{}: (1, {})} | custom-call | tf_op jit(solution)/shard_map/finish_moved/pallas_call | solution.py:655
  (108 shorter events, 27.6 us)
Async XLA Ops:
  2.2 2.6 %copy-start.10 = (bf16[128,4,128]{2,1,0:T(4,128)(2,1)S(1)}, bf16[128,4,128]{2,1,0:T(4,128)(2,1)}, u32[]{:S(2)}) copy-start(bf16[128,4,128]{2,1,0:T(4,128)(2,1)} %new_keys.1) | copy-start | bytes 393220
  2.2 2.6 %copy-start.11 = (bf16[128,4,128]{2,1,0:T(4,128)(2,1)S(1)}, bf16[128,4,128]{2,1,0:T(4,128)(2,1)}, u32[]{:S(2)}) copy-start(bf16[128,4,128]{2,1,0:T(4,128)(2,1)} %new_values.1) | copy-start | bytes 393220
  2.2 2.6 %copy-start.36 = (s32[128]{0:T(128)S(1)}, s32[128]{0:T(128)}, u32[]{:S(2)}) copy-start(s32[128]{0:T(128)} %partner.3) | copy-start | bytes 1540
  4.1 54.7 %collective-permute-start.8 = (bf16[2,640,1280]{2,1,0:T(8,128)(2,1)}, bf16[2,640,1280]{2,1,0:T(8,128)(2,1)S(1)}, u32[]{:S(2)}, u32[]{:S(2)}) collective-permute-start(bf16[2,640,1280]{2,1,0:T(8,128)(2,1)} %pad_maximum_fusion), channel_id=1, source_target_pairs={{0,1},{1,0},{2,3},{3,2},{4,5},{5,4},{6,7},{7,6},{8,9},{9,8},{10,11... | collective-permute-start | bytes 9830408 | tf_op jit(solution)/shard_map/ppermute | solution.py:471
  7.7 21.5 %copy-start.34 = (s32[32]{0:T(128)}, s32[32]{0:T(128)S(1)}, u32[]{:S(2)}) copy-start(s32[32]{0:T(128)S(1)} %reshape.21.fork) | copy-start | bytes 388
  9.9 8.8 %collective-permute-start = (bf16[288,128]{1,0:T(8,128)(2,1)S(1)}, bf16[288,128]{1,0:T(8,128)(2,1)S(1)}, u32[]{:S(2)}, u32[]{:S(2)}) collective-permute-start(bf16[288,128]{1,0:T(8,128)(2,1)S(1)} %get-tuple-element.18), channel_id=1, source_target_pairs={{0,4},{4,8},{8,12},{12,16},{16,20},{20,24},{24,28},{28,0},{1,5},{5... | collective-permute-start | bytes 221192 | tf_op jit(solution)/shard_map/ppermute | solution.py:436
  12.5 8.6 %collective-permute-start.1 = (bf16[288,128]{1,0:T(8,128)(2,1)S(1)}, bf16[288,128]{1,0:T(8,128)(2,1)S(1)}, u32[]{:S(2)}, u32[]{:S(2)}) collective-permute-start(bf16[288,128]{1,0:T(8,128)(2,1)S(1)} %get-tuple-element.19), channel_id=1, source_target_pairs={{0,8},{4,12},{8,16},{12,20},{16,24},{20,28},{24,0},{28,4},{1,9},{5... | collective-permute-start | bytes 221192 | tf_op jit(solution)/shard_map/ppermute | solution.py:436
  14.1 10.9 %collective-permute-start.2 = (bf16[288,128]{1,0:T(8,128)(2,1)S(1)}, bf16[288,128]{1,0:T(8,128)(2,1)S(1)}, u32[]{:S(2)}, u32[]{:S(2)}) collective-permute-start(bf16[288,128]{1,0:T(8,128)(2,1)S(1)} %get-tuple-element.20), channel_id=1, source_target_pairs={{0,12},{4,16},{8,20},{12,24},{16,28},{20,0},{24,4},{28,8},{1,13},{... | collective-permute-start | bytes 221192 | tf_op jit(solution)/shard_map/ppermute | solution.py:436
  16.6 15.5 %collective-permute-start.3 = (bf16[288,128]{1,0:T(8,128)(2,1)}, bf16[288,128]{1,0:T(8,128)(2,1)}, u32[]{:S(2)}, u32[]{:S(2)}) collective-permute-start(bf16[288,128]{1,0:T(8,128)(2,1)} %get-tuple-element.21), channel_id=1, source_target_pairs={{0,16},{4,20},{8,24},{12,28},{16,0},{20,4},{24,8},{28,12},{1,17},{... | collective-permute-start | bytes 221192 | tf_op jit(solution)/shard_map/ppermute | solution.py:436
  19.3 12.8 %collective-permute-start.4 = (bf16[288,128]{1,0:T(8,128)(2,1)}, bf16[288,128]{1,0:T(8,128)(2,1)}, u32[]{:S(2)}, u32[]{:S(2)}) collective-permute-start(bf16[288,128]{1,0:T(8,128)(2,1)} %get-tuple-element.22), channel_id=1, source_target_pairs={{0,20},{4,24},{8,28},{12,0},{16,4},{20,8},{24,12},{28,16},{1,21},{... | collective-permute-start | bytes 221192 | tf_op jit(solution)/shard_map/ppermute | solution.py:436
  21.7 10.3 %collective-permute-start.5 = (bf16[288,128]{1,0:T(8,128)(2,1)}, bf16[288,128]{1,0:T(8,128)(2,1)}, u32[]{:S(2)}, u32[]{:S(2)}) collective-permute-start(bf16[288,128]{1,0:T(8,128)(2,1)} %get-tuple-element.23), channel_id=1, source_target_pairs={{0,24},{4,28},{8,0},{12,4},{16,8},{20,12},{24,16},{28,20},{1,25},{... | collective-permute-start | bytes 221192 | tf_op jit(solution)/shard_map/ppermute | solution.py:436
  25.6 6.5 %collective-permute-start.6 = (bf16[288,128]{1,0:T(8,128)(2,1)}, bf16[288,128]{1,0:T(8,128)(2,1)}, u32[]{:S(2)}, u32[]{:S(2)}) collective-permute-start(bf16[288,128]{1,0:T(8,128)(2,1)} %get-tuple-element.24), channel_id=1, source_target_pairs={{0,28},{4,0},{8,4},{12,8},{16,12},{20,16},{24,20},{28,24},{1,29},{... | collective-permute-start | bytes 221192 | tf_op jit(solution)/shard_map/ppermute | solution.py:436
  47.0 8.4 %copy-start.16 = (bf16[512,128]{1,0:T(8,128)(2,1)}, bf16[512,128]{1,0:T(8,128)(2,1)S(1)}, u32[]{:S(2)}) copy-start(bf16[512,128]{1,0:T(8,128)(2,1)S(1)} %get-tuple-element.26.refs_5_.pk) | copy-start | bytes 393220
  47.0 8.4 %copy-start.18 = (bf16[512,128]{1,0:T(8,128)(2,1)}, bf16[512,128]{1,0:T(8,128)(2,1)S(1)}, u32[]{:S(2)}) copy-start(bf16[512,128]{1,0:T(8,128)(2,1)S(1)} %get-tuple-element.27.refs_6_.pv) | copy-start | bytes 393220
  47.0 8.4 %copy-start.32 = (bf16[4,32,128]{2,1,0:T(8,128)(2,1)}, bf16[4,32,128]{2,1,0:T(8,128)(2,1)S(1)}, u32[]{:S(2)}) copy-start(bf16[4,32,128]{2,1,0:T(8,128)(2,1)S(1)} %get-tuple-element.28.x) | copy-start | bytes 98308
  55.5 2.3 %collective-permute-start.10 = (bf16[384,640]{1,0:T(8,128)(2,1)}, bf16[384,640]{1,0:T(8,128)(2,1)}, u32[]{:S(2)}, u32[]{:S(2)}) collective-permute-start(bf16[384,640]{1,0:T(8,128)(2,1)} %attend.1.h_own), channel_id=1, source_target_pairs={{0,1},{1,0},{2,3},{3,2},{4,5},{5,4},{6,7},{7,6},{8,9},{9,8},{10,11... | collective-permute-start | bytes 1474568 | tf_op jit(solution)/shard_map/ppermute | solution.py:586
  55.7 9.6 %collective-permute-start.7 = (bf16[128,640]{1,0:T(8,128)(2,1)}, bf16[128,640]{1,0:T(8,128)(2,1)S(1)}, u32[]{:S(2)}, u32[]{:S(2)}) collective-permute-start(bf16[128,640]{1,0:T(8,128)(2,1)} %copy-done.12), channel_id=1, source_target_pairs={{0,1},{1,0},{2,3},{3,2},{4,5},{5,4},{6,7},{7,6},{8,9},{9,8},{10,11... | collective-permute-start | bytes 491528 | tf_op jit(solution)/shard_map/ppermute | solution.py:584
  58.9 2.9 %copy-start = (bf16[640,5120]{1,0:T(8,128)(2,1)S(1)}, bf16[640,5120]{1,0:T(8,128)(2,1)}, u32[]{:S(2)}) copy-start(bf16[640,5120]{1,0:T(8,128)(2,1)} %w_there.1) | copy-start | bytes 19660804
  61.8 3.5 %copy-start.13 = (bf16[128,640]{1,0:T(8,128)(2,1)S(1)}, bf16[128,640]{1,0:T(8,128)(2,1)}, u32[]{:S(2)}) copy-start(bf16[128,640]{1,0:T(8,128)(2,1)} %copy-done.12) | copy-start | bytes 491524
  63.7 45.9 %collective-permute-start.12 = (bf16[128,1280]{1,0:T(8,128)(2,1)}, bf16[128,1280]{1,0:T(8,128)(2,1)}, u32[]{:S(2)}, u32[]{:S(2)}) collective-permute-start(bf16[128,1280]{1,0:T(8,128)(2,1)} %project.10), channel_id=1, source_target_pairs={{0,2},{1,3},{2,0},{3,1},{4,6},{5,7},{6,4},{7,5},{8,10},{9,11},{10,... | collective-permute-start | bytes 983048 | tf_op jit(solution)/shard_map/ppermute | solution.py:589
  67.2 38.9 %collective-permute-start.9 = (bf16[128,1280]{1,0:T(8,128)(2,1)}, bf16[128,1280]{1,0:T(8,128)(2,1)}, u32[]{:S(2)}, u32[]{:S(2)}) collective-permute-start(bf16[128,1280]{1,0:T(8,128)(2,1)} %project.7), channel_id=1, source_target_pairs={{0,2},{1,3},{2,0},{3,1},{4,6},{5,7},{6,4},{7,5},{8,10},{9,11},{10,... | collective-permute-start | bytes 983048 | tf_op jit(solution)/shard_map/ppermute | solution.py:585
  67.7 6.0 %copy-start.5 = (bf16[128,64,128]{2,1,0:T(8,128)(2,1)S(1)}, bf16[128,64,128]{2,1,0:T(8,128)(2,1)}, u32[]{:S(2)}) copy-start(bf16[128,64,128]{2,1,0:T(8,128)(2,1)} %cv.1) | copy-start | bytes 6291460
  69.6 38.2 %collective-permute-start.11 = (bf16[128,1280]{1,0:T(8,128)(2,1)}, bf16[128,1280]{1,0:T(8,128)(2,1)}, u32[]{:S(2)}, u32[]{:S(2)}) collective-permute-start(bf16[128,1280]{1,0:T(8,128)(2,1)} %project.9), channel_id=1, source_target_pairs={{0,2},{1,3},{2,0},{3,1},{4,6},{5,7},{6,4},{7,5},{8,10},{9,11},{10,... | collective-permute-start | bytes 983048 | tf_op jit(solution)/shard_map/ppermute | solution.py:589
  71.1 18.4 %slice-start = ((s8[6553600]{0:T(1024)(128)(4,1)}), s8[4194304]{0:T(1024)(128)(4,1)S(1)}, s32[]{:S(2)}) async-start(s8[6553600]{0:T(1024)(128)(4,1)} %bitcast.10), calls=%async_computation.1 | async-start | bytes 8388608
  71.2 2.5 %copy-start.25 = (s32[536]{0:T(1024)S(1)}, s32[536]{0:T(1024)}, u32[]{:S(2)}) copy-start(s32[536]{0:T(1024)} %meta.1) | copy-start | bytes 6436
  71.2 2.5 %copy-start.33 = (bf16[4,32,128]{2,1,0:T(8,128)(2,1)S(1)}, bf16[4,32,128]{2,1,0:T(8,128)(2,1)}, u32[]{:S(2)}) copy-start(bf16[4,32,128]{2,1,0:T(8,128)(2,1)} %copy-done.32) | copy-start | bytes 98308
  71.2 18.4 %slice-start.1 = ((s8[6553600]{0:T(1024)(128)(4,1)}), s8[2359296]{0:T(1024)(128)(4,1)S(1)}, s32[]{:S(2)}) async-start(s8[6553600]{0:T(1024)(128)(4,1)} %bitcast.10), calls=%async_computation.2 | async-start | bytes 4718592
  73.1 38.3 %collective-permute-start.13 = (bf16[128,1280]{1,0:T(8,128)(2,1)}, bf16[128,1280]{1,0:T(8,128)(2,1)}, u32[]{:S(2)}, u32[]{:S(2)}) collective-permute-start(bf16[128,1280]{1,0:T(8,128)(2,1)} %project.11), channel_id=1, source_target_pairs={{0,2},{1,3},{2,0},{3,1},{4,6},{5,7},{6,4},{7,5},{8,10},{9,11},{10,... | collective-permute-start | bytes 983048 | tf_op jit(solution)/shard_map/ppermute | solution.py:589
  88.3 1.3 %collective-permute-start.14 = (bf16[8,32,128]{2,1,0:T(8,128)(2,1)S(1)}, bf16[8,32,128]{2,1,0:T(8,128)(2,1)S(1)}, u32[]{:S(2)}, u32[]{:S(2)}) collective-permute-start(bf16[8,32,128]{2,1,0:T(8,128)(2,1)S(1)} %all_to_all.5.ret_own), channel_id=1, source_target_pairs={{0,1},{1,0},{2,3},{3,2},{4,5},{5,4},{6,7},{7,6},{8,9},{9,8},{10,11... | collective-permute-start | bytes 196616 | tf_op jit(solution)/shard_map/ppermute | solution.py:598
  91.9 21.4 %collective-permute-start.15 = (bf16[16,1280]{1,0:T(8,128)(2,1)}, bf16[16,1280]{1,0:T(8,128)(2,1)}, u32[]{:S(2)}, u32[]{:S(2)}) collective-permute-start(bf16[16,1280]{1,0:T(8,128)(2,1)} %get-tuple-element.30), channel_id=1, source_target_pairs={{0,2},{1,3},{2,0},{3,1},{4,6},{5,7},{6,4},{7,5},{8,10},{9,11},{10,... | collective-permute-start | bytes 122888 | tf_op jit(solution)/shard_map/ppermute | solution.py:623
  96.7 2.9 %copy-start.1 = (bf16[640,5120]{1,0:T(8,128)(2,1)S(1)}, bf16[640,5120]{1,0:T(8,128)(2,1)}, u32[]{:S(2)}) copy-start(bf16[640,5120]{1,0:T(8,128)(2,1)} %w_there.1) | copy-start | bytes 19660804
  100.9 3.9 %copy-start.15 = (bf16[128,640]{1,0:T(8,128)(2,1)S(1)}, bf16[128,640]{1,0:T(8,128)(2,1)}, u32[]{:S(2)}) copy-start(bf16[128,640]{1,0:T(8,128)(2,1)} %copy-done.14) | copy-start | bytes 491524
  (24 other events, 30.6 us)

commit v2 on v0

v2 whole, which is shorter than its diff:
```python
import functools
import math

import jax
import jax.numpy as jnp
from jax import lax
from jax.experimental import pallas as pl
from jax.experimental.pallas import tpu as pltpu
from jax.sharding import PartitionSpec as P

HEAD_DIM = 128
LOWEST = -1e30
EXP2_SCALE = math.log2(math.e) / math.sqrt(HEAD_DIM)
VMEM_BYTES = 32 * 1024 * 1024
BLOCK = 32
NT = (((1,), (1,)), ((), ()))
NN = (((1,), (0,)), ((), ()))

ANY = pl.BlockSpec(memory_space=pl.ANY)
SMEM = pl.BlockSpec(memory_space=pltpu.SMEM)
VMEM = pl.BlockSpec(memory_space=pltpu.VMEM)


def params(side_effects=False):
    return pltpu.CompilerParams(vmem_limit_bytes=VMEM_BYTES, has_side_effects=side_effects)


def matmul(a, b, dims):
    return lax.dot_general(a, b, dims, preferred_element_type=jnp.float32)


def in_hbm(*arrays):
    return [pltpu.with_memory_space_constraint(x, pltpu.HBM) for x in arrays]


def iota(shape, dim):
    return lax.broadcasted_iota(jnp.int32, shape, dim)


def load(pairs, sem):
    copies = [pltpu.make_async_copy(a, b, sem.at[i]) for i, (a, b) in enumerate(pairs)]
    for copy in copies:
        copy.start()

    def wait():
        for copy in copies:
            copy.wait()

    return wait


def list_pairs(row_of, pairs, me, replicas, moved):
    count = jnp.int32(0)
    for j in range(replicas):
        pairs[count] = row_of[j]
        pairs[moved + 1 + count] = j
        count = jnp.minimum(count + jnp.where((row_of[j] >= 0) & (j != me), 1, 0), moved)


def find_pairs(partner, row_of, replicas, local_rows):
    for j in range(replicas):
        row_of[j] = -1

    def note(r, carry):
        row_of[lax.div(partner[r], local_rows)] = r
        return carry

    lax.fori_loop(0, local_rows, note, 0, unroll=8)


def pairs_kernel(partner, pairs, row_of, *, replicas, local_rows, moved):
    find_pairs(partner, row_of, replicas, local_rows)
    list_pairs(row_of, pairs, lax.axis_index("replica"), replicas, moved)


def pack_kernel(
    fork, partner, queries, new_keys, new_values, keys, values, *rest, replicas, slots, moved
):
    outs = rest[: replicas - 1]
    pairs, qv, nkv, nvv, row_of, sems, row_sems = rest[replicas - 1 :]
    me = lax.axis_index("replica")
    held, prefix = keys.shape[0], keys.shape[1]
    local_rows = queries.shape[0]
    groups = queries.shape[2] // HEAD_DIM
    copies = []
    for k in range(1, replicas):
        peer = lax.rem(me + k, replicas)
        offset = jnp.int32(0)
        for s in range(slots):
            prompt = fork[s, peer]
            offset = jnp.where(lax.div(prompt, held) == me, lax.rem(prompt, held), offset)
        for n, source in enumerate((keys, values)):
            copy = pltpu.make_async_copy(
                source.at[offset], outs[k - 1].at[pl.ds(n * prefix, prefix)], sems.at[k - 1, n]
            )
            copy.start()
            copies.append(copy)
    find_pairs(partner, row_of, replicas, local_rows)
    rows = [jnp.maximum(row_of[lax.rem(me + k, replicas)], 0) for k in range(1, replicas)]
    fetched = [
        load([(queries.at[r], qv.at[i]), (new_keys.at[r], nkv.at[i]), (new_values.at[r], nvv.at[i])], row_sems.at[i])
        for i, r in enumerate(rows)
    ]
    for k in range(1, replicas):
        fetched[k - 1]()
        q = qv[k - 1].astype(jnp.float32)
        parts = [q[:, h * HEAD_DIM : (h + 1) * HEAD_DIM] for h in range(groups)]
        parts += [nkv[k - 1].astype(jnp.float32), nvv[k - 1].astype(jnp.float32)]
        pad = outs[k - 1].shape[0] - 2 * prefix - sum(p.shape[0] for p in parts)
        parts += [jnp.zeros((pad, HEAD_DIM), jnp.float32)]
        outs[k - 1][2 * prefix :, :] = jnp.concatenate(parts, axis=0).astype(outs[k - 1].dtype)
    list_pairs(row_of, pairs, me, replicas, moved)
    for copy in copies:
        copy.wait()


def softmax_weights(prompt, new, cache, prompt_mask, new_mask, cache_mask):
    prompt = jnp.where(prompt_mask, prompt, LOWEST)
    new = jnp.where(new_mask, new, LOWEST)
    cache = jnp.where(cache_mask, cache, LOWEST)
    top = jnp.max(jnp.maximum(jnp.maximum(prompt, new), cache), axis=1, keepdims=True)
    prompt = jnp.exp2((prompt - top) * EXP2_SCALE)
    new = jnp.exp2((new - top) * EXP2_SCALE)
    cache = jnp.exp2((cache - top) * EXP2_SCALE)
    inverse = 1.0 / jnp.sum(prompt + new + cache, axis=1, keepdims=True)
    return prompt * inverse, new * inverse, cache * inverse


def pick_slot(scores, slot, slots, prefix):
    picked = scores[:, :prefix]
    for s in range(1, slots):
        picked = jnp.where(slot == s, scores[:, s * prefix : (s + 1) * prefix], picked)
    return picked


def spread_slot(weights, slot, slots):
    return jnp.concatenate(
        [jnp.where(slot == s, weights, 0.0).astype(jnp.bfloat16) for s in range(slots)], axis=1
    )


def fill_meta(lookup, local_row, span, row_meta, alive_rows):
    row_slot, fork, prompt_lengths, cache_lengths, finished, me, slots, local_rows = lookup
    g = me * local_rows + local_row
    slot = row_slot[g]
    values = (slot, prompt_lengths[fork[slot, me]], cache_lengths[g])
    size = span.stop - span.start
    for i, value in enumerate(values):
        row_meta[i, span, :] = jnp.full((size, HEAD_DIM), value, jnp.int32)
    alive_rows[span, :] = jnp.full((size, HEAD_DIM), 1 - finished[g], jnp.int32).astype(jnp.float32)


def attend_scores(q, ck, cache_scores, *, steps, suffix):
    n = q.shape[0]
    groups = q.shape[1] // HEAD_DIM
    keys_sub = 4 * suffix
    half = 2 * suffix
    for sub in range(n // 16):
        r0 = sub * 16
        qs = jnp.concatenate(
            [q[r0 : r0 + 16, h * HEAD_DIM : (h + 1) * HEAD_DIM] for h in range(groups)], axis=0
        )
        s = matmul(qs, ck[sub * keys_sub : (sub + 1) * keys_sub, :], NT)
        for h in range(groups):
            cache_scores[h, r0 : r0 + 8, :] = s[16 * h : 16 * h + 8, :half]
            cache_scores[h, r0 + 8 : r0 + 16, :] = s[16 * h + 8 : 16 * h + 16, half:]


def attend_block(
    q, nk, nv, cv, pk, pv, heads, row_meta, alive_rows, cache_scores, weights, cache_weights, mixed,
    *, steps, slots, suffix
):
    n = q.shape[0]
    groups = q.shape[1] // HEAD_DIM
    prefix = pk.shape[0] // slots
    keys_sub = 4 * suffix
    half = 2 * suffix
    shape = (n, HEAD_DIM)
    lane, row = iota(shape, 1), iota(shape, 0)
    cache_own = (lane // suffix) == ((row % 8) // steps)
    cache_lane = jnp.where(cache_own, lane % suffix, suffix)
    new_mask = ((lane // steps) == (row // steps)) & ((lane % steps) <= (row % steps))
    first_half = (row % 16) < 8
    slot = row_meta[0]
    prompt_mask = lane < row_meta[1]
    cache_mask = cache_lane < row_meta[2]
    q_all = jnp.concatenate([q[:, h * HEAD_DIM : (h + 1) * HEAD_DIM] for h in range(groups)], axis=0)
    prompt_all = matmul(q_all, pk[...], NT)
    new_all = matmul(q_all, nk[...], NT)
    for h in range(groups):
        part = slice(h * n, (h + 1) * n)
        prompt = pick_slot(prompt_all[part], slot, slots, prefix)
        wp, wn, wc = softmax_weights(
            prompt, new_all[part], cache_scores[h], prompt_mask, new_mask, cache_mask
        )
        cache_weights[h, :, :half] = jnp.where(first_half, wc, 0.0).astype(jnp.bfloat16)
        cache_weights[h, :, half:] = jnp.where(first_half, 0.0, wc).astype(jnp.bfloat16)
        weights[part, : slots * prefix] = spread_slot(wp, slot, slots)
        weights[part, slots * prefix :] = wn.astype(jnp.bfloat16)
    mixed[...] = matmul(weights[:, : slots * prefix], pv[...], NN) + matmul(
        weights[:, slots * prefix :], nv[...], NN
    )
    for sub in range(n // 16):
        r0 = sub * 16
        w = jnp.concatenate([cache_weights[h, r0 : r0 + 16, :] for h in range(groups)], axis=0)
        o = matmul(w, cv[sub * keys_sub : (sub + 1) * keys_sub, :], NN)
        for h in range(groups):
            total = mixed[h * n + r0 : h * n + r0 + 16, :] + o[16 * h : 16 * h + 16, :]
            heads[r0 : r0 + 16, h * HEAD_DIM : (h + 1) * HEAD_DIM] = (
                total * alive_rows[r0 : r0 + 16, :]
            ).astype(heads.dtype)


def moved_block(x, pk, pv, keys, values, slot, plen, clen, alive, wait, *, steps, slots, groups, span, suffix):
    prefix = pk.shape[0] // slots
    shape = (4 * span, HEAD_DIM)
    lane, row = iota(shape, 1), iota(shape, 0)
    prompt_mask = lane < plen
    cache_mask = ((lane // suffix) == ((row // span) % 2)) & ((lane % suffix) < clen)
    past = (lane % span) - groups * steps
    new_mask = ((lane // span) == (row // span)) & (past >= 0) & (past <= row % steps)
    prompt = pick_slot(matmul(x, pk[...], NT), slot, slots, prefix)
    new = matmul(x, x, NT)
    wait()
    cache = matmul(x, keys[...], NT)
    half = 2 * suffix
    top_half = row < 2 * span
    cache = jnp.where(top_half, cache[:, :half], cache[:, half:])
    wp, wn, wc = softmax_weights(prompt, new, cache, prompt_mask, new_mask, cache_mask)
    wc = jnp.concatenate(
        [jnp.where(top_half, wc, 0.0), jnp.where(top_half, 0.0, wc)], axis=1
    ).astype(jnp.bfloat16)
    wn = pltpu.roll(wn, steps, 1).astype(jnp.bfloat16)
    mixed = (
        matmul(spread_slot(wp, slot, slots), pv[...], NN)
        + matmul(wn, x, NN)
        + matmul(wc, values[...], NN)
    )
    mixed = (mixed * alive).astype(jnp.bfloat16)
    row, col = iota((4 * steps, 4 * span), 0), iota((4 * steps, 4 * span), 1)
    cols = []
    for h in range(groups):
        take = ((row // steps) == (col // span)) & ((col % span) == h * steps + row % steps)
        cols.append(matmul(take.astype(jnp.bfloat16), mixed, NN).astype(jnp.bfloat16))
    return jnp.concatenate(cols, axis=1)


def attend_kernel(
    cols, fork, pairs, row_slot, prompt_lengths, cache_lengths, finished, q, nk, nv, ck, cv, own_keys, own_values,
    w_own, w_sib, *rest, stacked, replicas, slots, moved, local_rows, steps, suffix, span
):
    count = 1 if stacked else replicas - 1
    recvs, rest = rest[:count], rest[count:]
    heads, w_here, w_there = rest[:3]
    pk, pv, qv, nkv, nvv, ckv, cvv, x, keys, values = rest[3:13]
    row_meta, alive_rows, moved_meta, moved_alive, cache_scores, weights, cache_weights, mixed = rest[13:21]
    local_sems, sems, moved_sems, cache_sems, w_sems = rest[21:]
    me = lax.axis_index("replica")
    held, prefix = own_keys.shape[0], own_keys.shape[1]
    blocks, n = qv.shape[:2]
    groups = qv.shape[2] // HEAD_DIM
    rows = n // steps
    local = (q, nk, nv, ck, cv)
    buffers = [[v.at[i] for v in (qv, nkv, nvv, ckv, cvv)] for i in range(blocks)]
    spans = [(pl.ds(i * n, n), pl.ds(i * rows * suffix, rows * suffix)) for i in range(blocks)]
    scores_ready = [
        load([(q.at[a], qv.at[i]), (ck.at[b], ckv.at[i])], local_sems.at[i, 0]) for i, (a, b) in enumerate(spans)
    ]
    for s in range(slots):
        prompt = fork[s, me]
        owner = lax.div(prompt, held)
        offset = lax.rem(prompt, held)
        targets = (pk.at[pl.ds(s * prefix, prefix)], pv.at[pl.ds(s * prefix, prefix)])
        if stacked:
            for i in range(2):
                pltpu.make_async_copy(
                    recvs[0].at[owner, pl.ds(i * prefix, prefix)], targets[i], sems.at[s, i]
                ).start()
            continue
        k = lax.rem(me - owner + replicas, replicas)

        @pl.when(k == 0)
        def _():
            pltpu.make_async_copy(own_keys.at[offset], targets[0], sems.at[s, 0]).start()
            pltpu.make_async_copy(own_values.at[offset], targets[1], sems.at[s, 1]).start()

        for kk in range(1, replicas):

            @pl.when(k == kk)
            def _():
                for i in range(2):
                    pltpu.make_async_copy(
                        recvs[kk - 1].at[pl.ds(i * prefix, prefix)], targets[i], sems.at[s, i]
                    ).start()

    for i in range(moved):
        peer = pairs[moved + 1 + i]
        if stacked:
            pltpu.make_async_copy(
                recvs[0].at[peer, pl.ds(2 * prefix, span)], x.at[pl.ds(i * span, span)], moved_sems.at[i]
            ).start()
        else:
            k = lax.rem(me - peer + replicas, replicas)
            for kk in range(1, replicas):

                @pl.when(k == kk)
                def _():
                    pltpu.make_async_copy(
                        recvs[kk - 1].at[pl.ds(2 * prefix, span)],
                        x.at[pl.ds(i * span, span)],
                        moved_sems.at[i],
                    ).start()

    cache_copies = []
    for i in range(moved):
        r = pairs[i]
        for j, (source, target) in enumerate(((ck, keys), (cv, values))):
            copy = pltpu.make_async_copy(
                source.at[pl.ds(pl.multiple_of(r * suffix, suffix), suffix)],
                target.at[pl.ds(i * suffix, suffix)],
                cache_sems.at[i, j],
            )
            copy.start()
            cache_copies.append(copy)
    lookup = (row_slot, fork, prompt_lengths, cache_lengths, finished, me, slots, local_rows)
    for i in range(moved):
        fill_meta(lookup, pairs[i], slice(i * span, (i + 1) * span), moved_meta, moved_alive)

    rest_ready = [
        load([(nk.at[a], nkv.at[i]), (nv.at[a], nvv.at[i]), (cv.at[b], cvv.at[i])], local_sems.at[i, 1])
        for i, (a, b) in enumerate(spans)
    ]
    width, model = w_own.shape[0], w_there.shape[1]
    weights_ready = load(
        [
            (w.at[:, pl.ds(pl.multiple_of(cols[i] * model, HEAD_DIM), model)], target.at[pl.ds(j * width, width)])
            for i, target in enumerate((w_here, w_there))
            for j, w in enumerate((w_own, w_sib))
        ],
        w_sems,
    )
    for b in range(local_rows):
        i, at = b // rows, b % rows
        fill_meta(lookup, b, slice(at * steps, (at + 1) * steps), row_meta.at[i], alive_rows.at[i])
    def wait_prompts():
        for s in range(slots):
            for i, target in enumerate((pk, pv)):
                pltpu.make_async_copy(
                    own_keys.at[0], target.at[pl.ds(s * prefix, prefix)], sems.at[s, i]
                ).wait()

    sizes = dict(steps=steps, suffix=suffix)
    for i in range(blocks):
        scores_ready[i]()
        attend_scores(qv.at[i], ckv.at[i], cache_scores.at[i], **sizes)
    wait_prompts()
    for ready in rest_ready:
        ready()
    for i in range(blocks):
        attend_block(
            qv.at[i], nkv.at[i], nvv.at[i], cvv.at[i], pk, pv, heads.at[pl.ds(i * n, n)], row_meta.at[i],
            alive_rows.at[i], cache_scores.at[i], weights.at[i], cache_weights.at[i], mixed.at[i],
            slots=slots, **sizes,
        )
    for i in range(moved):
        pltpu.make_async_copy(
            own_keys.at[0, pl.ds(0, span)], x.at[pl.ds(i * span, span)], moved_sems.at[i]
        ).wait()

    def wait_caches():
        for copy in cache_copies:
            copy.wait()

    first = blocks * n
    for g in range(moved // 4):
        part = slice(g * 4 * span, (g + 1) * 4 * span)
        kpart = slice(g * 4 * suffix, (g + 1) * 4 * suffix)
        heads[first + g * 4 * steps : first + (g + 1) * 4 * steps, :] = moved_block(
            x[part, :], pk, pv, keys.at[kpart], values.at[kpart],
            moved_meta[0, part, :], moved_meta[1, part, :], moved_meta[2, part, :], moved_alive[part, :],
            wait_caches if g == 0 else (lambda: None),
            steps=steps, slots=slots, groups=groups, span=span, suffix=suffix,
        )
    weights_ready()


def project_kernel(h_own, h_sib, weights, out, moved_out):
    rows = out.shape[0]
    total = matmul(jnp.concatenate([h_own[...], h_sib[...]], axis=1), weights[...], NN)
    out[...] = total[:rows].astype(out.dtype)
    moved_out[...] = total[rows:].astype(out.dtype)


def base_kernel(h_own, h_sib, weights, residual, after, out, moved_out):
    rows = out.shape[0]
    steps = residual.shape[1]
    total = matmul(jnp.concatenate([h_own[...], h_sib[...]], axis=1), weights[...], NN)
    moved_out[...] = total[rows:]
    for b in range(rows // steps):
        part = slice(b * steps, (b + 1) * steps)
        out[part, :] = total[part] + residual[b].astype(jnp.float32)


def moved_sum_kernel(pairs, base, recv, *outs, moved, steps, replicas, split):
    me = lax.axis_index("replica")
    total = base[...] + recv[...].astype(jnp.float32)
    for i in range(moved):
        peer = pairs[moved + 1 + i]
        value = total[i * steps : (i + 1) * steps, :]
        if split:
            k = jnp.bitwise_xor(me, peer)
            place = 2 * lax.rem(lax.div(k, 2), 2) + lax.div(k, 4)

            @pl.when(lax.rem(k, 2) == 0)
            def _():
                outs[0][place] = value

            @pl.when(lax.rem(k, 2) == 1)
            def _():
                outs[1][place] = value

        else:
            outs[0][peer] = value


def finish_kernel(pairs, base, recv, residual, *rest, moved, replicas, split):
    backs, (out, branch, before, sems) = rest[:-4], rest[-4:]
    me = lax.axis_index("replica")
    step = pl.program_id(0)
    rows, steps = out.shape[:2]

    @pl.when(step == 0)
    def _():
        for i in range(moved):
            peer = pairs[moved + 1 + i]
            pltpu.make_async_copy(residual.at[pairs[i]], before.at[i], sems.at[i, 0]).start()
            if split:
                k = jnp.bitwise_xor(me, peer)
                places = {1: (0, 0), 2: (1, 0), 3: (1, 2), 4: (2, 0), 5: (2, 1), 6: (2, 2), 7: (2, 3)}
                for d, (which, index) in places.items():

                    @pl.when(k == d)
                    def _():
                        pltpu.make_async_copy(backs[which].at[index], branch.at[i], sems.at[i, 1]).start()

            else:
                pltpu.make_async_copy(backs[0].at[peer], branch.at[i], sems.at[i, 1]).start()

    part = pl.ds(pl.multiple_of(step * rows * steps, rows * steps), rows * steps)
    total = base[part, :] + recv[part, :].astype(jnp.float32)
    for b in range(rows):
        out[b] = total[b * steps : (b + 1) * steps].astype(out.dtype)

    @pl.when(step == 0)
    def _():
        for i in range(moved):
            pltpu.make_async_copy(residual.at[0], before.at[i], sems.at[i, 0]).wait()
            pltpu.make_async_copy(backs[0].at[0], branch.at[i], sems.at[i, 1]).wait()

    for i in range(moved):
        r = pairs[i]

        @pl.when(lax.div(r, rows) == step)
        def _():
            out[lax.rem(r, rows)] = (branch[i] + before[i].astype(jnp.float32)).astype(out.dtype)


def exchange_pack(
    fork, partner, row_slot, queries, new_keys, new_values, fork_table, prompt_keys, prompt_values, span, moved
):
    replicas = lax.axis_size("replica")
    me = lax.axis_index("replica")
    local_rows, steps, width = queries.shape
    groups = width // HEAD_DIM
    held, prefix = prompt_keys.shape[:2]
    dtype = queries.dtype
    pairs_shape = jax.ShapeDtypeStruct((2 * (moved + 1),), jnp.int32)
    if replicas <= 8:
        *packed, pairs = pl.pallas_call(
            functools.partial(pack_kernel, replicas=replicas, slots=fork_table.shape[1], moved=moved),
            out_shape=[pltpu.VMEM((2 * prefix + span, HEAD_DIM), dtype)] * (replicas - 1) + [pairs_shape],
            in_specs=[SMEM, SMEM] + [ANY] * 5,
            out_specs=[VMEM] * (replicas - 1) + [SMEM],
            scratch_shapes=[
                pltpu.VMEM((replicas - 1, steps, width), dtype),
                pltpu.VMEM((replicas - 1, steps, HEAD_DIM), dtype),
                pltpu.VMEM((replicas - 1, steps, HEAD_DIM), dtype),
                pltpu.SMEM((replicas,), jnp.int32),
                pltpu.SemaphoreType.DMA((replicas - 1, 2)),
                pltpu.SemaphoreType.DMA((replicas - 1, 3)),
            ],
            compiler_params=params(),
            name="pack",
        )(fork, partner, *in_hbm(queries, new_keys, new_values, prompt_keys, prompt_values))
        received = [
            lax.ppermute(packed[k - 1], "replica", [(i, (i + k) % replicas) for i in range(replicas)])
            for k in range(1, replicas)
        ]
        return received, pairs
    chosen = (fork_table // held) == me
    offsets = jnp.sum(jnp.where(chosen, fork_table % held, 0), axis=1)
    peer_of = partner // local_rows
    pairing = (peer_of[None, :] == jnp.arange(replicas, dtype=jnp.int32)[:, None]) & (
        peer_of[None, :] != me
    )
    row_of = jnp.sum(jnp.where(pairing, jnp.arange(local_rows, dtype=jnp.int32)[None, :], 0), axis=1)
    q = queries[row_of].reshape(replicas, steps, groups, HEAD_DIM).transpose(0, 2, 1, 3)
    q = q.reshape(replicas, groups * steps, HEAD_DIM)
    pad = jnp.zeros((replicas, span - (groups + 2) * steps, HEAD_DIM), dtype)
    block = jnp.concatenate(
        [prompt_keys[offsets], prompt_values[offsets], q, new_keys[row_of], new_values[row_of], pad], axis=1
    )
    pairs = pl.pallas_call(
        functools.partial(pairs_kernel, replicas=replicas, local_rows=local_rows, moved=moved),
        out_shape=pairs_shape,
        in_specs=[SMEM],
        out_specs=SMEM,
        scratch_shapes=[pltpu.SMEM((replicas,), jnp.int32)],
        name="pairs",
    )(partner)
    return [lax.all_to_all(block, "replica", split_axis=0, concat_axis=0, tiled=True)], pairs


def body(
    residual,
    queries,
    new_keys,
    new_values,
    cache_keys,
    cache_values,
    cache_lengths,
    finished,
    partner,
    row_slot,
    fork_table,
    prompt_keys,
    prompt_values,
    prompt_lengths,
    out_proj,
):
    replicas = lax.axis_size("replica")
    tensors = lax.axis_size("tensor")
    place = lax.axis_index("tensor")
    local_rows, steps, width = queries.shape
    groups = width // HEAD_DIM
    suffix = cache_keys.shape[1]
    held, prefix = prompt_keys.shape[:2]
    slots = fork_table.shape[1]
    moved = replicas // 2
    stacked = replicas > 8
    model = residual.shape[2]
    n = local_rows * steps
    span = 32
    dtype = queries.dtype
    fork = fork_table.T
    sibling = [(i, i ^ 1) for i in range(tensors)]
    across = [(i, i ^ 2) for i in range(tensors)]

    received, pairs = exchange_pack(
        fork, partner, row_slot, queries, new_keys, new_values, fork_table, prompt_keys, prompt_values, span, moved
    )
    w_sib = lax.ppermute(out_proj, "tensor", sibling)
    local = (
        queries.reshape(n, width),
        new_keys.reshape(n, HEAD_DIM),
        new_values.reshape(n, HEAD_DIM),
        cache_keys.reshape(local_rows * suffix, HEAD_DIM),
        cache_values.reshape(local_rows * suffix, HEAD_DIM),
    )
    sizes = dict(local_rows=local_rows, steps=steps, slots=slots, suffix=suffix)
    lookup = (row_slot, prompt_lengths, cache_lengths, finished)

    dma = lambda *shape: pltpu.SemaphoreType.DMA(shape)
    blocks = local_rows // BLOCK
    nb = BLOCK * steps
    assert nb == HEAD_DIM
    cols = jnp.stack([place, place ^ 2]).astype(jnp.int32)
    heads, w_here, w_there = pl.pallas_call(
        functools.partial(attend_kernel, stacked=stacked, replicas=replicas, moved=moved, span=span, **sizes),
        out_shape=[
            pltpu.VMEM(((local_rows + moved) * steps, width), dtype),
            pltpu.VMEM((2 * width, model), dtype),
            pltpu.VMEM((2 * width, model), dtype),
        ],
        in_specs=[SMEM] * 7 + [ANY] * (9 + len(received)),
        out_specs=[VMEM] * 3,
        scratch_shapes=[
            pltpu.VMEM((slots * prefix, HEAD_DIM), dtype),
            pltpu.VMEM((slots * prefix, HEAD_DIM), dtype),
            pltpu.VMEM((blocks, nb, width), dtype),
            pltpu.VMEM((blocks, nb, HEAD_DIM), dtype),
            pltpu.VMEM((blocks, nb, HEAD_DIM), dtype),
            pltpu.VMEM((blocks, BLOCK * suffix, HEAD_DIM), dtype),
            pltpu.VMEM((blocks, BLOCK * suffix, HEAD_DIM), dtype),
            pltpu.VMEM((moved * span, HEAD_DIM), dtype),
            pltpu.VMEM((moved * suffix, HEAD_DIM), dtype),
            pltpu.VMEM((moved * suffix, HEAD_DIM), dtype),
            pltpu.VMEM((blocks, 3, nb, HEAD_DIM), jnp.int32),
            pltpu.VMEM((blocks, nb, HEAD_DIM), jnp.float32),
            pltpu.VMEM((3, moved * span, HEAD_DIM), jnp.int32),
            pltpu.VMEM((moved * span, HEAD_DIM), jnp.float32),
            pltpu.VMEM((blocks, groups, nb, HEAD_DIM), jnp.float32),
            pltpu.VMEM((blocks, groups * nb, slots * prefix + HEAD_DIM), jnp.bfloat16),
            pltpu.VMEM((blocks, groups, nb, 2 * HEAD_DIM), jnp.bfloat16),
            pltpu.VMEM((blocks, groups * nb, HEAD_DIM), jnp.float32),
            dma(blocks, 2, 3),
            dma(slots, 2),
            dma(moved),
            dma(moved, 2),
            dma(4),
        ],
        compiler_params=params(),
        name="attend",
    )(cols, fork, pairs, *lookup, *in_hbm(*local, prompt_keys, prompt_values, out_proj), w_sib, *received)

    sib = lax.ppermute(heads, "tensor", sibling)
    m = moved * steps

    def call(kernel, kind, name, *operands, specs):
        return pl.pallas_call(
            kernel,
            out_shape=[pltpu.VMEM((n, model), kind), pltpu.VMEM((m, model), kind)],
            in_specs=specs,
            out_specs=[VMEM, VMEM],
            compiler_params=params(),
            name=name,
        )(*operands)

    crossed, crossed_moved = call(
        project_kernel, dtype, "project", heads, sib, w_there, specs=[VMEM] * 3
    )
    got_moved = lax.ppermute(crossed_moved, "tensor", across)
    got = lax.ppermute(crossed, "tensor", across)
    base, base_moved = call(
        base_kernel, jnp.float32, "base", heads, sib, w_here, residual, crossed, specs=[VMEM] * 4 + [ANY]
    )

    back_shape = pltpu.VMEM((replicas if stacked else 4, steps, model), jnp.float32)
    back = pl.pallas_call(
        functools.partial(moved_sum_kernel, moved=moved, steps=steps, replicas=replicas, split=not stacked),
        out_shape=[back_shape] * (1 if stacked else 2),
        in_specs=[SMEM, VMEM, VMEM],
        out_specs=[VMEM] * (1 if stacked else 2),
        compiler_params=params(),
        name="moved_sum",
    )(pairs, base_moved, got_moved)
    if stacked:
        backs = [lax.all_to_all(back[0], "replica", split_axis=0, concat_axis=0, tiled=True)]
    else:
        flip = lambda x, bit: lax.ppermute(x, "replica", [(i, i ^ bit) for i in range(replicas)])
        kept = back[0]
        one = flip(back[1], 1)
        two = flip(jnp.concatenate([kept[2:], one[2:]]), 2)
        four = flip(jnp.concatenate([kept[1:2], one[1:2], two[1:2], two[3:4]]), 4)
        backs = [one, two, four]

    return pl.pallas_call(
        functools.partial(finish_kernel, moved=moved, replicas=replicas, split=not stacked),
        grid=(blocks,),
        in_specs=[SMEM, VMEM, VMEM, ANY] + [ANY] * len(backs),
        out_specs=pl.BlockSpec((BLOCK, steps, model), lambda i: (i, 0, 0)),
        out_shape=jax.ShapeDtypeStruct(residual.shape, residual.dtype),
        scratch_shapes=[
            pltpu.VMEM((moved, steps, model), jnp.float32),
            pltpu.VMEM((moved, steps, model), dtype),
            dma(moved, 2),
        ],
        compiler_params=params(),
        name="finish",
    )(pairs, base, got, *in_hbm(residual), *backs)


def solution(mesh):
    rows = P("replica", None, "tensor")
    in_specs = (rows,) * 6 + (P(), P(), P("replica"), P(), P(), rows, rows, P(), P("tensor", None))
    return jax.shard_map(body, mesh=mesh, in_specs=in_specs, out_specs=rows, check_vma=False)
```

time: 234 us -> 89.2 us (0.38)
  waiting for transfers between devices: 98.2 us -> 43.4 us
  local copies, waits for them, and re-layouts: 44.9 us -> 3.57 us
  matrix products: 30.7 us -> 0 us
  Pallas kernels: 0 us -> 21.1 us
  between operations: 13.8 us -> 0.11 us
  other arithmetic: 12.8 us -> 0.12 us
  starting transfers between devices: 32.4 us -> 20.7 us
    reduce_scatter x1 -> x0, waiting for transfers between devices: 86.7 us -> none  [body(): summed = lax.psum_scatter(terms, 'tensor', scatter_dimension=2, tiled=True)]
    ppermute x0 -> x14, waiting for transfers between devices: none -> 43.4 us  [the longest x1 27.7 us: body(): got_moved = lax.ppermute(crossed_moved, 'tensor', across)]
    gather x19 -> x0, local copies, waits for them, and re-layouts: 38.1 us -> none  [the longest x1 3.06 us: body(): pre_keys = slot_keys[my_slots]]
    all_to_all x6 -> x0, starting transfers between devices: 32.2 us -> none  [the longest x1 7.41 us: body(): lax.all_to_all(out_keys, 'replica', split_axis=0, concat_axis=0, tiled=True)]
    dot_general x7 -> x0, matrix products: 30.7 us -> none  [the longest x1 9.71 us: body(): jnp.einsum('bsh,hd->bsd', heads_out, out_proj, preferred_element_type=jnp...]
    pallas_call x0 -> x6, Pallas kernels: none -> 21.1 us  [the longest x1 10.3 us: body(): pl.pallas_call(functools.partial(attend_kernel, stacked=stacked, replicas...]
    ppermute x0 -> x14, starting transfers between devices: none -> 20.7 us  [the longest x7 12.7 us: exchange_pack(): lax.ppermute(packed[k - 1], 'replica', [(i, (i + k) % replicas) for i in...]
    all_to_all x6 -> x0, waiting for transfers between devices: 11.5 us -> none  [the longest x1 6.4 us: body(): lax.all_to_all(outgoing[3], 'replica', split_axis=0, concat_axis=0, tiled...]
  transfers between devices with their start and end apart: 7 -> 14, of which waited for: 3 -> 9; matrix products, arithmetic and copies ran while one was open for 24% -> 3% of each run, Pallas kernels for 0% -> 6%
where the time goes in v2:
time: 89.2 us; the launch traced here: 88.9 us
  waiting for transfers between devices  43.4 us (49%)
  Pallas kernels  21.1 us (24%)
  starting transfers between devices  20.7 us (23%)
  local copies, waits for them, and re-layouts  3.57 us (4%)
    ppermute x1, waiting for transfers between devices, body(): got_moved = lax.ppermute(crossed_moved, 'tensor', across)  27.7 us
    ppermute x7, starting transfers between devices, exchange_pack(): lax.ppermute(packed[k - 1], 'replica', [(i, (i + k) % replicas) for i in...  12.7 us
    pallas_call x1, Pallas kernels, body(): pl.pallas_call(functools.partial(attend_kernel, stacked=stacked, replicas...  10.3 us
    ppermute x3, waiting for transfers between devices, body(): lax.ppermute(x, 'replica', [(i, i ^ bit) for i in range(replicas)])  9.07 us
    ppermute x3, starting transfers between devices, body(): lax.ppermute(x, 'replica', [(i, i ^ bit) for i in range(replicas)])  5.33 us
    ppermute x7, waiting for transfers between devices, exchange_pack(): lax.ppermute(packed[k - 1], 'replica', [(i, (i + k) % replicas) for i in...  4.45 us
    pallas_call x2, Pallas kernels, call(): pl.pallas_call(kernel, out_shape=[pltpu.VMEM((n, model), kind), pltpu.VME...  3.89 us
    pallas_call x1, Pallas kernels, body(): pl.pallas_call(functools.partial(finish_kernel, moved=moved, replicas=rep...  3.34 us
  transfers between devices with their start and end apart: 14, of which 9 were waited for; matrix products, arithmetic and copies ran while one was open for 3% of the time, Pallas kernels for 6%

profile of v2, /device:TPU:0, one launch (start us, length us, event | category | flops | bytes accessed | tf_op | source)
XLA Modules:
  0.0 88.9 jit_solution(5241186643107719191)
XLA Ops:
  0.0 0.5 collective-permute-start
  0.5 0.7 copy-done.1
  1.1 0.7 copy-done.7
  1.8 3.0 %pack.1 = (bf16[288,128]{1,0:T(8,128)(2,1)S(1)}, bf16[288,128]{1,0:T(8,128)(2,1)S(1)}, bf16[288,128]{1,0:T(8,128)(2,1)S(1)}, bf16[288,128]{1,0:T(8,128)(2,1)S(1)...) custom-call(s32[4,8]{1,0:T(4,128)S(1)} %bitcast.7, ...), custom_call_target="tpu_custom_call" | custom-call | tf_op jit(solution)/shard_map/pack/pallas_call | solution.py:479
  4.8 2.6 %collective-permute-start.1 = (bf16[288,128]{1,0:T(8,128)(2,1)S(1)}, bf16[288,128]{1,0:T(8,128)(2,1)S(1)}, u32[]{:S(2)}, u32[]{:S(2)}) collective-permute-start(bf16[288,128]{1,0:T(8,128)(2,1)S(1)} %get-tuple-element.23), channel_id=1, source_target_pairs={{0,4},{4,8},{8,12},{12,16},{16,20},{20,24},{24,28},{28,0},{1,5},{5... | collective-permute-start | bytes 221192 | tf_op jit(solution)/shard_map/ppermute | solution.py:496
  7.4 1.6 %collective-permute-start.2 = (bf16[288,128]{1,0:T(8,128)(2,1)S(1)}, bf16[288,128]{1,0:T(8,128)(2,1)S(1)}, u32[]{:S(2)}, u32[]{:S(2)}) collective-permute-start(bf16[288,128]{1,0:T(8,128)(2,1)S(1)} %get-tuple-element.24), channel_id=1, source_target_pairs={{0,8},{4,12},{8,16},{12,20},{16,24},{20,28},{24,0},{28,4},{1,9},{5... | collective-permute-start | bytes 221192 | tf_op jit(solution)/shard_map/ppermute | solution.py:496
  9.0 2.5 %collective-permute-start.3 = (bf16[288,128]{1,0:T(8,128)(2,1)S(1)}, bf16[288,128]{1,0:T(8,128)(2,1)S(1)}, u32[]{:S(2)}, u32[]{:S(2)}) collective-permute-start(bf16[288,128]{1,0:T(8,128)(2,1)S(1)} %get-tuple-element.25), channel_id=1, source_target_pairs={{0,12},{4,16},{8,20},{12,24},{16,28},{20,0},{24,4},{28,8},{1,13},{... | collective-permute-start | bytes 221192 | tf_op jit(solution)/shard_map/ppermute | solution.py:496
  11.5 1.2 %collective-permute-start.4 = (bf16[288,128]{1,0:T(8,128)(2,1)S(1)}, bf16[288,128]{1,0:T(8,128)(2,1)S(1)}, u32[]{:S(2)}, u32[]{:S(2)}) collective-permute-start(bf16[288,128]{1,0:T(8,128)(2,1)S(1)} %get-tuple-element.26), channel_id=1, source_target_pairs={{0,16},{4,20},{8,24},{12,28},{16,0},{20,4},{24,8},{28,12},{1,17},{... | collective-permute-start | bytes 221192 | tf_op jit(solution)/shard_map/ppermute | solution.py:496
  12.7 2.2 %reshape.15.q = bf16[512,640]{1,0:T(8,128)(2,1)} reshape(bf16[128,4,640]{2,1,0:T(4,128)(2,1)} %queries.1) | data formatting | bytes 1310720 | tf_op jit(solution)/shard_map/reshape | solution.py:564
  14.9 2.6 %collective-permute-start.5 = (bf16[288,128]{1,0:T(8,128)(2,1)S(1)}, bf16[288,128]{1,0:T(8,128)(2,1)S(1)}, u32[]{:S(2)}, u32[]{:S(2)}) collective-permute-start(bf16[288,128]{1,0:T(8,128)(2,1)S(1)} %get-tuple-element.27), channel_id=1, source_target_pairs={{0,20},{4,24},{8,28},{12,0},{16,4},{20,8},{24,12},{28,16},{1,21},{... | collective-permute-start | bytes 221192 | tf_op jit(solution)/shard_map/ppermute | solution.py:496
  17.6 1.3 %collective-permute-start.6 = (bf16[288,128]{1,0:T(8,128)(2,1)S(1)}, bf16[288,128]{1,0:T(8,128)(2,1)S(1)}, u32[]{:S(2)}, u32[]{:S(2)}) collective-permute-start(bf16[288,128]{1,0:T(8,128)(2,1)S(1)} %get-tuple-element.28), channel_id=1, source_target_pairs={{0,24},{4,28},{8,0},{12,4},{16,8},{20,12},{24,16},{28,20},{1,25},{... | collective-permute-start | bytes 221192 | tf_op jit(solution)/shard_map/ppermute | solution.py:496
  18.9 0.9 %collective-permute-done.3.rest_2_ = bf16[288,128]{1,0:T(8,128)(2,1)S(1)} collective-permute-done((bf16[288,128]{1,0:T(8,128)(2,1)S(1)}, bf16[288,128]{1,0:T(8,128)(2,1)S(1)}, u32[]{:S(2)}, u32[]{:S(2)}) %collective-permute-start.3) | collective-permute-done | bytes 73760 | tf_op jit(solution)/shard_map/ppermute | solution.py:496
  19.9 0.8 collective-permute-start.7
  20.7 0.1 pad_add_fusion.cols
  20.7 2.3 %collective-permute-done.5.rest_4_ = bf16[288,128]{1,0:T(8,128)(2,1)S(1)} collective-permute-done((bf16[288,128]{1,0:T(8,128)(2,1)S(1)}, bf16[288,128]{1,0:T(8,128)(2,1)S(1)}, u32[]{:S(2)}, u32[]{:S(2)}) %collective-permute-start.5) | collective-permute-done | bytes 73760 | tf_op jit(solution)/shard_map/ppermute | solution.py:496
  23.0 0.2 collective-permute-done.6.rest_5_
  23.2 1.0 %collective-permute-done.7.rest_6_ = bf16[288,128]{1,0:T(8,128)(2,1)S(1)} collective-permute-done((bf16[288,128]{1,0:T(8,128)(2,1)S(1)}, bf16[288,128]{1,0:T(8,128)(2,1)S(1)}, u32[]{:S(2)}, u32[]{:S(2)}) %collective-permute-start.7) | collective-permute-done | bytes 73760 | tf_op jit(solution)/shard_map/ppermute | solution.py:496
  24.3 10.3 %attend.1 = (bf16[528,640]{1,0:T(8,128)(2,1)S(1)}, bf16[1280,1280]{1,0:T(8,128)(2,1)S(1)}, bf16[1280,1280]{1,0:T(8,128)(2,1)S(1)}) custom-call(s32[2]{0:T(128)S(1)} %pad_add_fusion.cols, s32[4,8]{1,0:T(4,128)S(1)} %bitcast.8, s32[10]{0:T(128)S(1)} %get-tuple-element.22.pairs, s32[1024]{0:T(1024)S(1)} %copy-done.3, s32[32]{0:T(128)S(1)} %copy-done.6, ...), custom_call_target="tpu_custom_call" | custom-call | tf_op jit(solution)/shard_map/attend/pallas_call | solution.py:578
  34.6 2.1 %collective-permute-done.8.h_sib = bf16[528,640]{1,0:T(8,128)(2,1)S(1)} collective-permute-done((bf16[528,640]{1,0:T(8,128)(2,1)S(1)}, bf16[528,640]{1,0:T(8,128)(2,1)S(1)}, u32[]{:S(2)}, u32[]{:S(2)}) %collective-permute-start.8) | collective-permute-done | bytes 675872 | tf_op jit(solution)/shard_map/ppermute | solution.py:616
  36.8 1.9 %project.1 = (bf16[512,1280]{1,0:T(8,128)(2,1)S(1)}, bf16[16,1280]{1,0:T(8,128)(2,1)S(1)}) custom-call(bf16[528,640]{1,0:T(8,128)(2,1)S(1)} %get-tuple-element.30.h_own, bf16[528,640]{1,0:T(8,128)(2,1)S(1)} %collective-permute-done.8.h_sib, bf16[1280,1280]{1,0:T(8,128)(2,1)S(1)} %get-tuple-element.32.weights), custom_call_target="tpu_custom_call" | custom-call | tf_op jit(solution)/shard_map/project/pallas_call | solution.py:620
  38.7 1.6 %collective-permute-start.9 = (bf16[512,1280]{1,0:T(8,128)(2,1)S(1)}, bf16[512,1280]{1,0:T(8,128)(2,1)S(1)}, u32[]{:S(2)}, u32[]{:S(2)}) collective-permute-start(bf16[512,1280]{1,0:T(8,128)(2,1)S(1)} %get-tuple-element.33.after), channel_id=1, source_target_pairs={{0,2},{1,3},{2,0},{3,1},{4,6},{5,7},{6,4},{7,5},{8,10},{9,11},{10,... | collective-permute-start | bytes 3932168 | tf_op jit(solution)/shard_map/ppermute | solution.py:633
  40.3 0.5 collective-permute-start.10
  40.8 2.0 %base.1 = (f32[512,1280]{1,0:T(8,128)S(1)}, f32[16,1280]{1,0:T(8,128)S(1)}) custom-call(bf16[528,640]{1,0:T(8,128)(2,1)S(1)} %get-tuple-element.30.h_own, bf16[528,640]{1,0:T(8,128)(2,1)S(1)} %collective-permute-done.8.h_sib, bf16[1280,1280]{1,0:T(8,128)(2,1)S(1)} %get-tuple-element.31.weights, bf16[128,4,1280]{2,1,0:T(4,128)(2,1)S(1)} %copy-done, ...), custom_call_target="tpu_custom_call" | custom-call | tf_op jit(solution)/shard_map/base/pallas_call | solution.py:620
  42.8 27.7 %collective-permute-done.10.recv = bf16[16,1280]{1,0:T(8,128)(2,1)S(1)} collective-permute-done((bf16[16,1280]{1,0:T(8,128)(2,1)S(1)}, bf16[16,1280]{1,0:T(8,128)(2,1)S(1)}, u32[]{:S(2)}, u32[]{:S(2)}) %collective-permute-start.10) | collective-permute-done | bytes 40992 | tf_op jit(solution)/shard_map/ppermute | solution.py:632
  70.5 0.6 moved_sum.1
  71.1 1.3 %collective-permute-start.11 = (f32[4,4,1280]{2,1,0:T(4,128)S(1)}, f32[4,4,1280]{2,1,0:T(4,128)S(1)}, u32[]{:S(2)}, u32[]{:S(2)}) collective-permute-start(f32[4,4,1280]{2,1,0:T(4,128)S(1)} %get-tuple-element.37), channel_id=1, source_target_pairs={{0,4},{4,0},{8,12},{12,8},{16,20},{20,16},{24,28},{28,24},{1,5},{5... | collective-permute-start | bytes 245768 | tf_op jit(solution)/shard_map/ppermute | solution.py:650
  72.5 3.2 %collective-permute-done.11.rest_0_ = f32[4,4,1280]{2,1,0:T(4,128)S(1)} collective-permute-done((f32[4,4,1280]{2,1,0:T(4,128)S(1)}, f32[4,4,1280]{2,1,0:T(4,128)S(1)}, u32[]{:S(2)}, u32[]{:S(2)}) %collective-permute-start.11) | collective-permute-done | bytes 81952 | tf_op jit(solution)/shard_map/ppermute | solution.py:650
  75.6 1.2 %collective-permute-start.12 = (f32[4,4,1280]{2,1,0:T(4,128)S(1)}, f32[4,4,1280]{2,1,0:T(4,128)S(1)}, u32[]{:S(2)}, u32[]{:S(2)}) collective-permute-start(f32[4,4,1280]{2,1,0:T(4,128)S(1)} %pad_maximum_fusion), channel_id=1, source_target_pairs={{0,8},{4,12},{8,0},{12,4},{16,24},{20,28},{24,16},{28,20},{1,9},{5... | collective-permute-start | bytes 245768 | tf_op jit(solution)/shard_map/ppermute | solution.py:650
  76.8 3.3 %collective-permute-done.12.rest_1_ = f32[4,4,1280]{2,1,0:T(4,128)S(1)} collective-permute-done((f32[4,4,1280]{2,1,0:T(4,128)S(1)}, f32[4,4,1280]{2,1,0:T(4,128)S(1)}, u32[]{:S(2)}, u32[]{:S(2)}) %collective-permute-start.12) | collective-permute-done | bytes 81952 | tf_op jit(solution)/shard_map/ppermute | solution.py:650
  80.2 2.8 %collective-permute-start.13 = (f32[4,4,1280]{2,1,0:T(4,128)S(1)}, f32[4,4,1280]{2,1,0:T(4,128)S(1)}, u32[]{:S(2)}, u32[]{:S(2)}) collective-permute-start(f32[4,4,1280]{2,1,0:T(4,128)S(1)} %pad_maximum_fusion.1), channel_id=1, source_target_pairs={{0,16},{4,20},{8,24},{12,28},{16,0},{20,4},{24,8},{28,12},{1,17},{... | collective-permute-start | bytes 245768 | tf_op jit(solution)/shard_map/ppermute | solution.py:650
  83.0 2.6 %collective-permute-done.13.rest_2_ = f32[4,4,1280]{2,1,0:T(4,128)S(1)} collective-permute-done((f32[4,4,1280]{2,1,0:T(4,128)S(1)}, f32[4,4,1280]{2,1,0:T(4,128)S(1)}, u32[]{:S(2)}, u32[]{:S(2)}) %collective-permute-start.13) | collective-permute-done | bytes 81952 | tf_op jit(solution)/shard_map/ppermute | solution.py:650
  85.6 3.3 %finish.1 = bf16[128,4,1280]{2,1,0:T(4,128)(2,1)} custom-call(s32[10]{0:T(128)S(1)} %get-tuple-element.22.pairs, f32[512,1280]{1,0:T(8,128)S(1)} %get-tuple-element.34.base, bf16[512,1280]{1,0:T(8,128)(2,1)S(1)} %collective-permute-done.9.recv, bf16[128,4,1280]{2,1,0:T(4,128)(2,1)} %residual.3, f32[4,4,1280]{2,1,0:T(4,128)S(1)} %collective-permute-done.11.rest_0_, ...), custom_call_target="tpu_custom_call" | custom-call | tf_op jit(solution)/shard_map/finish/pallas_call | solution.py:657
  (27 shorter events, 0.2 us)
Async XLA Ops:
  0.0 24.2 %copy-start.6 = (s32[32]{0:T(128)S(1)}, s32[32]{0:T(128)}, u32[]{:S(2)}) copy-start(s32[32]{0:T(128)} %prompt_lengths.1) | copy-start | bytes 388
  0.0 24.2 %collective-permute-start = (bf16[640,5120]{1,0:T(8,128)(2,1)}, bf16[640,5120]{1,0:T(8,128)(2,1)}, u32[]{:S(2)}, u32[]{:S(2)}) collective-permute-start(bf16[640,5120]{1,0:T(8,128)(2,1)} %w_own.1), channel_id=1, source_target_pairs={{0,1},{1,0},{2,3},{3,2},{4,5},{5,4},{6,7},{7,6},{8,9},{9,8},{10,11... | collective-permute-start | bytes 19660808 | tf_op jit(solution)/shard_map/ppermute | solution.py:562
  0.5 0.7 copy-start.1
  1.1 0.7 copy-start.7
  1.8 22.5 %copy-start.2 = (s32[8,4]{0,1:T(4,128)S(1)}, s32[8,4]{0,1:T(4,128)}, u32[]{:S(2)}) copy-start(s32[8,4]{0,1:T(4,128)} %param.25) | copy-start | bytes 388
  1.8 22.5 %copy-start.3 = (s32[1024]{0:T(1024)S(1)}, s32[1024]{0:T(1024)}, u32[]{:S(2)}) copy-start(s32[1024]{0:T(1024)} %row_slot.1) | copy-start | bytes 12292
  1.8 22.5 %copy-start.4 = (s32[1024]{0:T(1024)S(1)}, s32[1024]{0:T(1024)}, u32[]{:S(2)}) copy-start(s32[1024]{0:T(1024)} %cache_lengths.1) | copy-start | bytes 12292
  1.8 22.5 %copy-start.5 = (s32[1024]{0:T(1024)S(1)}, s32[1024]{0:T(1024)}, u32[]{:S(2)}) copy-start(s32[1024]{0:T(1024)} %finished.1) | copy-start | bytes 12292
  4.8 10.1 %collective-permute-start.1 = (bf16[288,128]{1,0:T(8,128)(2,1)S(1)}, bf16[288,128]{1,0:T(8,128)(2,1)S(1)}, u32[]{:S(2)}, u32[]{:S(2)}) collective-permute-start(bf16[288,128]{1,0:T(8,128)(2,1)S(1)} %get-tuple-element.23), channel_id=1, source_target_pairs={{0,4},{4,8},{8,12},{12,16},{16,20},{20,24},{24,28},{28,0},{1,5},{5... | collective-permute-start | bytes 221192 | tf_op jit(solution)/shard_map/ppermute | solution.py:496
  7.4 10.2 %collective-permute-start.2 = (bf16[288,128]{1,0:T(8,128)(2,1)S(1)}, bf16[288,128]{1,0:T(8,128)(2,1)S(1)}, u32[]{:S(2)}, u32[]{:S(2)}) collective-permute-start(bf16[288,128]{1,0:T(8,128)(2,1)S(1)} %get-tuple-element.24), channel_id=1, source_target_pairs={{0,8},{4,12},{8,16},{12,20},{16,24},{20,28},{24,0},{28,4},{1,9},{5... | collective-permute-start | bytes 221192 | tf_op jit(solution)/shard_map/ppermute | solution.py:496
  9.0 10.9 %collective-permute-start.3 = (bf16[288,128]{1,0:T(8,128)(2,1)S(1)}, bf16[288,128]{1,0:T(8,128)(2,1)S(1)}, u32[]{:S(2)}, u32[]{:S(2)}) collective-permute-start(bf16[288,128]{1,0:T(8,128)(2,1)S(1)} %get-tuple-element.25), channel_id=1, source_target_pairs={{0,12},{4,16},{8,20},{12,24},{16,28},{20,0},{24,4},{28,8},{1,13},{... | collective-permute-start | bytes 221192 | tf_op jit(solution)/shard_map/ppermute | solution.py:496
  11.5 9.2 %collective-permute-start.4 = (bf16[288,128]{1,0:T(8,128)(2,1)S(1)}, bf16[288,128]{1,0:T(8,128)(2,1)S(1)}, u32[]{:S(2)}, u32[]{:S(2)}) collective-permute-start(bf16[288,128]{1,0:T(8,128)(2,1)S(1)} %get-tuple-element.26), channel_id=1, source_target_pairs={{0,16},{4,20},{8,24},{12,28},{16,0},{20,4},{24,8},{28,12},{1,17},{... | collective-permute-start | bytes 221192 | tf_op jit(solution)/shard_map/ppermute | solution.py:496
  14.9 8.1 %collective-permute-start.5 = (bf16[288,128]{1,0:T(8,128)(2,1)S(1)}, bf16[288,128]{1,0:T(8,128)(2,1)S(1)}, u32[]{:S(2)}, u32[]{:S(2)}) collective-permute-start(bf16[288,128]{1,0:T(8,128)(2,1)S(1)} %get-tuple-element.27), channel_id=1, source_target_pairs={{0,20},{4,24},{8,28},{12,0},{16,4},{20,8},{24,12},{28,16},{1,21},{... | collective-permute-start | bytes 221192 | tf_op jit(solution)/shard_map/ppermute | solution.py:496
  17.6 5.7 %collective-permute-start.6 = (bf16[288,128]{1,0:T(8,128)(2,1)S(1)}, bf16[288,128]{1,0:T(8,128)(2,1)S(1)}, u32[]{:S(2)}, u32[]{:S(2)}) collective-permute-start(bf16[288,128]{1,0:T(8,128)(2,1)S(1)} %get-tuple-element.28), channel_id=1, source_target_pairs={{0,24},{4,28},{8,0},{12,4},{16,8},{20,12},{24,16},{28,20},{1,25},{... | collective-permute-start | bytes 221192 | tf_op jit(solution)/shard_map/ppermute | solution.py:496
  19.9 4.4 %collective-permute-start.7 = (bf16[288,128]{1,0:T(8,128)(2,1)S(1)}, bf16[288,128]{1,0:T(8,128)(2,1)S(1)}, u32[]{:S(2)}, u32[]{:S(2)}) collective-permute-start(bf16[288,128]{1,0:T(8,128)(2,1)S(1)} %get-tuple-element.29), channel_id=1, source_target_pairs={{0,28},{4,0},{8,4},{12,8},{16,12},{20,16},{24,20},{28,24},{1,29},{... | collective-permute-start | bytes 221192 | tf_op jit(solution)/shard_map/ppermute | solution.py:496
  34.6 2.2 %collective-permute-start.8 = (bf16[528,640]{1,0:T(8,128)(2,1)S(1)}, bf16[528,640]{1,0:T(8,128)(2,1)S(1)}, u32[]{:S(2)}, u32[]{:S(2)}) collective-permute-start(bf16[528,640]{1,0:T(8,128)(2,1)S(1)} %get-tuple-element.30.h_own), channel_id=1, source_target_pairs={{0,1},{1,0},{2,3},{3,2},{4,5},{5,4},{6,7},{7,6},{8,9},{9,8},{10,11... | collective-permute-start | bytes 2027528 | tf_op jit(solution)/shard_map/ppermute | solution.py:616
  36.8 4.0 %copy-start = (bf16[128,4,1280]{2,1,0:T(4,128)(2,1)S(1)}, bf16[128,4,1280]{2,1,0:T(4,128)(2,1)}, u32[]{:S(2)}) copy-start(bf16[128,4,1280]{2,1,0:T(4,128)(2,1)} %residual.3) | copy-start | bytes 3932164
  38.7 46.9 %collective-permute-start.9 = (bf16[512,1280]{1,0:T(8,128)(2,1)S(1)}, bf16[512,1280]{1,0:T(8,128)(2,1)S(1)}, u32[]{:S(2)}, u32[]{:S(2)}) collective-permute-start(bf16[512,1280]{1,0:T(8,128)(2,1)S(1)} %get-tuple-element.33.after), channel_id=1, source_target_pairs={{0,2},{1,3},{2,0},{3,1},{4,6},{5,7},{6,4},{7,5},{8,10},{9,11},{10,... | collective-permute-start | bytes 3932168 | tf_op jit(solution)/shard_map/ppermute | solution.py:633
  40.3 30.2 %collective-permute-start.10 = (bf16[16,1280]{1,0:T(8,128)(2,1)S(1)}, bf16[16,1280]{1,0:T(8,128)(2,1)S(1)}, u32[]{:S(2)}, u32[]{:S(2)}) collective-permute-start(bf16[16,1280]{1,0:T(8,128)(2,1)S(1)} %get-tuple-element.36), channel_id=1, source_target_pairs={{0,2},{1,3},{2,0},{3,1},{4,6},{5,7},{6,4},{7,5},{8,10},{9,11},{10,... | collective-permute-start | bytes 122888 | tf_op jit(solution)/shard_map/ppermute | solution.py:632
  71.1 4.5 %collective-permute-start.11 = (f32[4,4,1280]{2,1,0:T(4,128)S(1)}, f32[4,4,1280]{2,1,0:T(4,128)S(1)}, u32[]{:S(2)}, u32[]{:S(2)}) collective-permute-start(f32[4,4,1280]{2,1,0:T(4,128)S(1)} %get-tuple-element.37), channel_id=1, source_target_pairs={{0,4},{4,0},{8,12},{12,8},{16,20},{20,16},{24,28},{28,24},{1,5},{5... | collective-permute-start | bytes 245768 | tf_op jit(solution)/shard_map/ppermute | solution.py:650
  75.6 4.5 %collective-permute-start.12 = (f32[4,4,1280]{2,1,0:T(4,128)S(1)}, f32[4,4,1280]{2,1,0:T(4,128)S(1)}, u32[]{:S(2)}, u32[]{:S(2)}) collective-permute-start(f32[4,4,1280]{2,1,0:T(4,128)S(1)} %pad_maximum_fusion), channel_id=1, source_target_pairs={{0,8},{4,12},{8,0},{12,4},{16,24},{20,28},{24,16},{28,20},{1,9},{5... | collective-permute-start | bytes 245768 | tf_op jit(solution)/shard_map/ppermute | solution.py:650
  80.2 5.4 %collective-permute-start.13 = (f32[4,4,1280]{2,1,0:T(4,128)S(1)}, f32[4,4,1280]{2,1,0:T(4,128)S(1)}, u32[]{:S(2)}, u32[]{:S(2)}) collective-permute-start(f32[4,4,1280]{2,1,0:T(4,128)S(1)} %pad_maximum_fusion.1), channel_id=1, source_target_pairs={{0,16},{4,20},{8,24},{12,28},{16,0},{20,4},{24,8},{28,12},{1,17},{... | collective-permute-start | bytes 245768 | tf_op jit(solution)/shard_map/ppermute | solution.py:650

commit v3 on v2

--- a/solution.py
+++ b/solution.py
@@ -166,6 +166,49 @@
             cache_scores[h, r0 + 8 : r0 + 16, :] = s[16 * h + 8 : 16 * h + 16, half:]
 
 
+def stage_kernel(
+    cols, fork, pairs, row_slot, prompt_lengths, cache_lengths, finished, queries, keys, values, weights, sibling,
+    q, scores, cv, w_there, row_meta, alive_rows, moved_keys, moved_values, moved_meta, moved_alive,
+    qv, ckv, sems, *, moved, slots, suffix, span
+):
+    local_rows, steps, width = queries.shape
+    blocks = scores.shape[0]
+    rows = local_rows // blocks
+    n = rows * steps
+    per = 16 // steps
+    first = load([(queries, qv)], sems.at[0])
+    ready = [
+        load([(keys.at[pl.ds(i * rows * suffix, rows * suffix)], ckv.at[i])], sems.at[1 + i]) for i in range(blocks)
+    ]
+    model = w_there.shape[1]
+    at = pl.ds(pl.multiple_of(cols[1] * model, HEAD_DIM), model)
+    copies = [
+        (values, cv),
+        (weights.at[:, at], w_there.at[pl.ds(0, width)]),
+        (sibling.at[:, at], w_there.at[pl.ds(width, width)]),
+    ]
+    for i in range(moved):
+        source = pl.ds(pl.multiple_of(pairs[i] * suffix, suffix), suffix)
+        target = pl.ds(i * suffix, suffix)
+        copies += [(keys.at[source], moved_keys.at[target]), (values.at[source], moved_values.at[target])]
+    rest = load(copies, sems.at[1 + blocks])
+    me = lax.axis_index("replica")
+    lookup = (row_slot, fork, prompt_lengths, cache_lengths, finished, me, slots, local_rows)
+    for b in range(local_rows):
+        i, low = b // rows, b % rows * steps
+        fill_meta(lookup, b, slice(low, low + steps), row_meta.at[i], alive_rows.at[i])
+    for i in range(moved):
+        fill_meta(lookup, pairs[i], slice(i * span, (i + 1) * span), moved_meta, moved_alive)
+    first()
+    for b in range(0, local_rows, per):
+        part = [qv[b + i].astype(jnp.float32) for i in range(per)]
+        q[b * steps : (b + per) * steps, :] = jnp.concatenate(part, axis=0).astype(q.dtype)
+    for i in range(blocks):
+        ready[i]()
+        attend_scores(q.at[pl.ds(i * n, n)], ckv.at[i], scores.at[i], steps=steps, suffix=suffix)
+    rest()
+
+
 def attend_block(
     q, nk, nv, cv, pk, pv, heads, row_meta, alive_rows, cache_scores, weights, cache_weights, mixed,
     *, steps, slots, suffix
@@ -211,7 +254,7 @@
             ).astype(heads.dtype)
 
 
-def moved_block(x, pk, pv, keys, values, slot, plen, clen, alive, wait, *, steps, slots, groups, span, suffix):
+def moved_block(x, pk, pv, keys, values, slot, plen, clen, alive, *, steps, slots, groups, span, suffix):
     prefix = pk.shape[0] // slots
     shape = (4 * span, HEAD_DIM)
     lane, row = iota(shape, 1), iota(shape, 0)
@@ -221,7 +264,6 @@
     new_mask = ((lane // span) == (row // span)) & (past >= 0) & (past <= row % steps)
     prompt = pick_slot(matmul(x, pk[...], NT), slot, slots, prefix)
     new = matmul(x, x, NT)
-    wait()
     cache = matmul(x, keys[...], NT)
     half = 2 * suffix
     top_half = row < 2 * span
@@ -246,26 +288,17 @@
 
 
 def attend_kernel(
-    cols, fork, pairs, row_slot, prompt_lengths, cache_lengths, finished, q, nk, nv, ck, cv, own_keys, own_values,
-    w_own, w_sib, *rest, stacked, replicas, slots, moved, local_rows, steps, suffix, span
+    fork, pairs, q, nk, nv, cache_scores, cv, row_meta, alive_rows, keys, values, moved_meta, moved_alive, own_keys,
+    own_values, *rest, stacked, replicas, slots, moved, steps, suffix, span
 ):
     count = 1 if stacked else replicas - 1
     recvs, rest = rest[:count], rest[count:]
-    heads, w_here, w_there = rest[:3]
-    pk, pv, qv, nkv, nvv, ckv, cvv, x, keys, values = rest[3:13]
-    row_meta, alive_rows, moved_meta, moved_alive, cache_scores, weights, cache_weights, mixed = rest[13:21]
-    local_sems, sems, moved_sems, cache_sems, w_sems = rest[21:]
+    heads, pk, pv, x, weights, cache_weights, mixed, sems, moved_sems = rest
     me = lax.axis_index("replica")
     held, prefix = own_keys.shape[0], own_keys.shape[1]
-    blocks, n = qv.shape[:2]
-    groups = qv.shape[2] // HEAD_DIM
+    blocks, n = row_meta.shape[0], row_meta.shape[2]
+    groups = q.shape[1] // HEAD_DIM
     rows = n // steps
-    local = (q, nk, nv, ck, cv)
-    buffers = [[v.at[i] for v in (qv, nkv, nvv, ckv, cvv)] for i in range(blocks)]
-    spans = [(pl.ds(i * n, n), pl.ds(i * rows * suffix, rows * suffix)) for i in range(blocks)]
-    scores_ready = [
-        load([(q.at[a], qv.at[i]), (ck.at[b], ckv.at[i])], local_sems.at[i, 0]) for i, (a, b) in enumerate(spans)
-    ]
     for s in range(slots):
         prompt = fork[s, me]
         owner = lax.div(prompt, held)
@@ -311,65 +344,20 @@
                         moved_sems.at[i],
                     ).start()
 
-    cache_copies = []
-    for i in range(moved):
-        r = pairs[i]
-        for j, (source, target) in enumerate(((ck, keys), (cv, values))):
-            copy = pltpu.make_async_copy(
-                source.at[pl.ds(pl.multiple_of(r * suffix, suffix), suffix)],
-                target.at[pl.ds(i * suffix, suffix)],
-                cache_sems.at[i, j],
-            )
-            copy.start()
-            cache_copies.append(copy)
-    lookup = (row_slot, fork, prompt_lengths, cache_lengths, finished, me, slots, local_rows)
-    for i in range(moved):
-        fill_meta(lookup, pairs[i], slice(i * span, (i + 1) * span), moved_meta, moved_alive)
-
-    rest_ready = [
-        load([(nk.at[a], nkv.at[i]), (nv.at[a], nvv.at[i]), (cv.at[b], cvv.at[i])], local_sems.at[i, 1])
-        for i, (a, b) in enumerate(spans)
-    ]
-    width, model = w_own.shape[0], w_there.shape[1]
-    weights_ready = load(
-        [
-            (w.at[:, pl.ds(pl.multiple_of(cols[i] * model, HEAD_DIM), model)], target.at[pl.ds(j * width, width)])
-            for i, target in enumerate((w_here, w_there))
-            for j, w in enumerate((w_own, w_sib))
-        ],
-        w_sems,
-    )
-    for b in range(local_rows):
-        i, at = b // rows, b % rows
-        fill_meta(lookup, b, slice(at * steps, (at + 1) * steps), row_meta.at[i], alive_rows.at[i])
-    def wait_prompts():
-        for s in range(slots):
-            for i, target in enumerate((pk, pv)):
-                pltpu.make_async_copy(
-                    own_keys.at[0], target.at[pl.ds(s * prefix, prefix)], sems.at[s, i]
-                ).wait()
-
-    sizes = dict(steps=steps, suffix=suffix)
+    for s in range(slots):
+        for i, target in enumerate((pk, pv)):
+            pltpu.make_async_copy(own_keys.at[0], target.at[pl.ds(s * prefix, prefix)], sems.at[s, i]).wait()
     for i in range(blocks):
-        scores_ready[i]()
-        attend_scores(qv.at[i], ckv.at[i], cache_scores.at[i], **sizes)
-    wait_prompts()
-    for ready in rest_ready:
-        ready()
-    for i in range(blocks):
+        part = pl.ds(i * n, n)
         attend_block(
-            qv.at[i], nkv.at[i], nvv.at[i], cvv.at[i], pk, pv, heads.at[pl.ds(i * n, n)], row_meta.at[i],
-            alive_rows.at[i], cache_scores.at[i], weights.at[i], cache_weights.at[i], mixed.at[i],
-            slots=slots, **sizes,
+            q.at[part], nk.at[part], nv.at[part], cv.at[pl.ds(i * rows * suffix, rows * suffix)], pk, pv,
+            heads.at[part], row_meta.at[i], alive_rows.at[i], cache_scores.at[i], weights.at[i],
+            cache_weights.at[i], mixed.at[i], steps=steps, slots=slots, suffix=suffix,
         )
     for i in range(moved):
         pltpu.make_async_copy(
             own_keys.at[0, pl.ds(0, span)], x.at[pl.ds(i * span, span)], moved_sems.at[i]
         ).wait()
-
-    def wait_caches():
-        for copy in cache_copies:
-            copy.wait()
 
     first = blocks * n
     for g in range(moved // 4):
@@ -378,35 +366,44 @@
         heads[first + g * 4 * steps : first + (g + 1) * 4 * steps, :] = moved_block(
             x[part, :], pk, pv, keys.at[kpart], values.at[kpart],
             moved_meta[0, part, :], moved_meta[1, part, :], moved_meta[2, part, :], moved_alive[part, :],
-            wait_caches if g == 0 else (lambda: None),
             steps=steps, slots=slots, groups=groups, span=span, suffix=suffix,
         )
-    weights_ready()
-
-
-def project_kernel(h_own, h_sib, weights, out, moved_out):
-    rows = out.shape[0]
-    total = matmul(jnp.concatenate([h_own[...], h_sib[...]], axis=1), weights[...], NN)
-    out[...] = total[:rows].astype(out.dtype)
-    moved_out[...] = total[rows:].astype(out.dtype)
-
-
-def base_kernel(h_own, h_sib, weights, residual, after, out, moved_out):
-    rows = out.shape[0]
+
+
+def project_kernel(h_own, h_sib, weights, out):
+    rows = pl.ds(0, out.shape[0])
+    both = jnp.concatenate([h_own[rows, :], h_sib[rows, :]], axis=1)
+    out[...] = matmul(both, weights[...], NN).astype(out.dtype)
+
+
+def base_kernel(cols, h_own, h_sib, w_own, w_sib, residual, after, out, weights, before, sems):
+    rows, model = out.shape
+    width = w_own.shape[0]
     steps = residual.shape[1]
-    total = matmul(jnp.concatenate([h_own[...], h_sib[...]], axis=1), weights[...], NN)
-    moved_out[...] = total[rows:]
-    for b in range(rows // steps):
+    at = pl.ds(pl.multiple_of(cols[0] * model, HEAD_DIM), model)
+    ready = load(
+        [
+            (w_own.at[:, at], weights.at[pl.ds(0, width)]),
+            (w_sib.at[:, at], weights.at[pl.ds(width, width)]),
+            (residual, before),
+        ],
+        sems,
+    )
+    both = jnp.concatenate([h_own[pl.ds(0, rows), :], h_sib[pl.ds(0, rows), :]], axis=1)
+    ready()
+    total = matmul(both, weights[...], NN)
+    for b in range(residual.shape[0]):
         part = slice(b * steps, (b + 1) * steps)
-        out[part, :] = total[part] + residual[b].astype(jnp.float32)
-
-
-def moved_sum_kernel(pairs, base, recv, *outs, moved, steps, replicas, split):
+        out[part, :] = total[part] + before[b].astype(jnp.float32)
+
+
+def moved_send_kernel(pairs, h_own, h_sib, after, *outs, moved, steps, split):
     me = lax.axis_index("replica")
-    total = base[...] + recv[...].astype(jnp.float32)
+    rows = pl.ds(h_own.shape[0] - moved * steps, moved * steps)
+    both = jnp.concatenate([h_own[rows, :], h_sib[rows, :]], axis=1).astype(jnp.float32)
     for i in range(moved):
         peer = pairs[moved + 1 + i]
-        value = total[i * steps : (i + 1) * steps, :]
+        value = both[i * steps : (i + 1) * steps].astype(outs[0].dtype)
         if split:
             k = jnp.bitwise_xor(me, peer)
             place = 2 * lax.rem(lax.div(k, 2), 2) + lax.div(k, 4)
@@ -423,28 +420,39 @@
             outs[0][peer] = value
 
 
-def finish_kernel(pairs, base, recv, residual, *rest, moved, replicas, split):
-    backs, (out, branch, before, sems) = rest[:-4], rest[-4:]
+def moved_project_kernel(pairs, w_here, w_there, *rest, moved, steps, split):
+    backs, (cross, base, heads) = rest[:-3], rest[-3:]
     me = lax.axis_index("replica")
+    for i in range(moved):
+        peer = pairs[moved + 1 + i]
+        part = slice(i * steps, (i + 1) * steps)
+        if split:
+            k = jnp.bitwise_xor(me, peer)
+            places = {1: (0, 0), 2: (1, 0), 3: (1, 2), 4: (2, 0), 5: (2, 1), 6: (2, 2), 7: (2, 3)}
+            for d, (which, index) in places.items():
+
+                @pl.when(k == d)
+                def _():
+                    heads[part, :] = backs[which][index].astype(jnp.float32)
+
+        else:
+            heads[part, :] = backs[0][peer].astype(jnp.float32)
+    both = heads[...].astype(cross.dtype)
+    cross[...] = matmul(both, w_there[...], NN).astype(cross.dtype)
+    base[...] = matmul(both, w_here[...], NN)
+
+
+def finish_kernel(pairs, base, recv, base_moved, recv_moved, residual, out, before, sems, *, moved):
     step = pl.program_id(0)
     rows, steps = out.shape[:2]
+    copies = [
+        pltpu.make_async_copy(residual.at[pairs[i]], before.at[i], sems.at[i]) for i in range(moved)
+    ]
 
     @pl.when(step == 0)
     def _():
-        for i in range(moved):
-            peer = pairs[moved + 1 + i]
-            pltpu.make_async_copy(residual.at[pairs[i]], before.at[i], sems.at[i, 0]).start()
-            if split:
-                k = jnp.bitwise_xor(me, peer)
-                places = {1: (0, 0), 2: (1, 0), 3: (1, 2), 4: (2, 0), 5: (2, 1), 6: (2, 2), 7: (2, 3)}
-                for d, (which, index) in places.items():
-
-                    @pl.when(k == d)
-                    def _():
-                        pltpu.make_async_copy(backs[which].at[index], branch.at[i], sems.at[i, 1]).start()
-
-            else:
-                pltpu.make_async_copy(backs[0].at[peer], branch.at[i], sems.at[i, 1]).start()
+        for copy in copies:
+            copy.start()
 
     part = pl.ds(pl.multiple_of(step * rows * steps, rows * steps), rows * steps)
     total = base[part, :] + recv[part, :].astype(jnp.float32)
@@ -453,16 +461,17 @@
 
     @pl.when(step == 0)
     def _():
-        for i in range(moved):
-            pltpu.make_async_copy(residual.at[0], before.at[i], sems.at[i, 0]).wait()
-            pltpu.make_async_copy(backs[0].at[0], branch.at[i], sems.at[i, 1]).wait()
-
+        for copy in copies:
+            copy.wait()
+
+    branch = base_moved[...] + recv_moved[...].astype(jnp.float32)
     for i in range(moved):
         r = pairs[i]
 
         @pl.when(lax.div(r, rows) == step)
         def _():
-            out[lax.rem(r, rows)] = (branch[i] + before[i].astype(jnp.float32)).astype(out.dtype)
+            value = branch[i * steps : (i + 1) * steps] + before[i].astype(jnp.float32)
+            out[lax.rem(r, rows)] = value.astype(out.dtype)
 
 
 def exchange_pack(
@@ -491,7 +500,7 @@
             ],
             compiler_params=params(),
             name="pack",
-        )(fork, partner, *in_hbm(queries, new_keys, new_values, prompt_keys, prompt_values))
+        )(*in_hbm(fork, partner, queries, new_keys, new_values, prompt_keys, prompt_values))
         received = [
             lax.ppermute(packed[k - 1], "replica", [(i, (i + k) % replicas) for i in range(replicas)])
             for k in range(1, replicas)
@@ -560,14 +569,10 @@
         fork, partner, row_slot, queries, new_keys, new_values, fork_table, prompt_keys, prompt_values, span, moved
     )
     w_sib = lax.ppermute(out_proj, "tensor", sibling)
-    local = (
-        queries.reshape(n, width),
-        new_keys.reshape(n, HEAD_DIM),
-        new_values.reshape(n, HEAD_DIM),
-        cache_keys.reshape(local_rows * suffix, HEAD_DIM),
-        cache_values.reshape(local_rows * suffix, HEAD_DIM),
-    )
-    sizes = dict(local_rows=local_rows, steps=steps, slots=slots, suffix=suffix)
+    nk2 = new_keys.reshape(n, HEAD_DIM)
+    nv2 = new_values.reshape(n, HEAD_DIM)
+    ck2 = cache_keys.reshape(local_rows * suffix, HEAD_DIM)
+    cv2 = cache_values.reshape(local_rows * suffix, HEAD_DIM)
     lookup = (row_slot, prompt_lengths, cache_lengths, finished)
 
     dma = lambda *shape: pltpu.SemaphoreType.DMA(shape)
@@ -575,75 +580,86 @@
     nb = BLOCK * steps
     assert nb == HEAD_DIM
     cols = jnp.stack([place, place ^ 2]).astype(jnp.int32)
-    heads, w_here, w_there = pl.pallas_call(
-        functools.partial(attend_kernel, stacked=stacked, replicas=replicas, moved=moved, span=span, **sizes),
+    q2, scores, cvv, w_there, *staged = pl.pallas_call(
+        functools.partial(stage_kernel, moved=moved, slots=slots, suffix=suffix, span=span),
         out_shape=[
-            pltpu.VMEM(((local_rows + moved) * steps, width), dtype),
+            pltpu.VMEM((n, width), dtype),
+            pltpu.VMEM((blocks, groups, nb, HEAD_DIM), jnp.float32),
+            pltpu.VMEM((local_rows * suffix, HEAD_DIM), dtype),
             pltpu.VMEM((2 * width, model), dtype),
-            pltpu.VMEM((2 * width, model), dtype),
+            pltpu.VMEM((blocks, 3, nb, HEAD_DIM), jnp.int32),
+            pltpu.VMEM((blocks, nb, HEAD_DIM), jnp.float32),
+            pltpu.VMEM((moved * suffix, HEAD_DIM), dtype),
+            pltpu.VMEM((moved * suffix, HEAD_DIM), dtype),
+            pltpu.VMEM((3, moved * span, HEAD_DIM), jnp.int32),
+            pltpu.VMEM((moved * span, HEAD_DIM), jnp.float32),
         ],
-        in_specs=[SMEM] * 7 + [ANY] * (9 + len(received)),
-        out_specs=[VMEM] * 3,
+        in_specs=[SMEM] * 7 + [ANY] * 5,
+        out_specs=[VMEM] * 10,
+        scratch_shapes=[
+            pltpu.VMEM((local_rows, steps, width), dtype),
+            pltpu.VMEM((blocks, BLOCK * suffix, HEAD_DIM), dtype),
+            dma(2 + blocks, 3 + 2 * moved),
+        ],
+        compiler_params=params(),
+        name="stage",
+    )(*in_hbm(cols, fork, pairs, *lookup, queries, ck2, cv2, out_proj, w_sib))
+    (heads,) = pl.pallas_call(
+        functools.partial(
+            attend_kernel, stacked=stacked, replicas=replicas, slots=slots, moved=moved, steps=steps, suffix=suffix,
+            span=span,
+        ),
+        out_shape=[pltpu.VMEM(((local_rows + moved) * steps, width), dtype)],
+        in_specs=[SMEM] * 2 + [VMEM] * 11 + [ANY] * (2 + len(received)),
+        out_specs=[VMEM],
         scratch_shapes=[
             pltpu.VMEM((slots * prefix, HEAD_DIM), dtype),
             pltpu.VMEM((slots * prefix, HEAD_DIM), dtype),
-            pltpu.VMEM((blocks, nb, width), dtype),
-            pltpu.VMEM((blocks, nb, HEAD_DIM), dtype),
-            pltpu.VMEM((blocks, nb, HEAD_DIM), dtype),
-            pltpu.VMEM((blocks, BLOCK * suffix, HEAD_DIM), dtype),
-            pltpu.VMEM((blocks, BLOCK * suffix, HEAD_DIM), dtype),
             pltpu.VMEM((moved * span, HEAD_DIM), dtype),
-            pltpu.VMEM((moved * suffix, HEAD_DIM), dtype),
-            pltpu.VMEM((moved * suffix, HEAD_DIM), dtype),
-            pltpu.VMEM((blocks, 3, nb, HEAD_DIM), jnp.int32),
-            pltpu.VMEM((blocks, nb, HEAD_DIM), jnp.float32),
-            pltpu.VMEM((3, moved * span, HEAD_DIM), jnp.int32),
-            pltpu.VMEM((moved * span, HEAD_DIM), jnp.float32),
-            pltpu.VMEM((blocks, groups, nb, HEAD_DIM), jnp.float32),
             pltpu.VMEM((blocks, groups * nb, slots * prefix + HEAD_DIM), jnp.bfloat16),
             pltpu.VMEM((blocks, groups, nb, 2 * HEAD_DIM), jnp.bfloat16),
             pltpu.VMEM((blocks, groups * nb, HEAD_DIM), jnp.float32),
-            dma(blocks, 2, 3),
             dma(slots, 2),
             dma(moved),
-            dma(moved, 2),
-            dma(4),
         ],
         compiler_params=params(),
         name="attend",
-    )(cols, fork, pairs, *lookup, *in_hbm(*local, prompt_keys, prompt_values, out_proj), w_sib, *received)
+    )(*in_hbm(fork, pairs), q2, nk2, nv2, scores, cvv, *staged, *in_hbm(prompt_keys, prompt_values), *received)
 
     sib = lax.ppermute(heads, "tensor", sibling)
     m = moved * steps
 
-    def call(kernel, kind, name, *operands, specs):
+    def call(kernel, name, shapes, specs, operands, extra=()):
         return pl.pallas_call(
             kernel,
-            out_shape=[pltpu.VMEM((n, model), kind), pltpu.VMEM((m, model), kind)],
+            out_shape=[pltpu.VMEM(shape, kind) for shape, kind in shapes],
             in_specs=specs,
-            out_specs=[VMEM, VMEM],
+            out_specs=[VMEM] * len(shapes),
+            scratch_shapes=list(extra),
             compiler_params=params(),
             name=name,
         )(*operands)
 
-    crossed, crossed_moved = call(
-        project_kernel, dtype, "project", heads, sib, w_there, specs=[VMEM] * 3
-    )
-    got_moved = lax.ppermute(crossed_moved, "tensor", across)
+    (crossed,) = call(project_kernel, "project", [((n, model), dtype)], [VMEM] * 3, (heads, sib, w_there))
     got = lax.ppermute(crossed, "tensor", across)
-    base, base_moved = call(
-        base_kernel, jnp.float32, "base", heads, sib, w_here, residual, crossed, specs=[VMEM] * 4 + [ANY]
-    )
-
-    back_shape = pltpu.VMEM((replicas if stacked else 4, steps, model), jnp.float32)
-    back = pl.pallas_call(
-        functools.partial(moved_sum_kernel, moved=moved, steps=steps, replicas=replicas, split=not stacked),
-        out_shape=[back_shape] * (1 if stacked else 2),
-        in_specs=[SMEM, VMEM, VMEM],
-        out_specs=[VMEM] * (1 if stacked else 2),
-        compiler_params=params(),
-        name="moved_sum",
-    )(pairs, base_moved, got_moved)
+    base, w_here = call(
+        base_kernel,
+        "base",
+        [((n, model), jnp.float32), ((2 * width, model), dtype)],
+        [SMEM, VMEM, VMEM, ANY, ANY, ANY, ANY],
+        (*in_hbm(cols), heads, sib, *in_hbm(out_proj, w_sib, residual), crossed),
+        [pltpu.VMEM(residual.shape, dtype), dma(3)],
+    )
+
+    options = dict(moved=moved, steps=steps, split=not stacked)
+    shape = ((replicas if stacked else 4, steps, 2 * width), dtype)
+    back = call(
+        functools.partial(moved_send_kernel, **options),
+        "moved_send",
+        [shape] * (1 if stacked else 2),
+        [SMEM, VMEM, VMEM, ANY],
+        (*in_hbm(pairs), heads, sib, crossed),
+    )
     if stacked:
         backs = [lax.all_to_all(back[0], "replica", split_axis=0, concat_axis=0, tiled=True)]
     else:
@@ -653,21 +669,26 @@
         two = flip(jnp.concatenate([kept[2:], one[2:]]), 2)
         four = flip(jnp.concatenate([kept[1:2], one[1:2], two[1:2], two[3:4]]), 4)
         backs = [one, two, four]
+    crossed_moved, base_moved = call(
+        functools.partial(moved_project_kernel, **options),
+        "moved_project",
+        [((m, model), dtype), ((m, model), jnp.float32)],
+        [SMEM] + [VMEM] * (2 + len(backs)),
+        (*in_hbm(pairs), w_here, w_there, *backs),
+        [pltpu.VMEM((m, 2 * width), jnp.float32)],
+    )
+    got_moved = lax.ppermute(crossed_moved, "tensor", across)
 
     return pl.pallas_call(
-        functools.partial(finish_kernel, moved=moved, replicas=replicas, split=not stacked),
+        functools.partial(finish_kernel, moved=moved),
         grid=(blocks,),
-        in_specs=[SMEM, VMEM, VMEM, ANY] + [ANY] * len(backs),
+        in_specs=[SMEM, VMEM, VMEM, VMEM, VMEM, ANY],
         out_specs=pl.BlockSpec((BLOCK, steps, model), lambda i: (i, 0, 0)),
         out_shape=jax.ShapeDtypeStruct(residual.shape, residual.dtype),
-        scratch_shapes=[
-            pltpu.VMEM((moved, steps, model), jnp.float32),
-            pltpu.VMEM((moved, steps, model), dtype),
-            dma(moved, 2),
-        ],
+        scratch_shapes=[pltpu.VMEM((moved, steps, model), dtype), dma(moved)],
         compiler_params=params(),
         name="finish",
-    )(pairs, base, got, *in_hbm(residual), *backs)
+    )(*in_hbm(pairs), base, got, base_moved, got_moved, *in_hbm(residual))
 
 
 def solution(mesh):

time: 89.2 us -> 72 us (0.81)
  waiting for transfers between devices: 43.4 us -> 24.8 us
  Pallas kernels: 21.1 us -> 27.1 us
  local copies, waits for them, and re-layouts: 3.57 us -> 0.05 us
  starting transfers between devices: 20.7 us -> 18.6 us
    ppermute x1, waiting for transfers between devices: 27.7 us -> 13.9 us  [body(): got_moved = lax.ppermute(crossed_moved, 'tensor', across)]
    pallas_call x4 -> x6, Pallas kernels: 7.84 us -> 17.6 us  [the longest x4 9.31 us: call(): pl.pallas_call(kernel, out_shape=[pltpu.VMEM(shape, kind) for shape, kind...]
    ppermute x3, starting transfers between devices: 5.33 us -> 0.21 us  [body(): lax.ppermute(x, 'replica', [(i, i ^ bit) for i in range(replicas)])]
    pallas_call x1, Pallas kernels: 10.3 us -> 6.45 us  [body(): pl.pallas_call(functools.partial(attend_kernel, stacked=stacked, replicas...]
    ppermute x7, waiting for transfers between devices: 4.45 us -> 0.85 us  [exchange_pack(): lax.ppermute(packed[k - 1], 'replica', [(i, (i + k) % replicas) for i in...]
    ppermute x7, starting transfers between devices: 12.7 us -> 15.8 us  [exchange_pack(): lax.ppermute(packed[k - 1], 'replica', [(i, (i + k) % replicas) for i in...]
    reshape x1 -> x0, local copies, waits for them, and re-layouts: 2.19 us -> none  [body(): queries.reshape(n, width)]
    unnamed x16 -> x6, local copies, waits for them, and re-layouts: 1.36 us -> 0.01 us
  transfers between devices with their start and end apart: 14 -> 14, of which waited for: 9 -> 5; matrix products, arithmetic and copies ran while one was open for 3% -> 1% of each run, Pallas kernels for 6% -> 22%
where the time goes in v3:
time: 72 us; the launch traced here: 71.4 us
  Pallas kernels  27.1 us (38%)
  waiting for transfers between devices  24.8 us (34%)
  starting transfers between devices  18.6 us (26%)
    ppermute x7, starting transfers between devices, exchange_pack(): lax.ppermute(packed[k - 1], 'replica', [(i, (i + k) % replicas) for i in...  15.8 us
    ppermute x1, waiting for transfers between devices, body(): got_moved = lax.ppermute(crossed_moved, 'tensor', across)  13.9 us
    pallas_call x4, Pallas kernels, call(): pl.pallas_call(kernel, out_shape=[pltpu.VMEM(shape, kind) for shape, kind...  9.31 us
    ppermute x3, waiting for transfers between devices, body(): lax.ppermute(x, 'replica', [(i, i ^ bit) for i in range(replicas)])  7.93 us
    pallas_call x1, Pallas kernels, body(): pl.pallas_call(functools.partial(attend_kernel, stacked=stacked, replicas...  6.45 us
    pallas_call x1, Pallas kernels, body(): pl.pallas_call(functools.partial(stage_kernel, moved=moved, slots=slots,...  5.03 us
    pallas_call x1, Pallas kernels, body(): pl.pallas_call(functools.partial(finish_kernel, moved=moved), grid=(block...  3.23 us
    pallas_call x1, Pallas kernels, exchange_pack(): pl.pallas_call(functools.partial(pack_kernel, replicas=replicas, slots=fo...  3.1 us
  transfers between devices with their start and end apart: 14, of which 5 were waited for; matrix products, arithmetic and copies ran while one was open for 1% of the time, Pallas kernels for 22%

profile of v3, /device:TPU:0, one launch (start us, length us, event | category | flops | bytes accessed | tf_op | source)
XLA Modules:
  0.0 71.4 jit_solution(6218454253319450546)
XLA Ops:
  0.0 0.5 collective-permute-start
  0.5 3.1 %pack.1 = (bf16[288,128]{1,0:T(8,128)(2,1)S(1)}, bf16[288,128]{1,0:T(8,128)(2,1)S(1)}, bf16[288,128]{1,0:T(8,128)(2,1)S(1)}, bf16[288,128]{1,0:T(8,128)(2,1)S(1)...) custom-call(s32[4,8]{1,0:T(4,128)} %bitcast.11, ...), custom_call_target="tpu_custom_call" | custom-call | tf_op jit(solution)/shard_map/pack/pallas_call | solution.py:488
  3.6 2.6 %collective-permute-start.1 = (bf16[288,128]{1,0:T(8,128)(2,1)S(1)}, bf16[288,128]{1,0:T(8,128)(2,1)S(1)}, u32[]{:S(2)}, u32[]{:S(2)}) collective-permute-start(bf16[288,128]{1,0:T(8,128)(2,1)S(1)} %get-tuple-element.39), channel_id=1, source_target_pairs={{0,4},{4,8},{8,12},{12,16},{16,20},{20,24},{24,28},{28,0},{1,5},{5... | collective-permute-start | bytes 221192 | tf_op jit(solution)/shard_map/ppermute | solution.py:505
  6.1 1.6 %collective-permute-start.2 = (bf16[288,128]{1,0:T(8,128)(2,1)S(1)}, bf16[288,128]{1,0:T(8,128)(2,1)S(1)}, u32[]{:S(2)}, u32[]{:S(2)}) collective-permute-start(bf16[288,128]{1,0:T(8,128)(2,1)S(1)} %get-tuple-element.40), channel_id=1, source_target_pairs={{0,8},{4,12},{8,16},{12,20},{16,24},{20,28},{24,0},{28,4},{1,9},{5... | collective-permute-start | bytes 221192 | tf_op jit(solution)/shard_map/ppermute | solution.py:505
  7.7 2.5 %collective-permute-start.3 = (bf16[288,128]{1,0:T(8,128)(2,1)S(1)}, bf16[288,128]{1,0:T(8,128)(2,1)S(1)}, u32[]{:S(2)}, u32[]{:S(2)}) collective-permute-start(bf16[288,128]{1,0:T(8,128)(2,1)S(1)} %get-tuple-element.41), channel_id=1, source_target_pairs={{0,12},{4,16},{8,20},{12,24},{16,28},{20,0},{24,4},{28,8},{1,13},{... | collective-permute-start | bytes 221192 | tf_op jit(solution)/shard_map/ppermute | solution.py:505
  10.3 1.2 %collective-permute-start.4 = (bf16[288,128]{1,0:T(8,128)(2,1)S(1)}, bf16[288,128]{1,0:T(8,128)(2,1)S(1)}, u32[]{:S(2)}, u32[]{:S(2)}) collective-permute-start(bf16[288,128]{1,0:T(8,128)(2,1)S(1)} %get-tuple-element.42), channel_id=1, source_target_pairs={{0,16},{4,20},{8,24},{12,28},{16,0},{20,4},{24,8},{28,12},{1,17},{... | collective-permute-start | bytes 221192 | tf_op jit(solution)/shard_map/ppermute | solution.py:505
  11.5 0.8 %collective-permute-done.1.rest_0_ = bf16[288,128]{1,0:T(8,128)(2,1)S(1)} collective-permute-done((bf16[288,128]{1,0:T(8,128)(2,1)S(1)}, bf16[288,128]{1,0:T(8,128)(2,1)S(1)}, u32[]{:S(2)}, u32[]{:S(2)}) %collective-permute-start.1) | collective-permute-done | bytes 73760 | tf_op jit(solution)/shard_map/ppermute | solution.py:505
  12.3 1.8 %collective-permute-start.5 = (bf16[288,128]{1,0:T(8,128)(2,1)S(1)}, bf16[288,128]{1,0:T(8,128)(2,1)S(1)}, u32[]{:S(2)}, u32[]{:S(2)}) collective-permute-start(bf16[288,128]{1,0:T(8,128)(2,1)S(1)} %get-tuple-element.43), channel_id=1, source_target_pairs={{0,20},{4,24},{8,28},{12,0},{16,4},{20,8},{24,12},{28,16},{1,21},{... | collective-permute-start | bytes 221192 | tf_op jit(solution)/shard_map/ppermute | solution.py:505
  14.1 0.0 collective-permute-done.2.rest_1_
  14.1 1.3 %collective-permute-start.6 = (bf16[288,128]{1,0:T(8,128)(2,1)S(1)}, bf16[288,128]{1,0:T(8,128)(2,1)S(1)}, u32[]{:S(2)}, u32[]{:S(2)}) collective-permute-start(bf16[288,128]{1,0:T(8,128)(2,1)S(1)} %get-tuple-element.44), channel_id=1, source_target_pairs={{0,24},{4,28},{8,0},{12,4},{16,8},{20,12},{24,16},{28,20},{1,25},{... | collective-permute-start | bytes 221192 | tf_op jit(solution)/shard_map/ppermute | solution.py:505
  15.5 4.7 %collective-permute-start.7 = (bf16[288,128]{1,0:T(8,128)(2,1)S(1)}, bf16[288,128]{1,0:T(8,128)(2,1)S(1)}, u32[]{:S(2)}, u32[]{:S(2)}) collective-permute-start(bf16[288,128]{1,0:T(8,128)(2,1)S(1)} %get-tuple-element.45), channel_id=1, source_target_pairs={{0,28},{4,0},{8,4},{12,8},{16,12},{20,16},{24,20},{28,24},{1,29},{... | collective-permute-start | bytes 221192 | tf_op jit(solution)/shard_map/ppermute | solution.py:505
  20.2 0.6 pad_add_fusion.cols
  20.8 5.0 %stage.1 = (bf16[512,640]{1,0:T(8,128)(2,1)S(1)}, f32[4,5,128,128]{3,2,1,0:T(8,128)S(1)}, bf16[8192,128]{1,0:T(8,128)(2,1)S(1)}, bf16[1280,1280]{1,0:T(8,128)(2,...) custom-call(s32[2]{0:T(128)} %pad_add_fusion.cols, ...), custom_call_target="tpu_custom_call" | custom-call | tf_op jit(solution)/shard_map/stage/pallas_call | solution.py:583
  25.9 0.0 collective-permute-done.3.rest_2_
  25.9 0.0 collective-permute-done.4.rest_3_
  25.9 0.0 collective-permute-done.6.rest_5_
  25.9 6.5 %attend.1.h_own = bf16[528,640]{1,0:T(8,128)(2,1)S(1)} custom-call(s32[4,8]{1,0:T(4,128)} %bitcast.13, s32[10]{0:T(128)} %copy-done.2, bf16[512,640]{1,0:T(8,128)(2,1)S(1)} %get-tuple-element.30.q, bf16[512,128]{1,0:T(8,128)(2,1)S(1)} %bitcast.7, bf16[512,128]{1,0:T(8,128)(2,1)S(1)} %bitcast.8, f32[4,5,128,128]{3,2,1,0:T(8,128)S(1)} %get-tuple-element.31.cache_scores, ...), custom_call_target="tpu_custom_call" | custom-call | tf_op jit(solution)/shard_map/attend/pallas_call | solution.py:607
  32.4 0.1 collective-permute-start.8
  32.5 2.1 %collective-permute-done.8.h_sib = bf16[528,640]{1,0:T(8,128)(2,1)S(1)} collective-permute-done((bf16[528,640]{1,0:T(8,128)(2,1)S(1)}, bf16[528,640]{1,0:T(8,128)(2,1)S(1)}, u32[]{:S(2)}, u32[]{:S(2)}) %collective-permute-start.8) | collective-permute-done | bytes 675872 | tf_op jit(solution)/shard_map/ppermute | solution.py:629
  34.6 1.9 %project.1.after = bf16[512,1280]{1,0:T(8,128)(2,1)S(1)} custom-call(bf16[528,640]{1,0:T(8,128)(2,1)S(1)} %attend.1.h_own, bf16[528,640]{1,0:T(8,128)(2,1)S(1)} %collective-permute-done.8.h_sib, bf16[1280,1280]{1,0:T(8,128)(2,1)S(1)} %get-tuple-element.46.weights.w_there), custom_call_target="tpu_custom_call" | custom-call | tf_op jit(solution)/shard_map/project/pallas_call | solution.py:633
  36.4 1.6 %collective-permute-start.9 = (bf16[512,1280]{1,0:T(8,128)(2,1)S(1)}, bf16[512,1280]{1,0:T(8,128)(2,1)S(1)}, u32[]{:S(2)}, u32[]{:S(2)}) collective-permute-start(bf16[512,1280]{1,0:T(8,128)(2,1)S(1)} %project.1.after), channel_id=1, source_target_pairs={{0,2},{1,3},{2,0},{3,1},{4,6},{5,7},{6,4},{7,5},{8,10},{9,11},{10,... | collective-permute-start | bytes 3932168 | tf_op jit(solution)/shard_map/ppermute | solution.py:644
  38.0 0.8 %moved_send.1 = (bf16[4,4,1280]{2,1,0:T(4,128)(2,1)S(1)}, bf16[4,4,1280]{2,1,0:T(4,128)(2,1)S(1)}) custom-call(s32[10]{0:T(128)} %copy-done.2, bf16[528,640]{1,0:T(8,128)(2,1)S(1)} %attend.1.h_own, bf16[528,640]{1,0:T(8,128)(2,1)S(1)} %collective-permute-done.8.h_sib, bf16[512,1280]{1,0:T(8,128)(2,1)S(1)} %project.1.after), custom_call_target="tpu_custom_call" | custom-call | tf_op jit(solution)/shard_map/moved_send/pallas_call | solution.py:633
  38.8 0.1 collective-permute-start.10
  38.9 4.0 %collective-permute-done.10.rest_0_ = bf16[4,4,1280]{2,1,0:T(4,128)(2,1)S(1)} collective-permute-done((bf16[4,4,1280]{2,1,0:T(4,128)(2,1)S(1)}, bf16[4,4,1280]{2,1,0:T(4,128)(2,1)S(1)}, u32[]{:S(2)}, u32[]{:S(2)}) %collective-permute-start.10) | collective-permute-done | bytes 40992 | tf_op jit(solution)/shard_map/ppermute | solution.py:666
  42.9 0.1 collective-permute-start.11
  43.0 4.0 %collective-permute-done.11.rest_1_ = bf16[4,4,1280]{2,1,0:T(4,128)(2,1)S(1)} collective-permute-done((bf16[4,4,1280]{2,1,0:T(4,128)(2,1)S(1)}, bf16[4,4,1280]{2,1,0:T(4,128)(2,1)S(1)}, u32[]{:S(2)}, u32[]{:S(2)}) %collective-permute-start.11) | collective-permute-done | bytes 40992 | tf_op jit(solution)/shard_map/ppermute | solution.py:666
  47.0 0.1 collective-permute-start.12
  47.1 4.9 %base.1 = (f32[512,1280]{1,0:T(8,128)S(1)}, bf16[1280,1280]{1,0:T(8,128)(2,1)S(1)}) custom-call(s32[2]{0:T(128)} %pad_add_fusion.cols, bf16[528,640]{1,0:T(8,128)(2,1)S(1)} %attend.1.h_own, bf16[528,640]{1,0:T(8,128)(2,1)S(1)} %collective-permute-done.8.h_sib, bf16[640,5120]{1,0:T(8,128)(2,1)} %w_own.1, ...), custom_call_target="tpu_custom_call" | custom-call | tf_op jit(solution)/shard_map/base/pallas_call | solution.py:633
  52.0 1.8 %moved_project.1 = (bf16[16,1280]{1,0:T(8,128)(2,1)S(1)}, f32[16,1280]{1,0:T(8,128)S(1)}) custom-call(s32[10]{0:T(128)} %copy-done.2, bf16[1280,1280]{1,0:T(8,128)(2,1)S(1)} %get-tuple-element.48.w_here, bf16[1280,1280]{1,0:T(8,128)(2,1)S(1)} %get-tuple-element.46.weights.w_there, bf16[4,4,1280]{2,1,0:T(4,128)(2,1)S(1)} %collective-permute-done.10.rest_0_, ...), custom_call_target="tpu_custom_call" | custom-call | tf_op jit(solution)/shard_map/moved_project/pallas_call | solution.py:633
  53.8 0.5 collective-permute-start.13
  54.3 13.9 %collective-permute-done.13.recv_moved = bf16[16,1280]{1,0:T(8,128)(2,1)S(1)} collective-permute-done((bf16[16,1280]{1,0:T(8,128)(2,1)S(1)}, bf16[16,1280]{1,0:T(8,128)(2,1)S(1)}, u32[]{:S(2)}, u32[]{:S(2)}) %collective-permute-start.13) | collective-permute-done | bytes 40992 | tf_op jit(solution)/shard_map/ppermute | solution.py:680
  68.2 3.2 %finish.1 = bf16[128,4,1280]{2,1,0:T(4,128)(2,1)} custom-call(s32[10]{0:T(128)} %copy-done.2, f32[512,1280]{1,0:T(8,128)S(1)} %get-tuple-element.47.base, bf16[512,1280]{1,0:T(8,128)(2,1)S(1)} %collective-permute-done.9.recv, f32[16,1280]{1,0:T(8,128)S(1)} %get-tuple-element.51.base_moved, bf16[16,1280]{1,0:T(8,128)(2,1)S(1)} %collective-permute-done.13.recv_moved, ...), custom_call_target="tpu_custom_call" | custom-call | tf_op jit(solution)/shard_map/finish/pallas_call | solution.py:682
  (18 shorter events, 0.1 us)
Async XLA Ops:
  0.0 15.5 %collective-permute-start = (bf16[640,5120]{1,0:T(8,128)(2,1)}, bf16[640,5120]{1,0:T(8,128)(2,1)}, u32[]{:S(2)}, u32[]{:S(2)}) collective-permute-start(bf16[640,5120]{1,0:T(8,128)(2,1)} %w_own.1), channel_id=1, source_target_pairs={{0,1},{1,0},{2,3},{3,2},{4,5},{5,4},{6,7},{7,6},{8,9},{9,8},{10,11... | collective-permute-start | bytes 19660808 | tf_op jit(solution)/shard_map/ppermute | solution.py:571
  3.6 6.7 %copy-start.2 = (s32[10]{0:T(128)}, s32[10]{0:T(128)S(1)}, u32[]{:S(2)}) copy-start(s32[10]{0:T(128)S(1)} %get-tuple-element.29.pairs) | copy-start | bytes 124
  3.6 8.8 %collective-permute-start.1 = (bf16[288,128]{1,0:T(8,128)(2,1)S(1)}, bf16[288,128]{1,0:T(8,128)(2,1)S(1)}, u32[]{:S(2)}, u32[]{:S(2)}) collective-permute-start(bf16[288,128]{1,0:T(8,128)(2,1)S(1)} %get-tuple-element.39), channel_id=1, source_target_pairs={{0,4},{4,8},{8,12},{12,16},{16,20},{20,24},{24,28},{28,0},{1,5},{5... | collective-permute-start | bytes 221192 | tf_op jit(solution)/shard_map/ppermute | solution.py:505
  6.1 8.0 %collective-permute-start.2 = (bf16[288,128]{1,0:T(8,128)(2,1)S(1)}, bf16[288,128]{1,0:T(8,128)(2,1)S(1)}, u32[]{:S(2)}, u32[]{:S(2)}) collective-permute-start(bf16[288,128]{1,0:T(8,128)(2,1)S(1)} %get-tuple-element.40), channel_id=1, source_target_pairs={{0,8},{4,12},{8,16},{12,20},{16,24},{20,28},{24,0},{28,4},{1,9},{5... | collective-permute-start | bytes 221192 | tf_op jit(solution)/shard_map/ppermute | solution.py:505
  7.7 18.1 %collective-permute-start.3 = (bf16[288,128]{1,0:T(8,128)(2,1)S(1)}, bf16[288,128]{1,0:T(8,128)(2,1)S(1)}, u32[]{:S(2)}, u32[]{:S(2)}) collective-permute-start(bf16[288,128]{1,0:T(8,128)(2,1)S(1)} %get-tuple-element.41), channel_id=1, source_target_pairs={{0,12},{4,16},{8,20},{12,24},{16,28},{20,0},{24,4},{28,8},{1,13},{... | collective-permute-start | bytes 221192 | tf_op jit(solution)/shard_map/ppermute | solution.py:505
  10.3 15.6 %collective-permute-start.4 = (bf16[288,128]{1,0:T(8,128)(2,1)S(1)}, bf16[288,128]{1,0:T(8,128)(2,1)S(1)}, u32[]{:S(2)}, u32[]{:S(2)}) collective-permute-start(bf16[288,128]{1,0:T(8,128)(2,1)S(1)} %get-tuple-element.42), channel_id=1, source_target_pairs={{0,16},{4,20},{8,24},{12,28},{16,0},{20,4},{24,8},{28,12},{1,17},{... | collective-permute-start | bytes 221192 | tf_op jit(solution)/shard_map/ppermute | solution.py:505
  12.3 13.5 %collective-permute-start.5 = (bf16[288,128]{1,0:T(8,128)(2,1)S(1)}, bf16[288,128]{1,0:T(8,128)(2,1)S(1)}, u32[]{:S(2)}, u32[]{:S(2)}) collective-permute-start(bf16[288,128]{1,0:T(8,128)(2,1)S(1)} %get-tuple-element.43), channel_id=1, source_target_pairs={{0,20},{4,24},{8,28},{12,0},{16,4},{20,8},{24,12},{28,16},{1,21},{... | collective-permute-start | bytes 221192 | tf_op jit(solution)/shard_map/ppermute | solution.py:505
  14.1 11.7 %collective-permute-start.6 = (bf16[288,128]{1,0:T(8,128)(2,1)S(1)}, bf16[288,128]{1,0:T(8,128)(2,1)S(1)}, u32[]{:S(2)}, u32[]{:S(2)}) collective-permute-start(bf16[288,128]{1,0:T(8,128)(2,1)S(1)} %get-tuple-element.44), channel_id=1, source_target_pairs={{0,24},{4,28},{8,0},{12,4},{16,8},{20,12},{24,16},{28,20},{1,25},{... | collective-permute-start | bytes 221192 | tf_op jit(solution)/shard_map/ppermute | solution.py:505
  15.5 10.4 %collective-permute-start.7 = (bf16[288,128]{1,0:T(8,128)(2,1)S(1)}, bf16[288,128]{1,0:T(8,128)(2,1)S(1)}, u32[]{:S(2)}, u32[]{:S(2)}) collective-permute-start(bf16[288,128]{1,0:T(8,128)(2,1)S(1)} %get-tuple-element.45), channel_id=1, source_target_pairs={{0,28},{4,0},{8,4},{12,8},{16,12},{20,16},{24,20},{28,24},{1,29},{... | collective-permute-start | bytes 221192 | tf_op jit(solution)/shard_map/ppermute | solution.py:505
  20.8 5.1 %copy-start = (bf16[128,4,128]{2,1,0:T(4,128)(2,1)S(1)}, bf16[128,4,128]{2,1,0:T(4,128)(2,1)}, u32[]{:S(2)}) copy-start(bf16[128,4,128]{2,1,0:T(4,128)(2,1)} %new_keys.1) | copy-start | bytes 393220
  20.8 5.1 %copy-start.1 = (bf16[128,4,128]{2,1,0:T(4,128)(2,1)S(1)}, bf16[128,4,128]{2,1,0:T(4,128)(2,1)}, u32[]{:S(2)}) copy-start(bf16[128,4,128]{2,1,0:T(4,128)(2,1)} %new_values.1) | copy-start | bytes 393220
  32.4 2.2 %collective-permute-start.8 = (bf16[528,640]{1,0:T(8,128)(2,1)S(1)}, bf16[528,640]{1,0:T(8,128)(2,1)S(1)}, u32[]{:S(2)}, u32[]{:S(2)}) collective-permute-start(bf16[528,640]{1,0:T(8,128)(2,1)S(1)} %attend.1.h_own), channel_id=1, source_target_pairs={{0,1},{1,0},{2,3},{3,2},{4,5},{5,4},{6,7},{7,6},{8,9},{9,8},{10,11... | collective-permute-start | bytes 2027528 | tf_op jit(solution)/shard_map/ppermute | solution.py:629
  36.4 31.8 %collective-permute-start.9 = (bf16[512,1280]{1,0:T(8,128)(2,1)S(1)}, bf16[512,1280]{1,0:T(8,128)(2,1)S(1)}, u32[]{:S(2)}, u32[]{:S(2)}) collective-permute-start(bf16[512,1280]{1,0:T(8,128)(2,1)S(1)} %project.1.after), channel_id=1, source_target_pairs={{0,2},{1,3},{2,0},{3,1},{4,6},{5,7},{6,4},{7,5},{8,10},{9,11},{10,... | collective-permute-start | bytes 3932168 | tf_op jit(solution)/shard_map/ppermute | solution.py:644
  38.8 4.1 %collective-permute-start.10 = (bf16[4,4,1280]{2,1,0:T(4,128)(2,1)S(1)}, bf16[4,4,1280]{2,1,0:T(4,128)(2,1)S(1)}, u32[]{:S(2)}, u32[]{:S(2)}) collective-permute-start(bf16[4,4,1280]{2,1,0:T(4,128)(2,1)S(1)} %get-tuple-element.49), channel_id=1, source_target_pairs={{0,4},{4,0},{8,12},{12,8},{16,20},{20,16},{24,28},{28,24},{1,5},{5... | collective-permute-start | bytes 122888 | tf_op jit(solution)/shard_map/ppermute | solution.py:666
  42.9 4.1 %collective-permute-start.11 = (bf16[4,4,1280]{2,1,0:T(4,128)(2,1)S(1)}, bf16[4,4,1280]{2,1,0:T(4,128)(2,1)S(1)}, u32[]{:S(2)}, u32[]{:S(2)}) collective-permute-start(bf16[4,4,1280]{2,1,0:T(4,128)(2,1)S(1)} %pad_maximum_fusion), channel_id=1, source_target_pairs={{0,8},{4,12},{8,0},{12,4},{16,24},{20,28},{24,16},{28,20},{1,9},{5... | collective-permute-start | bytes 122888 | tf_op jit(solution)/shard_map/ppermute | solution.py:666
  47.0 5.0 %collective-permute-start.12 = (bf16[4,4,1280]{2,1,0:T(4,128)(2,1)S(1)}, bf16[4,4,1280]{2,1,0:T(4,128)(2,1)S(1)}, u32[]{:S(2)}, u32[]{:S(2)}) collective-permute-start(bf16[4,4,1280]{2,1,0:T(4,128)(2,1)S(1)} %pad_maximum_fusion.1), channel_id=1, source_target_pairs={{0,16},{4,20},{8,24},{12,28},{16,0},{20,4},{24,8},{28,12},{1,17},{... | collective-permute-start | bytes 122888 | tf_op jit(solution)/shard_map/ppermute | solution.py:666
  53.8 14.4 %collective-permute-start.13 = (bf16[16,1280]{1,0:T(8,128)(2,1)S(1)}, bf16[16,1280]{1,0:T(8,128)(2,1)S(1)}, u32[]{:S(2)}, u32[]{:S(2)}) collective-permute-start(bf16[16,1280]{1,0:T(8,128)(2,1)S(1)} %get-tuple-element.52), channel_id=1, source_target_pairs={{0,2},{1,3},{2,0},{3,1},{4,6},{5,7},{6,4},{7,5},{8,10},{9,11},{10,... | collective-permute-start | bytes 122888 | tf_op jit(solution)/shard_map/ppermute | solution.py:680

commit v4 on v3

v4 whole, which is shorter than its diff:
```python
import functools
import math

import jax
import jax.numpy as jnp
from jax import lax
from jax.experimental import pallas as pl
from jax.experimental.pallas import tpu as pltpu
from jax.sharding import PartitionSpec as P

HEAD_DIM = 128
LOWEST = -1e30
EXP2_SCALE = math.log2(math.e) / math.sqrt(HEAD_DIM)
VMEM_BYTES = 24 * 1024 * 1024
SMALL = pl.CostEstimate(flops=1, bytes_accessed=1, transcendentals=0)
BLOCK = 32
FIRST = 2
NT = (((1,), (1,)), ((), ()))
NN = (((1,), (0,)), ((), ()))

ANY = pl.BlockSpec(memory_space=pl.ANY)
SMEM = pl.BlockSpec(memory_space=pltpu.SMEM)
VMEM = pl.BlockSpec(memory_space=pltpu.VMEM)


def params(side_effects=False):
    return pltpu.CompilerParams(vmem_limit_bytes=VMEM_BYTES, has_side_effects=side_effects)


def matmul(a, b, dims):
    return lax.dot_general(a, b, dims, preferred_element_type=jnp.float32)


def columns(model, flip):
    place = jnp.bitwise_xor(lax.axis_index("tensor"), flip)
    return pl.ds(pl.multiple_of(place * model, HEAD_DIM), model)


def in_hbm(*arrays):
    return [pltpu.with_memory_space_constraint(x, pltpu.HBM) for x in arrays]


def iota(shape, dim):
    return lax.broadcasted_iota(jnp.int32, shape, dim)


def load(pairs, sem):
    copies = [pltpu.make_async_copy(a, b, sem.at[i]) for i, (a, b) in enumerate(pairs)]
    for copy in copies:
        copy.start()

    def wait():
        for copy in copies:
            copy.wait()

    return wait


def list_pairs(row_of, pairs, me, replicas, moved):
    count = jnp.int32(0)
    for j in range(replicas):
        pairs[count] = row_of[j]
        pairs[moved + 1 + count] = j
        pairs[2 * (moved + 1) + j] = jnp.maximum(row_of[j], 0)
        count = jnp.minimum(count + jnp.where((row_of[j] >= 0) & (j != me), 1, 0), moved)


def find_pairs(partner, row_of, replicas, local_rows):
    for j in range(replicas):
        row_of[j] = -1

    shift = local_rows.bit_length() - 1

    def note(r, carry):
        peer = partner[r] >> shift if local_rows == 1 << shift else lax.div(partner[r], local_rows)
        row_of[peer] = r
        return carry

    lax.fori_loop(0, local_rows, note, 0, unroll=8)


def send_prompts(shifts, fork, keys, values, outs, sems, replicas):
    me = lax.axis_index("replica")
    held, prefix = keys.shape[0], keys.shape[1]
    waits = []
    for i, k in enumerate(shifts):
        peer = lax.rem(me + k, replicas)
        offset = jnp.int32(0)
        for s in range(fork.shape[0]):
            prompt = fork[s, peer]
            offset = jnp.where(lax.div(prompt, held) == me, lax.rem(prompt, held), offset)
        copies = [
            (source.at[offset], outs[i].at[pl.ds(n * prefix, prefix)]) for n, source in enumerate((keys, values))
        ]
        waits.append(load(copies, sems.at[i]))
    return waits


def send_rows(shifts, row_of, hbm, vmem, outs, sems, replicas, prefix):
    me = lax.axis_index("replica")
    width = hbm[0].shape[2]
    waits = []
    for i, k in enumerate(shifts):
        r = row_of(lax.rem(me + k, replicas))
        waits.append(load([(a.at[r], b.at[i]) for a, b in zip(hbm, vmem)], sems.at[i]))
    for i in range(len(shifts)):
        waits[i]()
        q, nk, nv = [v[i].astype(jnp.float32) for v in vmem]
        parts = [q[:, low : low + HEAD_DIM] for low in range(0, width, HEAD_DIM)] + [nk, nv]
        pad = outs[i].shape[0] - 2 * prefix - sum(p.shape[0] for p in parts)
        parts += [jnp.zeros((pad, HEAD_DIM), jnp.float32)]
        outs[i][2 * prefix :, :] = jnp.concatenate(parts, axis=0).astype(outs[i].dtype)


def pairs_kernel(partner, pairs, row_of, *, replicas, local_rows, moved):
    find_pairs(partner, row_of, replicas, local_rows)
    list_pairs(row_of, pairs, lax.axis_index("replica"), replicas, moved)


def pack_kernel(
    fork, partner, queries, new_keys, new_values, keys, values, *rest, replicas, moved, shifts
):
    outs, (pairs, qv, nkv, nvv, row_of, sems, row_sems) = rest[: len(shifts)], rest[len(shifts) :]
    waits = send_prompts(shifts, fork, keys, values, outs, sems, replicas)
    find_pairs(partner, row_of, replicas, queries.shape[0])
    list_pairs(row_of, pairs, lax.axis_index("replica"), replicas, moved)
    send_rows(
        shifts, lambda j: jnp.maximum(row_of[j], 0), (queries, new_keys, new_values), (qv, nkv, nvv), outs, row_sems,
        replicas, keys.shape[1],
    )
    for wait in waits:
        wait()


def softmax_weights(prompt, new, cache, prompt_mask, new_mask, cache_mask):
    prompt = jnp.where(prompt_mask, prompt, LOWEST)
    new = jnp.where(new_mask, new, LOWEST)
    cache = jnp.where(cache_mask, cache, LOWEST)
    top = jnp.max(jnp.maximum(jnp.maximum(prompt, new), cache), axis=1, keepdims=True)
    prompt = jnp.exp2((prompt - top) * EXP2_SCALE)
    new = jnp.exp2((new - top) * EXP2_SCALE)
    cache = jnp.exp2((cache - top) * EXP2_SCALE)
    inverse = 1.0 / jnp.sum(prompt + new + cache, axis=1, keepdims=True)
    return prompt * inverse, new * inverse, cache * inverse


def pick_slot(scores, slot, slots, prefix):
    picked = scores[:, :prefix]
    for s in range(1, slots):
        picked = jnp.where(slot == s, scores[:, s * prefix : (s + 1) * prefix], picked)
    return picked


def spread_slot(weights, slot, slots):
    return jnp.concatenate(
        [jnp.where(slot == s, weights, 0.0).astype(jnp.bfloat16) for s in range(slots)], axis=1
    )


def fill_meta(lookup, local_row, span, meta):
    row_slot, fork, prompt_lengths, cache_lengths, finished, me, local_rows = lookup
    g = me * local_rows + local_row
    slot = row_slot[g]
    values = (slot, prompt_lengths[fork[slot, me]], cache_lengths[g], 1 - finished[g])
    size = span.stop - span.start
    for i, value in enumerate(values):
        meta[i, span, :] = jnp.full((size, HEAD_DIM), value, jnp.int32)


def attend_scores(q, ck, cache_scores, *, steps, suffix):
    n = q.shape[0]
    groups = q.shape[1] // HEAD_DIM
    keys_sub = 4 * suffix
    half = 2 * suffix
    for sub in range(n // 16):
        r0 = sub * 16
        qs = jnp.concatenate(
            [q[r0 : r0 + 16, h * HEAD_DIM : (h + 1) * HEAD_DIM] for h in range(groups)], axis=0
        )
        s = matmul(qs, ck[sub * keys_sub : (sub + 1) * keys_sub, :], NT)
        for h in range(groups):
            cache_scores[h, r0 : r0 + 8, :] = s[16 * h : 16 * h + 8, :half]
            cache_scores[h, r0 + 8 : r0 + 16, :] = s[16 * h + 8 : 16 * h + 16, half:]


def attend_block(
    q, nk, nv, cv, pk, pv, heads, meta, cache_scores, weights, cache_weights, mixed, wait,
    *, steps, slots, suffix
):
    n = q.shape[0]
    groups = q.shape[1] // HEAD_DIM
    prefix = pk.shape[0] // slots
    keys_sub = 4 * suffix
    half = 2 * suffix
    shape = (n, HEAD_DIM)
    lane, row = iota(shape, 1), iota(shape, 0)
    cache_own = (lane // suffix) == ((row % 8) // steps)
    cache_lane = jnp.where(cache_own, lane % suffix, suffix)
    new_mask = ((lane // steps) == (row // steps)) & ((lane % steps) <= (row % steps))
    first_half = (row % 16) < 8
    slot = meta[0]
    prompt_mask = lane < meta[1]
    cache_mask = cache_lane < meta[2]
    alive_rows = meta[3].astype(jnp.float32)
    q_all = jnp.concatenate([q[:, h * HEAD_DIM : (h + 1) * HEAD_DIM] for h in range(groups)], axis=0)
    prompt_all = matmul(q_all, pk[...], NT)
    new_all = matmul(q_all, nk[...], NT)
    for h in range(groups):
        part = slice(h * n, (h + 1) * n)
        prompt = pick_slot(prompt_all[part], slot, slots, prefix)
        wp, wn, wc = softmax_weights(
            prompt, new_all[part], cache_scores[h], prompt_mask, new_mask, cache_mask
        )
        cache_weights[h, :, :half] = jnp.where(first_half, wc, 0.0).astype(jnp.bfloat16)
        cache_weights[h, :, half:] = jnp.where(first_half, 0.0, wc).astype(jnp.bfloat16)
        weights[part, : slots * prefix] = spread_slot(wp, slot, slots)
        weights[part, slots * prefix :] = wn.astype(jnp.bfloat16)
    mixed[...] = matmul(weights[:, : slots * prefix], pv[...], NN) + matmul(
        weights[:, slots * prefix :], nv[...], NN
    )
    if wait is not None:
        wait()
    for sub in range(n // 16):
        r0 = sub * 16
        w = jnp.concatenate([cache_weights[h, r0 : r0 + 16, :] for h in range(groups)], axis=0)
        o = matmul(w, cv[sub * keys_sub : (sub + 1) * keys_sub, :], NN)
        for h in range(groups):
            total = mixed[h * n + r0 : h * n + r0 + 16, :] + o[16 * h : 16 * h + 16, :]
            heads[r0 : r0 + 16, h * HEAD_DIM : (h + 1) * HEAD_DIM] = (
                total * alive_rows[r0 : r0 + 16, :]
            ).astype(heads.dtype)


def moved_block(x, pk, pv, keys, values, slot, plen, clen, alive, *, steps, slots, groups, span, suffix):
    prefix = pk.shape[0] // slots
    shape = (4 * span, HEAD_DIM)
    lane, row = iota(shape, 1), iota(shape, 0)
    prompt_mask = lane < plen
    cache_mask = ((lane // suffix) == ((row // span) % 2)) & ((lane % suffix) < clen)
    past = (lane % span) - groups * steps
    new_mask = ((lane // span) == (row // span)) & (past >= 0) & (past <= row % steps)
    prompt = pick_slot(matmul(x, pk[...], NT), slot, slots, prefix)
    new = matmul(x, x, NT)
    cache = matmul(x, keys[...], NT)
    half = 2 * suffix
    top_half = row < 2 * span
    cache = jnp.where(top_half, cache[:, :half], cache[:, half:])
    wp, wn, wc = softmax_weights(prompt, new, cache, prompt_mask, new_mask, cache_mask)
    wc = jnp.concatenate(
        [jnp.where(top_half, wc, 0.0), jnp.where(top_half, 0.0, wc)], axis=1
    ).astype(jnp.bfloat16)
    wn = pltpu.roll(wn, steps, 1).astype(jnp.bfloat16)
    mixed = (
        matmul(spread_slot(wp, slot, slots), pv[...], NN)
        + matmul(wn, x, NN)
        + matmul(wc, values[...], NN)
    )
    mixed = (mixed * alive).astype(jnp.bfloat16)
    row, col = iota((4 * steps, 4 * span), 0), iota((4 * steps, 4 * span), 1)
    cols = []
    for h in range(groups):
        take = ((row // steps) == (col // span)) & ((col % span) == h * steps + row % steps)
        cols.append(matmul(take.astype(jnp.bfloat16), mixed, NN).astype(jnp.bfloat16))
    return jnp.concatenate(cols, axis=1)


def start_rows(first_row, hbm, vmem, sems, steps, suffix):
    rows = vmem[0].shape[0]
    part = pl.ds(first_row * steps, rows * steps)
    keys = pl.ds(first_row * suffix, rows * suffix)
    q, nk, nv, ck, cv = hbm
    return [
        load([(q.at[pl.ds(first_row, rows)], vmem[0]), (ck.at[keys], vmem[3])], sems.at[0]),
        load([(nk.at[part], vmem[1]), (nv.at[part], vmem[2])], sems.at[1]),
        load([(cv.at[keys], vmem[4])], sems.at[2]),
    ]


def attend_rows(lookup, first_row, waits, vmem, pk, pv, heads, work, *, steps, slots, suffix):
    q3, nk, nv, ck, cv = vmem
    q, meta, cache_scores, weights, cache_weights, mixed = work
    count, _, n, _ = meta.shape
    rows = n // steps
    per = 16 // steps
    for b in range(count * rows):
        low = b % rows * steps
        fill_meta(lookup, first_row + b, slice(low, low + steps), meta.at[b // rows])
    waits[0]()
    for b in range(0, count * rows, per):
        part = [q3[b + i].astype(jnp.float32) for i in range(per)]
        q[b * steps : (b + per) * steps, :] = jnp.concatenate(part, axis=0).astype(q.dtype)
    keys = rows * suffix
    for i in range(count):
        attend_scores(
            q.at[pl.ds(i * n, n)], ck.at[pl.ds(i * keys, keys)], cache_scores.at[i], steps=steps, suffix=suffix
        )
    waits[1]()
    for i in range(count):
        part = pl.ds(i * n, n)
        attend_block(
            q.at[part], nk.at[part], nv.at[part], cv.at[pl.ds(i * keys, keys)], pk, pv, heads.at[part],
            meta.at[i], cache_scores.at[i], weights.at[i], cache_weights.at[i], mixed.at[i],
            waits[2] if i == 0 else None, steps=steps, slots=slots, suffix=suffix,
        )


def first_kernel(
    fork, pairs, row_slot, prompt_lengths, cache_lengths, finished, q, nk, nv, ck, cv, own_keys, own_values, w_own, w_sib,
    *rest, stacked, replicas, slots, moved, steps, suffix, span
):
    recvs, rest = rest[:-24], rest[-24:]
    heads, pk, pv, w_there, x, keys, values, moved_meta = rest[:8]
    vmem, work, (row_sems, slot_sems, w_sems, sems, cache_sems) = rest[8:13], rest[13:19], rest[19:]
    me = lax.axis_index("replica")
    held, prefix = own_keys.shape[0], own_keys.shape[1]
    waits = start_rows(0, (q, nk, nv, ck, cv), vmem, row_sems, steps, suffix)
    for s in range(slots):
        prompt = fork[s, me]
        owner = lax.div(prompt, held)
        offset = lax.rem(prompt, held)
        targets = (pk.at[pl.ds(s * prefix, prefix)], pv.at[pl.ds(s * prefix, prefix)])
        if stacked:
            for i in range(2):
                pltpu.make_async_copy(
                    recvs[0].at[owner, pl.ds(i * prefix, prefix)], targets[i], slot_sems.at[s, i]
                ).start()
            continue
        k = lax.rem(me - owner + replicas, replicas)

        @pl.when(k == 0)
        def _():
            pltpu.make_async_copy(own_keys.at[offset], targets[0], slot_sems.at[s, 0]).start()
            pltpu.make_async_copy(own_values.at[offset], targets[1], slot_sems.at[s, 1]).start()

        for kk in range(1, replicas):

            @pl.when(k == kk)
            def _():
                for i in range(2):
                    pltpu.make_async_copy(
                        recvs[kk - 1].at[pl.ds(i * prefix, prefix)], targets[i], slot_sems.at[s, i]
                    ).start()

    groups = q.shape[2] // HEAD_DIM
    for i in range(moved):
        peer = pairs[moved + 1 + i]
        if stacked:
            pltpu.make_async_copy(
                recvs[0].at[peer, pl.ds(2 * prefix, span)], x.at[pl.ds(i * span, span)], sems.at[i]
            ).start()
        else:
            k = lax.rem(me - peer + replicas, replicas)
            for kk in range(1, replicas):

                @pl.when(k == kk)
                def _():
                    pltpu.make_async_copy(
                        recvs[kk - 1].at[pl.ds(2 * prefix, span)], x.at[pl.ds(i * span, span)], sems.at[i]
                    ).start()

    copies = []
    for i in range(moved):
        source = pl.ds(pl.multiple_of(pairs[i] * suffix, suffix), suffix)
        target = pl.ds(i * suffix, suffix)
        copies += [(ck.at[source], keys.at[target]), (cv.at[source], values.at[target])]
    caches_ready = load(copies, cache_sems)
    width, model = w_own.shape[0], w_there.shape[1]
    at = columns(model, 2)
    weights_ready = load(
        [(w_own.at[:, at], w_there.at[pl.ds(0, width)]), (w_sib.at[:, at], w_there.at[pl.ds(width, width)])], w_sems
    )

    def wait_second():
        waits[1]()
        for s in range(slots):
            for i, target in enumerate((pk, pv)):
                pltpu.make_async_copy(own_keys.at[0], target.at[pl.ds(s * prefix, prefix)], slot_sems.at[s, i]).wait()

    lookup = (row_slot, fork, prompt_lengths, cache_lengths, finished, me, q.shape[0])
    for i in range(moved):
        fill_meta(lookup, pairs[i], slice(i * span, (i + 1) * span), moved_meta)
    n = heads.shape[0] - moved * steps
    attend_rows(
        lookup, 0, (waits[0], wait_second, waits[2]), vmem, pk, pv, heads.at[pl.ds(0, n)], work,
        steps=steps, slots=slots, suffix=suffix,
    )
    for i in range(moved):
        source = recvs[0].at[0, pl.ds(0, span)] if stacked else recvs[0].at[pl.ds(0, span)]
        pltpu.make_async_copy(source, x.at[pl.ds(i * span, span)], sems.at[i]).wait()
    caches_ready()
    for g in range(moved // 4):
        part = slice(g * 4 * span, (g + 1) * 4 * span)
        kpart = slice(g * 4 * suffix, (g + 1) * 4 * suffix)
        heads[n + g * 4 * steps : n + (g + 1) * 4 * steps, :] = moved_block(
            x[part, :], pk, pv, keys.at[kpart], values.at[kpart],
            moved_meta[0, part, :], moved_meta[1, part, :], moved_meta[2, part, :],
            moved_meta[3, part, :].astype(jnp.float32),
            steps=steps, slots=slots, groups=groups, span=span, suffix=suffix,
        )
    weights_ready()


def second_kernel(
    fork, row_slot, prompt_lengths, cache_lengths, finished, pk, pv, q, nk, nv, ck, cv, after, *rest,
    first_row, slots, steps, suffix
):
    heads, vmem, work, row_sems = rest[0], rest[1:6], rest[6:12], rest[12]
    waits = start_rows(first_row, (q, nk, nv, ck, cv), vmem, row_sems, steps, suffix)
    lookup = (row_slot, fork, prompt_lengths, cache_lengths, finished, lax.axis_index("replica"), q.shape[0])
    attend_rows(
        lookup, first_row, waits, vmem, pk, pv, heads, work, steps=steps, slots=slots, suffix=suffix
    )


def project_kernel(h_own, h_sib, weights, out):
    rows = pl.ds(0, out.shape[0])
    both = jnp.concatenate([h_own[rows, :], h_sib[rows, :]], axis=1)
    out[...] = matmul(both, weights[...], NN).astype(out.dtype)


def base_kernel(
    h_first, s_first, h_second, s_second, h_moved, w_own, w_sib, residual, out, moved_out, weights, before, sems
):
    rows, model = out.shape
    width = w_own.shape[0]
    steps = residual.shape[1]
    at = columns(model, 0)
    ready = load(
        [
            (w_own.at[:, at], weights.at[pl.ds(0, width)]),
            (w_sib.at[:, at], weights.at[pl.ds(width, width)]),
            (residual, before),
        ],
        sems,
    )
    ready()
    moved_out[...] = matmul(h_moved[...], weights[...], NN)
    low = 0
    for h_own, h_sib, size in ((h_first, s_first, rows - h_second.shape[0]), (h_second, s_second, h_second.shape[0])):
        part = pl.ds(0, size)
        total = matmul(jnp.concatenate([h_own[part, :], h_sib[part, :]], axis=1), weights[...], NN)
        for b in range(0, size, steps):
            out[low : low + steps, :] = total[b : b + steps] + before[low // steps].astype(jnp.float32)
            low += steps


def moved_send_kernel(pairs, h_own, h_sib, after, *outs, moved, steps, split):
    me = lax.axis_index("replica")
    rows = pl.ds(h_own.shape[0] - moved * steps, moved * steps)
    both = jnp.concatenate([h_own[rows, :], h_sib[rows, :]], axis=1).astype(jnp.float32)
    for i in range(moved):
        peer = pairs[moved + 1 + i]
        value = both[i * steps : (i + 1) * steps].astype(outs[0].dtype)
        if split:
            k = jnp.bitwise_xor(me, peer)
            place = 2 * lax.rem(lax.div(k, 2), 2) + lax.div(k, 4)

            @pl.when(lax.rem(k, 2) == 0)
            def _():
                outs[0][place] = value

            @pl.when(lax.rem(k, 2) == 1)
            def _():
                outs[1][place] = value

        else:
            outs[0][peer] = value


def moved_project_kernel(pairs, w_there, *rest, moved, steps, split):
    backs, (cross, both_out, heads) = rest[:-3], rest[-3:]
    me = lax.axis_index("replica")
    for i in range(moved):
        peer = pairs[moved + 1 + i]
        part = slice(i * steps, (i + 1) * steps)
        if split:
            k = jnp.bitwise_xor(me, peer)
            places = {1: (0, 0), 2: (1, 0), 3: (1, 2), 4: (2, 0), 5: (2, 1), 6: (2, 2), 7: (2, 3)}
            for d, (which, index) in places.items():

                @pl.when(k == d)
                def _():
                    heads[part, :] = backs[which][index].astype(jnp.float32)

        else:
            heads[part, :] = backs[0][peer].astype(jnp.float32)
    both = heads[...].astype(cross.dtype)
    both_out[...] = both
    cross[...] = matmul(both, w_there[...], NN).astype(cross.dtype)


def add_rows(total, out, first, steps):
    for b in range(total.shape[0] // steps):
        out[first + b] = total[b * steps : (b + 1) * steps].astype(out.dtype)


def finish_first_kernel(base, recv, out):
    rows, steps = out.shape[:2]
    part = pl.ds(pl.multiple_of(pl.program_id(0) * rows * steps, rows * steps), rows * steps)
    add_rows(base[part, :] + recv[part, :].astype(jnp.float32), out, 0, steps)


def finish_second_kernel(
    pairs, base, recv, base_moved, recv_moved, residual, earlier, out, before, after, rows_out, sems, row_sems, *, moved
):
    later, steps = rows_out.shape[:2]
    half = out.shape[0] - later
    n = half * steps
    fetch = [load([(residual.at[pairs[i]], before.at[i])], sems.at[i]) for i in range(moved)]
    add_rows(base[n:, :] + recv[...].astype(jnp.float32), rows_out, 0, steps)
    branch = base_moved[...] + recv_moved[...].astype(jnp.float32)
    for i in range(moved):
        r = pairs[i]
        fetch[i]()
        value = branch[i * steps : (i + 1) * steps] + before[i].astype(jnp.float32)
        after[i] = value.astype(after.dtype)

        @pl.when(r >= half)
        def _():
            rows_out[jnp.maximum(r - half, 0)] = after[i]

        @pl.when(r < half)
        def _():
            pltpu.make_async_copy(after.at[i], out.at[r], sems.at[i, 0]).start()

    done = load([(rows_out, out.at[pl.ds(half, later)])], row_sems)
    for i in range(moved):
        r = pairs[i]

        @pl.when(r < half)
        def _():
            pltpu.make_async_copy(after.at[i], out.at[r], sems.at[i, 0]).wait()

    done()


def row_buffers(count, steps, width, dtype):
    return [pltpu.VMEM((count, steps, size), dtype) for size in (width, HEAD_DIM, HEAD_DIM)]


def exchange_pack(
    fork, partner, row_slot, queries, new_keys, new_values, fork_table, prompt_keys, prompt_values, span, moved
):
    replicas = lax.axis_size("replica")
    me = lax.axis_index("replica")
    local_rows, steps, width = queries.shape
    groups = width // HEAD_DIM
    held, prefix = prompt_keys.shape[:2]
    dtype = queries.dtype
    pairs_shape = jax.ShapeDtypeStruct((2 * (moved + 1) + replicas,), jnp.int32)
    if replicas <= 8:
        shifts = tuple(range(1, replicas))
        count = len(shifts)
        *packed, pairs = pl.pallas_call(
            functools.partial(pack_kernel, replicas=replicas, moved=moved, shifts=shifts),
            out_shape=[pltpu.VMEM((2 * prefix + span, HEAD_DIM), dtype)] * count + [pairs_shape],
            in_specs=[SMEM, SMEM] + [ANY] * 5,
            out_specs=[VMEM] * count + [SMEM],
            scratch_shapes=row_buffers(count, steps, width, dtype)
            + [
                pltpu.SMEM((replicas,), jnp.int32),
                pltpu.SemaphoreType.DMA((count, 2)),
                pltpu.SemaphoreType.DMA((count, 3)),
            ],
            compiler_params=params(),
            name="pack",
        )(*in_hbm(fork, partner, queries, new_keys, new_values, prompt_keys, prompt_values))
        return packed, pairs
    chosen = (fork_table // held) == me
    offsets = jnp.sum(jnp.where(chosen, fork_table % held, 0), axis=1)
    peer_of = partner // local_rows
    pairing = (peer_of[None, :] == jnp.arange(replicas, dtype=jnp.int32)[:, None]) & (
        peer_of[None, :] != me
    )
    row_of = jnp.sum(jnp.where(pairing, jnp.arange(local_rows, dtype=jnp.int32)[None, :], 0), axis=1)
    q = queries[row_of].reshape(replicas, steps, groups, HEAD_DIM).transpose(0, 2, 1, 3)
    q = q.reshape(replicas, groups * steps, HEAD_DIM)
    pad = jnp.zeros((replicas, span - (groups + 2) * steps, HEAD_DIM), dtype)
    block = jnp.concatenate(
        [prompt_keys[offsets], prompt_values[offsets], q, new_keys[row_of], new_values[row_of], pad], axis=1
    )
    pairs = pl.pallas_call(
        functools.partial(pairs_kernel, replicas=replicas, local_rows=local_rows, moved=moved),
        out_shape=pairs_shape,
        in_specs=[SMEM],
        out_specs=SMEM,
        scratch_shapes=[pltpu.SMEM((replicas,), jnp.int32)],
        name="pairs",
    )(partner)
    return [block], pairs


def body(
    residual,
    queries,
    new_keys,
    new_values,
    cache_keys,
    cache_values,
    cache_lengths,
    finished,
    partner,
    row_slot,
    fork_table,
    prompt_keys,
    prompt_values,
    prompt_lengths,
    out_proj,
):
    replicas = lax.axis_size("replica")
    tensors = lax.axis_size("tensor")
    local_rows, steps, width = queries.shape
    groups = width // HEAD_DIM
    suffix = cache_keys.shape[1]
    held, prefix = prompt_keys.shape[:2]
    slots = fork_table.shape[1]
    moved = replicas // 2
    stacked = replicas > 8
    model = residual.shape[2]
    n = local_rows * steps
    span = 32
    dtype = queries.dtype
    fork = fork_table.T
    sibling = [(i, i ^ 1) for i in range(tensors)]
    across = [(i, i ^ 2) for i in range(tensors)]

    packed, pairs = exchange_pack(
        fork, partner, row_slot, queries, new_keys, new_values, fork_table, prompt_keys, prompt_values, span, moved
    )
    w_sib = lax.ppermute(out_proj, "tensor", sibling)
    nk2 = new_keys.reshape(n, HEAD_DIM)
    nv2 = new_values.reshape(n, HEAD_DIM)
    ck2 = cache_keys.reshape(local_rows * suffix, HEAD_DIM)
    cv2 = cache_values.reshape(local_rows * suffix, HEAD_DIM)
    lookup = (row_slot, prompt_lengths, cache_lengths, finished)

    dma = lambda *shape: pltpu.SemaphoreType.DMA(shape)
    blocks = local_rows // BLOCK
    nb = BLOCK * steps
    assert nb == HEAD_DIM
    if stacked:
        received = [lax.all_to_all(packed[0], "replica", split_axis=0, concat_axis=0, tiled=True)]
    else:
        received = [
            lax.ppermute(block, "replica", [(i, (i + k) % replicas) for i in range(replicas)])
            for k, block in enumerate(packed, 1)
        ]

    m = moved * steps
    half = FIRST
    nh = half * nb
    prompts = pltpu.VMEM((slots * prefix, HEAD_DIM), dtype)

    def work(count):
        rows = count * BLOCK
        return [
            pltpu.VMEM((rows, steps, width), dtype),
            pltpu.VMEM((rows * steps, HEAD_DIM), dtype),
            pltpu.VMEM((rows * steps, HEAD_DIM), dtype),
            pltpu.VMEM((rows * suffix, HEAD_DIM), dtype),
            pltpu.VMEM((rows * suffix, HEAD_DIM), dtype),
            pltpu.VMEM((rows * steps, width), dtype),
            pltpu.VMEM((count, 4, nb, HEAD_DIM), jnp.int32),
            pltpu.VMEM((count, groups, nb, HEAD_DIM), jnp.float32),
            pltpu.VMEM((count, groups * nb, slots * prefix + HEAD_DIM), jnp.bfloat16),
            pltpu.VMEM((count, groups, nb, 2 * HEAD_DIM), jnp.bfloat16),
            pltpu.VMEM((count, groups * nb, HEAD_DIM), jnp.float32),
            dma(3, 2),
        ]

    sizes = dict(slots=slots, steps=steps, suffix=suffix)
    lookup = in_hbm(row_slot, prompt_lengths, cache_lengths, finished)
    rows_in = in_hbm(queries, nk2, nv2, ck2, cv2)
    h_first, pk, pv, w_there = pl.pallas_call(
        functools.partial(first_kernel, stacked=stacked, replicas=replicas, moved=moved, span=span, **sizes),
        out_shape=[pltpu.VMEM((nh + m, width), dtype), prompts, prompts, pltpu.VMEM((2 * width, model), dtype)],
        in_specs=[SMEM] * 6 + [ANY] * (9 + len(received)),
        out_specs=[VMEM] * 4,
        scratch_shapes=[
            pltpu.VMEM((moved * span, HEAD_DIM), dtype),
            pltpu.VMEM((moved * suffix, HEAD_DIM), dtype),
            pltpu.VMEM((moved * suffix, HEAD_DIM), dtype),
            pltpu.VMEM((4, moved * span, HEAD_DIM), jnp.int32),
        ]
        + work(half)
        + [dma(slots, 2), dma(2), dma(moved), dma(2 * moved)],
        compiler_params=params(),
        cost_estimate=SMALL,
        name="attend_first",
    )(*in_hbm(fork, pairs), *lookup, *rows_in, *in_hbm(prompt_keys, prompt_values, out_proj), w_sib, *received)

    def call(kernel, name, shapes, specs, operands, extra=()):
        return pl.pallas_call(
            kernel,
            out_shape=[pltpu.VMEM(shape, kind) for shape, kind in shapes],
            in_specs=specs,
            out_specs=[VMEM] * len(shapes),
            scratch_shapes=list(extra),
            compiler_params=params(),
            cost_estimate=SMALL,
            name=name,
        )(*operands)

    def cross(heads, rows):
        sib = lax.ppermute(heads, "tensor", sibling)
        (crossed,) = call(project_kernel, "project", [((rows, model), dtype)], [VMEM] * 3, (heads, sib, w_there))
        return sib, crossed, lax.ppermute(crossed, "tensor", across)

    s_first, c_first, got_first = cross(h_first, nh)
    options = dict(moved=moved, steps=steps, split=not stacked)
    shape = ((replicas if stacked else 4, steps, 2 * width), dtype)
    back = call(
        functools.partial(moved_send_kernel, **options),
        "moved_send",
        [shape] * (1 if stacked else 2),
        [SMEM, VMEM, VMEM, ANY],
        (*in_hbm(pairs), h_first, s_first, c_first),
    )
    (h_second,) = call(
        functools.partial(second_kernel, first_row=half * BLOCK, **sizes),
        "attend_second",
        [((n - nh, width), dtype)],
        [SMEM] * 5 + [VMEM] * 2 + [ANY] * 6,
        (*in_hbm(fork), *lookup, pk, pv, *rows_in, c_first),
        work(blocks - half),
    )
    s_second, c_second, got_second = cross(h_second, n - nh)
    if stacked:
        backs = [lax.all_to_all(back[0], "replica", split_axis=0, concat_axis=0, tiled=True)]
    else:
        flip = lambda x, bit: lax.ppermute(x, "replica", [(i, i ^ bit) for i in range(replicas)])
        kept = back[0]
        one = flip(back[1], 1)
        one, *_ = lax.optimization_barrier((one, c_second))
        two = flip(jnp.concatenate([kept[2:], one[2:]]), 2)
        two, *_ = lax.optimization_barrier((two, got_first))
        four = flip(jnp.concatenate([kept[1:2], one[1:2], two[1:2], two[3:4]]), 4)
        backs = [one, two, four]
    crossed_moved, home_heads = call(
        functools.partial(moved_project_kernel, **options),
        "moved_project",
        [((m, model), dtype), ((m, 2 * width), dtype)],
        [SMEM] + [VMEM] * (1 + len(backs)),
        (*in_hbm(pairs), w_there, *backs),
        [pltpu.VMEM((m, 2 * width), jnp.float32)],
    )
    got_moved = lax.ppermute(crossed_moved, "tensor", across)
    base, base_moved = call(
        base_kernel,
        "base",
        [((n, model), jnp.float32), ((m, model), jnp.float32)],
        [VMEM] * 5 + [ANY] * 3,
        (h_first, s_first, h_second, s_second, home_heads, *in_hbm(out_proj), w_sib, *in_hbm(residual)),
        [pltpu.VMEM((2 * width, model), dtype), pltpu.VMEM(residual.shape, dtype), dma(3)],
    )

    whole = jax.ShapeDtypeStruct(residual.shape, residual.dtype)
    out = pl.pallas_call(
        finish_first_kernel,
        grid=(half,),
        in_specs=[VMEM, VMEM],
        out_specs=pl.BlockSpec((BLOCK, steps, model), lambda i: (i, 0, 0)),
        out_shape=whole,
        compiler_params=params(),
        name="finish_first",
    )(base, got_first)
    return pl.pallas_call(
        functools.partial(finish_second_kernel, moved=moved),
        in_specs=[SMEM, VMEM, VMEM, VMEM, VMEM, ANY, ANY],
        out_specs=ANY,
        out_shape=whole,
        input_output_aliases={6: 0},
        scratch_shapes=[
            pltpu.VMEM((moved, steps, model), dtype),
            pltpu.VMEM((moved, steps, model), dtype),
            pltpu.VMEM(((blocks - half) * BLOCK, steps, model), dtype),
            dma(moved, 1),
            dma(1),
        ],
        compiler_params=params(),
        name="finish_second",
    )(*in_hbm(pairs), base, got_second, base_moved, got_moved, *in_hbm(residual), out)


def solution(mesh):
    rows = P("replica", None, "tensor")
    in_specs = (rows,) * 6 + (P(), P(), P("replica"), P(), P(), rows, rows, P(), P("tensor", None))
    return jax.shard_map(body, mesh=mesh, in_specs=in_specs, out_specs=rows, check_vma=False)
```

time: 72 us -> 66.5 us (0.924)
  waiting for transfers between devices: 24.8 us -> 17.7 us
  starting transfers between devices: 18.6 us -> 21.8 us
  Pallas kernels: 27.1 us -> 26.2 us
    ppermute x1, waiting for transfers between devices: 13.9 us -> 0.58 us  [body(): got_moved = lax.ppermute(crossed_moved, 'tensor', across)]
    ppermute x9 -> x11, waiting for transfers between devices: 2.97 us -> 10.3 us  [the longest x7 6.74 us: body(): lax.ppermute(block, 'replica', [(i, (i + k) % replicas) for i in range(re...]
    pallas_call x4, Pallas kernels: 17.8 us -> 12.4 us  [the longest x1 6.21 us: body(): pl.pallas_call(functools.partial(first_kernel, stacked=stacked, replicas=...]
    ppermute x3, starting transfers between devices: 0.21 us -> 4.85 us  [body(): lax.ppermute(x, 'replica', [(i, i ^ bit) for i in range(replicas)])]
    pallas_call x4 -> x6, Pallas kernels: 9.31 us -> 13.7 us  [call(): pl.pallas_call(kernel, out_shape=[pltpu.VMEM(shape, kind) for shape, kind...]
    ppermute x9 -> x11, starting transfers between devices: 17.4 us -> 15 us  [the longest x7 12.7 us: body(): lax.ppermute(block, 'replica', [(i, (i + k) % replicas) for i in range(re...]
    ppermute x3, waiting for transfers between devices: 7.93 us -> 6.83 us  [body(): lax.ppermute(x, 'replica', [(i, i ^ bit) for i in range(replicas)])]
    ppermute x1, starting transfers between devices: 0.51 us -> 1.51 us  [body(): got_moved = lax.ppermute(crossed_moved, 'tensor', across)]
  transfers between devices with their start and end apart: 14 -> 16, of which waited for: 5 -> 11; matrix products, arithmetic and copies ran while one was open for 1% -> 0% of each run, Pallas kernels for 22% -> 25%
where the time goes in v4:
time: 66.5 us; the launch traced here: 66.1 us
  Pallas kernels  26.2 us (39%)
  starting transfers between devices  21.8 us (33%)
  waiting for transfers between devices  17.7 us (27%)
    pallas_call x6, Pallas kernels, call(): pl.pallas_call(kernel, out_shape=[pltpu.VMEM(shape, kind) for shape, kind...  13.7 us
    ppermute x7, starting transfers between devices, body(): lax.ppermute(block, 'replica', [(i, (i + k) % replicas) for i in range(re...  12.7 us
    ppermute x3, waiting for transfers between devices, body(): lax.ppermute(x, 'replica', [(i, i ^ bit) for i in range(replicas)])  6.83 us
    ppermute x7, waiting for transfers between devices, body(): lax.ppermute(block, 'replica', [(i, (i + k) % replicas) for i in range(re...  6.74 us
    pallas_call x1, Pallas kernels, body(): pl.pallas_call(functools.partial(first_kernel, stacked=stacked, replicas=...  6.21 us
    ppermute x3, starting transfers between devices, body(): lax.ppermute(x, 'replica', [(i, i ^ bit) for i in range(replicas)])  4.85 us
    pallas_call x1, Pallas kernels, exchange_pack(): pl.pallas_call(functools.partial(pack_kernel, replicas=replicas, moved=mo...  2.97 us
    pallas_call x1, Pallas kernels, body(): pl.pallas_call(functools.partial(finish_second_kernel, moved=moved), in_s...  2.31 us
  transfers between devices with their start and end apart: 16, of which 11 were waited for; matrix products, arithmetic and copies ran while one was open for 0% of the time, Pallas kernels for 25%

profile of v4, /device:TPU:0, one launch (start us, length us, event | category | flops | bytes accessed | tf_op | source)
XLA Modules:
  0.0 66.1 jit_solution(16639631363801669314)
XLA Ops:
  0.5 3.0 %pack.1 = (bf16[288,128]{1,0:T(8,128)(2,1)S(1)}, bf16[288,128]{1,0:T(8,128)(2,1)S(1)}, bf16[288,128]{1,0:T(8,128)(2,1)S(1)}, bf16[288,128]{1,0:T(8,128)(2,1)S(1)...) custom-call(s32[4,8]{1,0:T(4,128)} %bitcast.13, ...), custom_call_target="tpu_custom_call" | custom-call | tf_op jit(solution)/shard_map/pack/pallas_call | solution.py:554
  3.4 2.6 %collective-permute-start.1 = (bf16[288,128]{1,0:T(8,128)(2,1)S(1)}, bf16[288,128]{1,0:T(8,128)(2,1)S(1)}, u32[]{:S(2)}, u32[]{:S(2)}) collective-permute-start(bf16[288,128]{1,0:T(8,128)(2,1)S(1)} %get-tuple-element.26), channel_id=1, source_target_pairs={{0,4},{4,8},{8,12},{12,16},{16,20},{20,24},{24,28},{28,0},{1,5},{5... | collective-permute-start | bytes 221192 | tf_op jit(solution)/shard_map/ppermute | solution.py:645
  6.0 1.6 %collective-permute-start.2 = (bf16[288,128]{1,0:T(8,128)(2,1)S(1)}, bf16[288,128]{1,0:T(8,128)(2,1)S(1)}, u32[]{:S(2)}, u32[]{:S(2)}) collective-permute-start(bf16[288,128]{1,0:T(8,128)(2,1)S(1)} %get-tuple-element.27), channel_id=1, source_target_pairs={{0,8},{4,12},{8,16},{12,20},{16,24},{20,28},{24,0},{28,4},{1,9},{5... | collective-permute-start | bytes 221192 | tf_op jit(solution)/shard_map/ppermute | solution.py:645
  7.6 2.5 %collective-permute-start.3 = (bf16[288,128]{1,0:T(8,128)(2,1)S(1)}, bf16[288,128]{1,0:T(8,128)(2,1)S(1)}, u32[]{:S(2)}, u32[]{:S(2)}) collective-permute-start(bf16[288,128]{1,0:T(8,128)(2,1)S(1)} %get-tuple-element.28), channel_id=1, source_target_pairs={{0,12},{4,16},{8,20},{12,24},{16,28},{20,0},{24,4},{28,8},{1,13},{... | collective-permute-start | bytes 221192 | tf_op jit(solution)/shard_map/ppermute | solution.py:645
  10.1 1.2 %collective-permute-start.4 = (bf16[288,128]{1,0:T(8,128)(2,1)S(1)}, bf16[288,128]{1,0:T(8,128)(2,1)S(1)}, u32[]{:S(2)}, u32[]{:S(2)}) collective-permute-start(bf16[288,128]{1,0:T(8,128)(2,1)S(1)} %get-tuple-element.29), channel_id=1, source_target_pairs={{0,16},{4,20},{8,24},{12,28},{16,0},{20,4},{24,8},{28,12},{1,17},{... | collective-permute-start | bytes 221192 | tf_op jit(solution)/shard_map/ppermute | solution.py:645
  11.4 0.8 %collective-permute-done.1.rest_0_ = bf16[288,128]{1,0:T(8,128)(2,1)S(1)} collective-permute-done((bf16[288,128]{1,0:T(8,128)(2,1)S(1)}, bf16[288,128]{1,0:T(8,128)(2,1)S(1)}, u32[]{:S(2)}, u32[]{:S(2)}) %collective-permute-start.1) | collective-permute-done | bytes 73760 | tf_op jit(solution)/shard_map/ppermute | solution.py:645
  12.2 1.8 %collective-permute-start.5 = (bf16[288,128]{1,0:T(8,128)(2,1)S(1)}, bf16[288,128]{1,0:T(8,128)(2,1)S(1)}, u32[]{:S(2)}, u32[]{:S(2)}) collective-permute-start(bf16[288,128]{1,0:T(8,128)(2,1)S(1)} %get-tuple-element.30), channel_id=1, source_target_pairs={{0,20},{4,24},{8,28},{12,0},{16,4},{20,8},{24,12},{28,16},{1,21},{... | collective-permute-start | bytes 221192 | tf_op jit(solution)/shard_map/ppermute | solution.py:645
  14.0 1.4 %collective-permute-start.6 = (bf16[288,128]{1,0:T(8,128)(2,1)S(1)}, bf16[288,128]{1,0:T(8,128)(2,1)S(1)}, u32[]{:S(2)}, u32[]{:S(2)}) collective-permute-start(bf16[288,128]{1,0:T(8,128)(2,1)S(1)} %get-tuple-element.31), channel_id=1, source_target_pairs={{0,24},{4,28},{8,0},{12,4},{16,8},{20,12},{24,16},{28,20},{1,25},{... | collective-permute-start | bytes 221192 | tf_op jit(solution)/shard_map/ppermute | solution.py:645
  15.4 3.1 %collective-permute-done.3.rest_2_ = bf16[288,128]{1,0:T(8,128)(2,1)S(1)} collective-permute-done((bf16[288,128]{1,0:T(8,128)(2,1)S(1)}, bf16[288,128]{1,0:T(8,128)(2,1)S(1)}, u32[]{:S(2)}, u32[]{:S(2)}) %collective-permute-start.3) | collective-permute-done | bytes 73760 | tf_op jit(solution)/shard_map/ppermute | solution.py:645
  18.5 1.6 %collective-permute-start.7 = (bf16[288,128]{1,0:T(8,128)(2,1)S(1)}, bf16[288,128]{1,0:T(8,128)(2,1)S(1)}, u32[]{:S(2)}, u32[]{:S(2)}) collective-permute-start(bf16[288,128]{1,0:T(8,128)(2,1)S(1)} %get-tuple-element.32), channel_id=1, source_target_pairs={{0,28},{4,0},{8,4},{12,8},{16,12},{20,16},{24,20},{28,24},{1,29},{... | collective-permute-start | bytes 221192 | tf_op jit(solution)/shard_map/ppermute | solution.py:645
  20.1 1.2 %collective-permute-done.5.rest_4_ = bf16[288,128]{1,0:T(8,128)(2,1)S(1)} collective-permute-done((bf16[288,128]{1,0:T(8,128)(2,1)S(1)}, bf16[288,128]{1,0:T(8,128)(2,1)S(1)}, u32[]{:S(2)}, u32[]{:S(2)}) %collective-permute-start.5) | collective-permute-done | bytes 73760 | tf_op jit(solution)/shard_map/ppermute | solution.py:645
  21.8 1.0 %collective-permute-done.7.rest_6_ = bf16[288,128]{1,0:T(8,128)(2,1)S(1)} collective-permute-done((bf16[288,128]{1,0:T(8,128)(2,1)S(1)}, bf16[288,128]{1,0:T(8,128)(2,1)S(1)}, u32[]{:S(2)}, u32[]{:S(2)}) %collective-permute-start.7) | collective-permute-done | bytes 73760 | tf_op jit(solution)/shard_map/ppermute | solution.py:645
  22.9 6.2 %attend_first.1 = (bf16[272,640]{1,0:T(8,128)(2,1)S(1)}, bf16[512,128]{1,0:T(8,128)(2,1)S(1)}, bf16[512,128]{1,0:T(8,128)(2,1)S(1)}, bf16[1280,1280]{1,0:T(8,128)(2,1)S(1)}) custom-call(s32[4,8]{1,0:T(4,128)} %bitcast.14, s32[18]{0:T(128)} %copy-done, s32[1024]{0:T(1024)} %row_slot.3, s32[32]{0:T(128)} %prompt_lengths.3, s32[1024]{0:T(1024)} %cache_lengths.3, ...), custom_call_target="tpu_custom_call" | custom-call | flops 1 | bytes 1 | tf_op jit(solution)/shard_map/attend_first/pallas_call | solution.py:674
  29.2 1.6 %collective-permute-done.8.h_sib.s_first = bf16[272,640]{1,0:T(8,128)(2,1)S(1)} collective-permute-done((bf16[272,640]{1,0:T(8,128)(2,1)S(1)}, bf16[272,640]{1,0:T(8,128)(2,1)S(1)}, u32[]{:S(2)}, u32[]{:S(2)}) %collective-permute-start.8) | collective-permute-done | bytes 348192 | tf_op jit(solution)/shard_map/ppermute | solution.py:705
  30.8 1.0 %project.2.after = bf16[256,1280]{1,0:T(8,128)(2,1)S(1)} custom-call(bf16[272,640]{1,0:T(8,128)(2,1)S(1)} %get-tuple-element.33.h_own.h_first, bf16[272,640]{1,0:T(8,128)(2,1)S(1)} %collective-permute-done.8.h_sib.s_first, bf16[1280,1280]{1,0:T(8,128)(2,1)S(1)} %get-tuple-element.36.weights.w_there), custom_call_target="tpu_custom_call" | custom-call | flops 1 | bytes 1 | tf_op jit(solution)/shard_map/project/pallas_call | solution.py:693
  31.8 1.6 %collective-permute-start.12 = (bf16[256,1280]{1,0:T(8,128)(2,1)S(1)}, bf16[256,1280]{1,0:T(8,128)(2,1)S(1)}, u32[]{:S(2)}, u32[]{:S(2)}) collective-permute-start(bf16[256,1280]{1,0:T(8,128)(2,1)S(1)} %project.2.after), channel_id=1, source_target_pairs={{0,2},{1,3},{2,0},{3,1},{4,6},{5,7},{6,4},{7,5},{8,10},{9,11},{10,... | collective-permute-start | bytes 1966088 | tf_op jit(solution)/shard_map/ppermute | solution.py:707
  33.4 5.2 %attend_second.1.h_own.h_second = bf16[256,640]{1,0:T(8,128)(2,1)S(1)} custom-call(s32[4,8]{1,0:T(4,128)} %bitcast.15, s32[1024]{0:T(1024)} %row_slot.3, s32[32]{0:T(128)} %prompt_lengths.3, s32[1024]{0:T(1024)} %cache_lengths.3, s32[1024]{0:T(1024)} %finished.3, bf16[512,128]{1,0:T(8,128)(2,1)S(1)} %get-tuple-element.34.pk, ...), custom_call_target="tpu_custom_call" | custom-call | flops 1 | bytes 1 | tf_op jit(solution)/shard_map/attend_second/pallas_call | solution.py:693
  38.6 0.8 %moved_send.1 = (bf16[4,4,1280]{2,1,0:T(4,128)(2,1)S(1)}, bf16[4,4,1280]{2,1,0:T(4,128)(2,1)S(1)}) custom-call(s32[18]{0:T(128)} %copy-done, bf16[272,640]{1,0:T(8,128)(2,1)S(1)} %get-tuple-element.33.h_own.h_first, bf16[272,640]{1,0:T(8,128)(2,1)S(1)} %collective-permute-done.8.h_sib.s_first, bf16[256,1280]{1,0:T(8,128)(2,1)S(1)} %project.2.after), custom_call_target="tpu_custom_call" | custom-call | flops 1 | bytes 1 | tf_op jit(solution)/shard_map/moved_send/pallas_call | solution.py:693
  39.4 1.3 %collective-permute-start.10 = (bf16[4,4,1280]{2,1,0:T(4,128)(2,1)S(1)}, bf16[4,4,1280]{2,1,0:T(4,128)(2,1)S(1)}, u32[]{:S(2)}, u32[]{:S(2)}) collective-permute-start(bf16[4,4,1280]{2,1,0:T(4,128)(2,1)S(1)} %get-tuple-element.37), channel_id=1, source_target_pairs={{0,4},{4,0},{8,12},{12,8},{16,20},{20,16},{24,28},{28,24},{1,5},{5... | collective-permute-start | bytes 122888 | tf_op jit(solution)/shard_map/ppermute | solution.py:731
  40.7 1.0 %project.3 = bf16[256,1280]{1,0:T(8,128)(2,1)S(1)} custom-call(bf16[256,640]{1,0:T(8,128)(2,1)S(1)} %attend_second.1.h_own.h_second, bf16[256,640]{1,0:T(8,128)(2,1)S(1)} %collective-permute-done.9.h_sib.s_second, bf16[1280,1280]{1,0:T(8,128)(2,1)S(1)} %get-tuple-element.36.weights.w_there), custom_call_target="tpu_custom_call" | custom-call | flops 1 | bytes 1 | tf_op jit(solution)/shard_map/project/pallas_call | solution.py:693
  41.7 1.7 %collective-permute-done.10.rest_0_ = bf16[4,4,1280]{2,1,0:T(4,128)(2,1)S(1)} collective-permute-done((bf16[4,4,1280]{2,1,0:T(4,128)(2,1)S(1)}, bf16[4,4,1280]{2,1,0:T(4,128)(2,1)S(1)}, u32[]{:S(2)}, u32[]{:S(2)}) %collective-permute-start.10) | collective-permute-done | bytes 40992 | tf_op jit(solution)/shard_map/ppermute | solution.py:731
  43.5 1.9 %collective-permute-start.11 = (bf16[4,4,1280]{2,1,0:T(4,128)(2,1)S(1)}, bf16[4,4,1280]{2,1,0:T(4,128)(2,1)S(1)}, u32[]{:S(2)}, u32[]{:S(2)}) collective-permute-start(bf16[4,4,1280]{2,1,0:T(4,128)(2,1)S(1)} %pad_maximum_fusion), channel_id=1, source_target_pairs={{0,8},{4,12},{8,0},{12,4},{16,24},{20,28},{24,16},{28,20},{1,9},{5... | collective-permute-start | bytes 122888 | tf_op jit(solution)/shard_map/ppermute | solution.py:731
  45.4 0.6 collective-permute-start.14
  46.0 1.6 %collective-permute-done.11.rest_1_ = bf16[4,4,1280]{2,1,0:T(4,128)(2,1)S(1)} collective-permute-done((bf16[4,4,1280]{2,1,0:T(4,128)(2,1)S(1)}, bf16[4,4,1280]{2,1,0:T(4,128)(2,1)S(1)}, u32[]{:S(2)}, u32[]{:S(2)}) %collective-permute-start.11) | collective-permute-done | bytes 40992 | tf_op jit(solution)/shard_map/ppermute | solution.py:731
  47.6 1.9 %collective-permute-done.12.recv = bf16[256,1280]{1,0:T(8,128)(2,1)S(1)} collective-permute-done((bf16[256,1280]{1,0:T(8,128)(2,1)S(1)}, bf16[256,1280]{1,0:T(8,128)(2,1)S(1)}, u32[]{:S(2)}, u32[]{:S(2)}) %collective-permute-start.12) | collective-permute-done | bytes 655392 | tf_op jit(solution)/shard_map/ppermute | solution.py:707
  49.5 1.7 %collective-permute-start.13 = (bf16[4,4,1280]{2,1,0:T(4,128)(2,1)S(1)}, bf16[4,4,1280]{2,1,0:T(4,128)(2,1)S(1)}, u32[]{:S(2)}, u32[]{:S(2)}) collective-permute-start(bf16[4,4,1280]{2,1,0:T(4,128)(2,1)S(1)} %pad_maximum_fusion.1), channel_id=1, source_target_pairs={{0,16},{4,20},{8,24},{12,28},{16,0},{20,4},{24,8},{28,12},{1,17},{... | collective-permute-start | bytes 122888 | tf_op jit(solution)/shard_map/ppermute | solution.py:731
  51.2 3.6 %collective-permute-done.13.rest_2_ = bf16[4,4,1280]{2,1,0:T(4,128)(2,1)S(1)} collective-permute-done((bf16[4,4,1280]{2,1,0:T(4,128)(2,1)S(1)}, bf16[4,4,1280]{2,1,0:T(4,128)(2,1)S(1)}, u32[]{:S(2)}, u32[]{:S(2)}) %collective-permute-start.13) | collective-permute-done | bytes 40992 | tf_op jit(solution)/shard_map/ppermute | solution.py:731
  54.8 1.5 %moved_project.1 = (bf16[16,1280]{1,0:T(8,128)(2,1)S(1)}, bf16[16,1280]{1,0:T(8,128)(2,1)S(1)}) custom-call(s32[18]{0:T(128)} %copy-done, bf16[1280,1280]{1,0:T(8,128)(2,1)S(1)} %get-tuple-element.36.weights.w_there, bf16[4,4,1280]{2,1,0:T(4,128)(2,1)S(1)} %collective-permute-done.10.rest_0_, bf16[4,4,1280]{2,1,0:T(4,128)(2,1)S(1)} %collective-permute-done.11.rest_1_, ...), custom_call_target="tpu_custom_call" | custom-call | flops 1 | bytes 1 | tf_op jit(solution)/shard_map/moved_project/pallas_call | solution.py:693
  56.3 1.5 %collective-permute-start.15 = (bf16[16,1280]{1,0:T(8,128)(2,1)S(1)}, bf16[16,1280]{1,0:T(8,128)(2,1)S(1)}, u32[]{:S(2)}, u32[]{:S(2)}) collective-permute-start(bf16[16,1280]{1,0:T(8,128)(2,1)S(1)} %get-tuple-element.44), channel_id=1, source_target_pairs={{0,2},{1,3},{2,0},{3,1},{4,6},{5,7},{6,4},{7,5},{8,10},{9,11},{10,... | collective-permute-start | bytes 122888 | tf_op jit(solution)/shard_map/ppermute | solution.py:747
  57.8 4.2 %base.1 = (f32[512,1280]{1,0:T(8,128)S(1)}, f32[16,1280]{1,0:T(8,128)S(1)}) custom-call(bf16[272,640]{1,0:T(8,128)(2,1)S(1)} %get-tuple-element.33.h_own.h_first, bf16[272,640]{1,0:T(8,128)(2,1)S(1)} %collective-permute-done.8.h_sib.s_first, bf16[256,640]{1,0:T(8,128)(2,1)S(1)} %attend_second.1.h_own.h_second, ...), custom_call_target="tpu_custom_call" | custom-call | flops 1 | bytes 1 | tf_op jit(solution)/shard_map/base/pallas_call | solution.py:693
  62.1 0.9 %finish_first.1.earlier = bf16[128,4,1280]{2,1,0:T(4,128)(2,1)} custom-call(f32[512,1280]{1,0:T(8,128)S(1)} %get-tuple-element.42.base, bf16[256,1280]{1,0:T(8,128)(2,1)S(1)} %collective-permute-done.12.recv), custom_call_target="tpu_custom_call" | custom-call | tf_op jit(solution)/shard_map/finish_first/pallas_call | solution.py:758
  63.6 2.3 %finish_second.1 = bf16[128,4,1280]{2,1,0:T(4,128)(2,1)} custom-call(s32[18]{0:T(128)} %copy-done, f32[512,1280]{1,0:T(8,128)S(1)} %get-tuple-element.42.base, bf16[256,1280]{1,0:T(8,128)(2,1)S(1)} %collective-permute-done.14.recv, f32[16,1280]{1,0:T(8,128)S(1)} %get-tuple-element.43.base_moved, ...), custom_call_target="tpu_custom_call", output_to_operand_aliasing={{}: (6, {})} | custom-call | tf_op jit(solution)/shard_map/finish_second/pallas_call | solution.py:767
  (19 shorter events, 1.8 us)
Async XLA Ops:
  0.0 22.9 %collective-permute-start = (bf16[640,5120]{1,0:T(8,128)(2,1)}, bf16[640,5120]{1,0:T(8,128)(2,1)S(1)}, u32[]{:S(2)}, u32[]{:S(2)}) collective-permute-start(bf16[640,5120]{1,0:T(8,128)(2,1)} %w_own.3), channel_id=1, source_target_pairs={{0,1},{1,0},{2,3},{3,2},{4,5},{5,4},{6,7},{7,6},{8,9},{9,8},{10,11... | collective-permute-start | bytes 19660808 | tf_op jit(solution)/shard_map/ppermute | solution.py:630
  3.4 19.4 %copy-start = (s32[18]{0:T(128)}, s32[18]{0:T(128)S(1)}, u32[]{:S(2)}) copy-start(s32[18]{0:T(128)S(1)} %get-tuple-element.25.pairs) | copy-start | bytes 220
  3.4 8.7 %collective-permute-start.1 = (bf16[288,128]{1,0:T(8,128)(2,1)S(1)}, bf16[288,128]{1,0:T(8,128)(2,1)S(1)}, u32[]{:S(2)}, u32[]{:S(2)}) collective-permute-start(bf16[288,128]{1,0:T(8,128)(2,1)S(1)} %get-tuple-element.26), channel_id=1, source_target_pairs={{0,4},{4,8},{8,12},{12,16},{16,20},{20,24},{24,28},{28,0},{1,5},{5... | collective-permute-start | bytes 221192 | tf_op jit(solution)/shard_map/ppermute | solution.py:645
  6.0 8.0 %collective-permute-start.2 = (bf16[288,128]{1,0:T(8,128)(2,1)S(1)}, bf16[288,128]{1,0:T(8,128)(2,1)S(1)}, u32[]{:S(2)}, u32[]{:S(2)}) collective-permute-start(bf16[288,128]{1,0:T(8,128)(2,1)S(1)} %get-tuple-element.27), channel_id=1, source_target_pairs={{0,8},{4,12},{8,16},{12,20},{16,24},{20,28},{24,0},{28,4},{1,9},{5... | collective-permute-start | bytes 221192 | tf_op jit(solution)/shard_map/ppermute | solution.py:645
  7.6 10.9 %collective-permute-start.3 = (bf16[288,128]{1,0:T(8,128)(2,1)S(1)}, bf16[288,128]{1,0:T(8,128)(2,1)S(1)}, u32[]{:S(2)}, u32[]{:S(2)}) collective-permute-start(bf16[288,128]{1,0:T(8,128)(2,1)S(1)} %get-tuple-element.28), channel_id=1, source_target_pairs={{0,12},{4,16},{8,20},{12,24},{16,28},{20,0},{24,4},{28,8},{1,13},{... | collective-permute-start | bytes 221192 | tf_op jit(solution)/shard_map/ppermute | solution.py:645
  10.1 10.0 %collective-permute-start.4 = (bf16[288,128]{1,0:T(8,128)(2,1)S(1)}, bf16[288,128]{1,0:T(8,128)(2,1)S(1)}, u32[]{:S(2)}, u32[]{:S(2)}) collective-permute-start(bf16[288,128]{1,0:T(8,128)(2,1)S(1)} %get-tuple-element.29), channel_id=1, source_target_pairs={{0,16},{4,20},{8,24},{12,28},{16,0},{20,4},{24,8},{28,12},{1,17},{... | collective-permute-start | bytes 221192 | tf_op jit(solution)/shard_map/ppermute | solution.py:645
  12.2 9.1 %collective-permute-start.5 = (bf16[288,128]{1,0:T(8,128)(2,1)S(1)}, bf16[288,128]{1,0:T(8,128)(2,1)S(1)}, u32[]{:S(2)}, u32[]{:S(2)}) collective-permute-start(bf16[288,128]{1,0:T(8,128)(2,1)S(1)} %get-tuple-element.30), channel_id=1, source_target_pairs={{0,20},{4,24},{8,28},{12,0},{16,4},{20,8},{24,12},{28,16},{1,21},{... | collective-permute-start | bytes 221192 | tf_op jit(solution)/shard_map/ppermute | solution.py:645
  14.0 7.8 %collective-permute-start.6 = (bf16[288,128]{1,0:T(8,128)(2,1)S(1)}, bf16[288,128]{1,0:T(8,128)(2,1)S(1)}, u32[]{:S(2)}, u32[]{:S(2)}) collective-permute-start(bf16[288,128]{1,0:T(8,128)(2,1)S(1)} %get-tuple-element.31), channel_id=1, source_target_pairs={{0,24},{4,28},{8,0},{12,4},{16,8},{20,12},{24,16},{28,20},{1,25},{... | collective-permute-start | bytes 221192 | tf_op jit(solution)/shard_map/ppermute | solution.py:645
  18.5 4.4 %collective-permute-start.7 = (bf16[288,128]{1,0:T(8,128)(2,1)S(1)}, bf16[288,128]{1,0:T(8,128)(2,1)S(1)}, u32[]{:S(2)}, u32[]{:S(2)}) collective-permute-start(bf16[288,128]{1,0:T(8,128)(2,1)S(1)} %get-tuple-element.32), channel_id=1, source_target_pairs={{0,28},{4,0},{8,4},{12,8},{16,12},{20,16},{24,20},{28,24},{1,29},{... | collective-permute-start | bytes 221192 | tf_op jit(solution)/shard_map/ppermute | solution.py:645
  29.1 1.7 %collective-permute-start.8 = (bf16[272,640]{1,0:T(8,128)(2,1)S(1)}, bf16[272,640]{1,0:T(8,128)(2,1)S(1)}, u32[]{:S(2)}, u32[]{:S(2)}) collective-permute-start(bf16[272,640]{1,0:T(8,128)(2,1)S(1)} %get-tuple-element.33.h_own.h_first), channel_id=1, source_target_pairs={{0,1},{1,0},{2,3},{3,2},{4,5},{5,4},{6,7},{7,6},{8,9},{9,8},{10,11... | collective-permute-start | bytes 1044488 | tf_op jit(solution)/shard_map/ppermute | solution.py:705
  31.8 17.6 %collective-permute-start.12 = (bf16[256,1280]{1,0:T(8,128)(2,1)S(1)}, bf16[256,1280]{1,0:T(8,128)(2,1)S(1)}, u32[]{:S(2)}, u32[]{:S(2)}) collective-permute-start(bf16[256,1280]{1,0:T(8,128)(2,1)S(1)} %project.2.after), channel_id=1, source_target_pairs={{0,2},{1,3},{2,0},{3,1},{4,6},{5,7},{6,4},{7,5},{8,10},{9,11},{10,... | collective-permute-start | bytes 1966088 | tf_op jit(solution)/shard_map/ppermute | solution.py:707
  38.6 2.1 %collective-permute-start.9 = (bf16[256,640]{1,0:T(8,128)(2,1)S(1)}, bf16[256,640]{1,0:T(8,128)(2,1)S(1)}, u32[]{:S(2)}, u32[]{:S(2)}) collective-permute-start(bf16[256,640]{1,0:T(8,128)(2,1)S(1)} %attend_second.1.h_own.h_second), channel_id=1, source_target_pairs={{0,1},{1,0},{2,3},{3,2},{4,5},{5,4},{6,7},{7,6},{8,9},{9,8},{10,11... | collective-permute-start | bytes 983048 | tf_op jit(solution)/shard_map/ppermute | solution.py:705
  39.4 4.1 %collective-permute-start.10 = (bf16[4,4,1280]{2,1,0:T(4,128)(2,1)S(1)}, bf16[4,4,1280]{2,1,0:T(4,128)(2,1)S(1)}, u32[]{:S(2)}, u32[]{:S(2)}) collective-permute-start(bf16[4,4,1280]{2,1,0:T(4,128)(2,1)S(1)} %get-tuple-element.37), channel_id=1, source_target_pairs={{0,4},{4,0},{8,12},{12,8},{16,20},{20,16},{24,28},{28,24},{1,5},{5... | collective-permute-start | bytes 122888 | tf_op jit(solution)/shard_map/ppermute | solution.py:731
  43.5 4.1 %collective-permute-start.11 = (bf16[4,4,1280]{2,1,0:T(4,128)(2,1)S(1)}, bf16[4,4,1280]{2,1,0:T(4,128)(2,1)S(1)}, u32[]{:S(2)}, u32[]{:S(2)}) collective-permute-start(bf16[4,4,1280]{2,1,0:T(4,128)(2,1)S(1)} %pad_maximum_fusion), channel_id=1, source_target_pairs={{0,8},{4,12},{8,0},{12,4},{16,24},{20,28},{24,16},{28,20},{1,9},{5... | collective-permute-start | bytes 122888 | tf_op jit(solution)/shard_map/ppermute | solution.py:731
  45.4 18.2 %collective-permute-start.14 = (bf16[256,1280]{1,0:T(8,128)(2,1)S(1)}, bf16[256,1280]{1,0:T(8,128)(2,1)S(1)}, u32[]{:S(2)}, u32[]{:S(2)}) collective-permute-start(bf16[256,1280]{1,0:T(8,128)(2,1)S(1)} %project.3), channel_id=1, source_target_pairs={{0,2},{1,3},{2,0},{3,1},{4,6},{5,7},{6,4},{7,5},{8,10},{9,11},{10,... | collective-permute-start | bytes 1966088 | tf_op jit(solution)/shard_map/ppermute | solution.py:707
  49.5 5.2 %collective-permute-start.13 = (bf16[4,4,1280]{2,1,0:T(4,128)(2,1)S(1)}, bf16[4,4,1280]{2,1,0:T(4,128)(2,1)S(1)}, u32[]{:S(2)}, u32[]{:S(2)}) collective-permute-start(bf16[4,4,1280]{2,1,0:T(4,128)(2,1)S(1)} %pad_maximum_fusion.1), channel_id=1, source_target_pairs={{0,16},{4,20},{8,24},{12,28},{16,0},{20,4},{24,8},{28,12},{1,17},{... | collective-permute-start | bytes 122888 | tf_op jit(solution)/shard_map/ppermute | solution.py:731
  56.3 7.3 %collective-permute-start.15 = (bf16[16,1280]{1,0:T(8,128)(2,1)S(1)}, bf16[16,1280]{1,0:T(8,128)(2,1)S(1)}, u32[]{:S(2)}, u32[]{:S(2)}) collective-permute-start(bf16[16,1280]{1,0:T(8,128)(2,1)S(1)} %get-tuple-element.44), channel_id=1, source_target_pairs={{0,2},{1,3},{2,0},{3,1},{4,6},{5,7},{6,4},{7,5},{8,10},{9,11},{10,... | collective-permute-start | bytes 122888 | tf_op jit(solution)/shard_map/ppermute | solution.py:747

commit v5 on v4

--- a/solution.py
+++ b/solution.py
@@ -56,6 +56,14 @@
     return wait
 
 
+def quotient(a, b):
+    return a >> (b.bit_length() - 1) if b & (b - 1) == 0 else lax.div(a, b)
+
+
+def remainder(a, b):
+    return a & (b - 1) if b & (b - 1) == 0 else lax.rem(a, b)
+
+
 def list_pairs(row_of, pairs, me, replicas, moved):
     count = jnp.int32(0)
     for j in range(replicas):
@@ -69,11 +77,8 @@
     for j in range(replicas):
         row_of[j] = -1
 
-    shift = local_rows.bit_length() - 1
-
     def note(r, carry):
-        peer = partner[r] >> shift if local_rows == 1 << shift else lax.div(partner[r], local_rows)
-        row_of[peer] = r
+        row_of[quotient(partner[r], local_rows)] = r
         return carry
 
     lax.fori_loop(0, local_rows, note, 0, unroll=8)
@@ -84,11 +89,11 @@
     held, prefix = keys.shape[0], keys.shape[1]
     waits = []
     for i, k in enumerate(shifts):
-        peer = lax.rem(me + k, replicas)
+        peer = remainder(me + k, replicas)
         offset = jnp.int32(0)
         for s in range(fork.shape[0]):
             prompt = fork[s, peer]
-            offset = jnp.where(lax.div(prompt, held) == me, lax.rem(prompt, held), offset)
+            offset = jnp.where(quotient(prompt, held) == me, remainder(prompt, held), offset)
         copies = [
             (source.at[offset], outs[i].at[pl.ds(n * prefix, prefix)]) for n, source in enumerate((keys, values))
         ]
@@ -101,7 +106,7 @@
     width = hbm[0].shape[2]
     waits = []
     for i, k in enumerate(shifts):
-        r = row_of(lax.rem(me + k, replicas))
+        r = row_of(remainder(me + k, replicas))
         waits.append(load([(a.at[r], b.at[i]) for a, b in zip(hbm, vmem)], sems.at[i]))
     for i in range(len(shifts)):
         waits[i]()
@@ -157,14 +162,20 @@
     )
 
 
-def fill_meta(lookup, local_row, span, meta):
-    row_slot, fork, prompt_lengths, cache_lengths, finished, me, local_rows = lookup
-    g = me * local_rows + local_row
-    slot = row_slot[g]
-    values = (slot, prompt_lengths[fork[slot, me]], cache_lengths[g], 1 - finished[g])
-    size = span.stop - span.start
+def row_values(slots_of, lengths, finished, fork, prompt_lengths, slots):
+    me = lax.axis_index("replica")
+    shape = (HEAD_DIM, slots_of.shape[1])
+    slot, length, done = [jnp.broadcast_to(v[pl.ds(me, 1), :], shape) for v in (slots_of, lengths, finished)]
+    prompt = jnp.zeros(shape, jnp.int32)
+    for s in range(slots):
+        prompt = jnp.where(slot == s, prompt_lengths[fork[s, me]], prompt)
+    return [v.astype(jnp.float32).astype(jnp.bfloat16) for v in (slot, prompt, length, 1 - done)]
+
+
+def fill_meta(values, row_of, meta):
+    take = (row_of == iota(row_of.shape, 1)).astype(jnp.float32).astype(jnp.bfloat16)
     for i, value in enumerate(values):
-        meta[i, span, :] = jnp.full((size, HEAD_DIM), value, jnp.int32)
+        meta[i] = matmul(take, value, NT).astype(jnp.int32)
 
 
 def attend_scores(q, ck, cache_scores, *, steps, suffix):
@@ -269,11 +280,15 @@
     part = pl.ds(first_row * steps, rows * steps)
     keys = pl.ds(first_row * suffix, rows * suffix)
     q, nk, nv, ck, cv = hbm
-    return [
-        load([(q.at[pl.ds(first_row, rows)], vmem[0]), (ck.at[keys], vmem[3])], sems.at[0]),
-        load([(nk.at[part], vmem[1]), (nv.at[part], vmem[2])], sems.at[1]),
-        load([(cv.at[keys], vmem[4])], sems.at[2]),
-    ]
+    first = load([(q.at[pl.ds(first_row, rows)], vmem[0]), (ck.at[keys], vmem[3])], sems.at[0])
+
+    def rest():
+        return [
+            load([(nk.at[part], vmem[1]), (nv.at[part], vmem[2])], sems.at[1]),
+            load([(cv.at[keys], vmem[4])], sems.at[2]),
+        ]
+
+    return first, rest
 
 
 def attend_rows(lookup, first_row, waits, vmem, pk, pv, heads, work, *, steps, slots, suffix):
@@ -282,9 +297,9 @@
     count, _, n, _ = meta.shape
     rows = n // steps
     per = 16 // steps
-    for b in range(count * rows):
-        low = b % rows * steps
-        fill_meta(lookup, first_row + b, slice(low, low + steps), meta.at[b // rows])
+    shape = (n, lookup[0].shape[1])
+    for i in range(count):
+        fill_meta(lookup, first_row + i * rows + iota(shape, 0) // steps, meta.at[i])
     waits[0]()
     for b in range(0, count * rows, per):
         part = [q3[b + i].astype(jnp.float32) for i in range(per)]
@@ -305,7 +320,7 @@
 
 
 def first_kernel(
-    fork, pairs, row_slot, prompt_lengths, cache_lengths, finished, q, nk, nv, ck, cv, own_keys, own_values, w_own, w_sib,
+    fork, pairs, prompt_lengths, row_slot, cache_lengths, finished, q, nk, nv, ck, cv, own_keys, own_values, w_own, w_sib,
     *rest, stacked, replicas, slots, moved, steps, suffix, span
 ):
     recvs, rest = rest[:-24], rest[-24:]
@@ -313,11 +328,11 @@
     vmem, work, (row_sems, slot_sems, w_sems, sems, cache_sems) = rest[8:13], rest[13:19], rest[19:]
     me = lax.axis_index("replica")
     held, prefix = own_keys.shape[0], own_keys.shape[1]
-    waits = start_rows(0, (q, nk, nv, ck, cv), vmem, row_sems, steps, suffix)
+    scores_ready, start_rest = start_rows(0, (q, nk, nv, ck, cv), vmem, row_sems, steps, suffix)
     for s in range(slots):
         prompt = fork[s, me]
-        owner = lax.div(prompt, held)
-        offset = lax.rem(prompt, held)
+        owner = quotient(prompt, held)
+        offset = remainder(prompt, held)
         targets = (pk.at[pl.ds(s * prefix, prefix)], pv.at[pl.ds(s * prefix, prefix)])
         if stacked:
             for i in range(2):
@@ -325,7 +340,7 @@
                     recvs[0].at[owner, pl.ds(i * prefix, prefix)], targets[i], slot_sems.at[s, i]
                 ).start()
             continue
-        k = lax.rem(me - owner + replicas, replicas)
+        k = remainder(me - owner + replicas, replicas)
 
         @pl.when(k == 0)
         def _():
@@ -341,6 +356,7 @@
                         recvs[kk - 1].at[pl.ds(i * prefix, prefix)], targets[i], slot_sems.at[s, i]
                     ).start()
 
+    waits = [scores_ready, *start_rest()]
     groups = q.shape[2] // HEAD_DIM
     for i in range(moved):
         peer = pairs[moved + 1 + i]
@@ -349,7 +365,7 @@
                 recvs[0].at[peer, pl.ds(2 * prefix, span)], x.at[pl.ds(i * span, span)], sems.at[i]
             ).start()
         else:
-            k = lax.rem(me - peer + replicas, replicas)
+            k = remainder(me - peer + replicas, replicas)
             for kk in range(1, replicas):
 
                 @pl.when(k == kk)
@@ -376,9 +392,13 @@
             for i, target in enumerate((pk, pv)):
                 pltpu.make_async_copy(own_keys.at[0], target.at[pl.ds(s * prefix, prefix)], slot_sems.at[s, i]).wait()
 
-    lookup = (row_slot, fork, prompt_lengths, cache_lengths, finished, me, q.shape[0])
+    lookup = row_values(row_slot, cache_lengths, finished, fork, prompt_lengths, slots)
+    shape = (moved * span, row_slot.shape[1])
+    item = iota(shape, 0) // span
+    row_of = jnp.zeros(shape, jnp.int32)
     for i in range(moved):
-        fill_meta(lookup, pairs[i], slice(i * span, (i + 1) * span), moved_meta)
+        row_of = jnp.where(item == i, pairs[i], row_of)
+    fill_meta(lookup, row_of, moved_meta)
     n = heads.shape[0] - moved * steps
     attend_rows(
         lookup, 0, (waits[0], wait_second, waits[2]), vmem, pk, pv, heads.at[pl.ds(0, n)], work,
@@ -401,12 +421,13 @@
 
 
 def second_kernel(
-    fork, row_slot, prompt_lengths, cache_lengths, finished, pk, pv, q, nk, nv, ck, cv, after, *rest,
+    fork, prompt_lengths, row_slot, cache_lengths, finished, pk, pv, q, nk, nv, ck, cv, after, *rest,
     first_row, slots, steps, suffix
 ):
     heads, vmem, work, row_sems = rest[0], rest[1:6], rest[6:12], rest[12]
-    waits = start_rows(first_row, (q, nk, nv, ck, cv), vmem, row_sems, steps, suffix)
-    lookup = (row_slot, fork, prompt_lengths, cache_lengths, finished, lax.axis_index("replica"), q.shape[0])
+    scores_ready, start_rest = start_rows(first_row, (q, nk, nv, ck, cv), vmem, row_sems, steps, suffix)
+    waits = [scores_ready, *start_rest()]
+    lookup = row_values(row_slot, cache_lengths, finished, fork, prompt_lengths, slots)
     attend_rows(
         lookup, first_row, waits, vmem, pk, pv, heads, work, steps=steps, slots=slots, suffix=suffix
     )
@@ -419,7 +440,7 @@
 
 
 def base_kernel(
-    h_first, s_first, h_second, s_second, h_moved, w_own, w_sib, residual, out, moved_out, weights, before, sems
+    pairs, h_first, s_first, h_second, s_second, h_moved, w_own, w_sib, residual, out, moved_out, weights, before, sems
 ):
     rows, model = out.shape
     width = w_own.shape[0]
@@ -434,7 +455,10 @@
         sems,
     )
     ready()
-    moved_out[...] = matmul(h_moved[...], weights[...], NN)
+    moved_total = matmul(h_moved[...], weights[...], NN)
+    for i in range(h_moved.shape[0] // steps):
+        part = slice(i * steps, (i + 1) * steps)
+        moved_out[part, :] = moved_total[part] + before[pairs[i]].astype(jnp.float32)
     low = 0
     for h_own, h_sib, size in ((h_first, s_first, rows - h_second.shape[0]), (h_second, s_second, h_second.shape[0])):
         part = pl.ds(0, size)
@@ -453,13 +477,13 @@
         value = both[i * steps : (i + 1) * steps].astype(outs[0].dtype)
         if split:
             k = jnp.bitwise_xor(me, peer)
-            place = 2 * lax.rem(lax.div(k, 2), 2) + lax.div(k, 4)
-
-            @pl.when(lax.rem(k, 2) == 0)
+            place = 2 * remainder(quotient(k, 2), 2) + quotient(k, 4)
+
+            @pl.when(remainder(k, 2) == 0)
             def _():
                 outs[0][place] = value
 
-            @pl.when(lax.rem(k, 2) == 1)
+            @pl.when(remainder(k, 2) == 1)
             def _():
                 outs[1][place] = value
 
@@ -500,38 +524,41 @@
     add_rows(base[part, :] + recv[part, :].astype(jnp.float32), out, 0, steps)
 
 
-def finish_second_kernel(
-    pairs, base, recv, base_moved, recv_moved, residual, earlier, out, before, after, rows_out, sems, row_sems, *, moved
-):
+def finish_second_kernel(pairs, base, recv, base_moved, recv_moved, earlier, out, after, rows_out, sems, row_sems, *, moved):
     later, steps = rows_out.shape[:2]
     half = out.shape[0] - later
-    n = half * steps
-    fetch = [load([(residual.at[pairs[i]], before.at[i])], sems.at[i]) for i in range(moved)]
-    add_rows(base[n:, :] + recv[...].astype(jnp.float32), rows_out, 0, steps)
     branch = base_moved[...] + recv_moved[...].astype(jnp.float32)
     for i in range(moved):
-        r = pairs[i]
-        fetch[i]()
-        value = branch[i * steps : (i + 1) * steps] + before[i].astype(jnp.float32)
-        after[i] = value.astype(after.dtype)
-
-        @pl.when(r >= half)
+        after[i] = branch[i * steps : (i + 1) * steps].astype(after.dtype)
+
+        @pl.when(pairs[i] < half)
         def _():
-            rows_out[jnp.maximum(r - half, 0)] = after[i]
-
-        @pl.when(r < half)
+            pltpu.make_async_copy(after.at[i], out.at[pairs[i]], sems.at[i]).start()
+
+    size = 16
+    done = []
+    for part in range(later // size):
+        low = part * size
+        rows = slice((half + low) * steps, (half + low + size) * steps)
+        got = slice(low * steps, (low + size) * steps)
+        add_rows(base[rows, :] + recv[got, :].astype(jnp.float32), rows_out, low, steps)
+        for i in range(moved):
+            r = pairs[i] - half
+
+            @pl.when((r >= low) & (r < low + size))
+            def _():
+                rows_out[r] = after[i]
+
+        piece = pl.ds(low, size)
+        done.append(load([(rows_out.at[piece], out.at[pl.ds(half + low, size)])], row_sems.at[part]))
+    for i in range(moved):
+
+        @pl.when(pairs[i] < half)
         def _():
-            pltpu.make_async_copy(after.at[i], out.at[r], sems.at[i, 0]).start()
-
-    done = load([(rows_out, out.at[pl.ds(half, later)])], row_sems)
-    for i in range(moved):
-        r = pairs[i]
-
-        @pl.when(r < half)
-        def _():
-            pltpu.make_async_copy(after.at[i], out.at[r], sems.at[i, 0]).wait()
-
-    done()
+            pltpu.make_async_copy(after.at[i], out.at[pairs[i]], sems.at[i]).wait()
+
+    for wait in done:
+        wait()
 
 
 def row_buffers(count, steps, width, dtype):
@@ -669,12 +696,13 @@
         ]
 
     sizes = dict(slots=slots, steps=steps, suffix=suffix)
-    lookup = in_hbm(row_slot, prompt_lengths, cache_lengths, finished)
+    by_replica = [x.reshape(replicas, local_rows) for x in (row_slot, cache_lengths, finished)]
+    lookup = in_hbm(prompt_lengths, *by_replica)
     rows_in = in_hbm(queries, nk2, nv2, ck2, cv2)
     h_first, pk, pv, w_there = pl.pallas_call(
         functools.partial(first_kernel, stacked=stacked, replicas=replicas, moved=moved, span=span, **sizes),
         out_shape=[pltpu.VMEM((nh + m, width), dtype), prompts, prompts, pltpu.VMEM((2 * width, model), dtype)],
-        in_specs=[SMEM] * 6 + [ANY] * (9 + len(received)),
+        in_specs=[SMEM] * 3 + [VMEM] * 3 + [ANY] * (9 + len(received)),
         out_specs=[VMEM] * 4,
         scratch_shapes=[
             pltpu.VMEM((moved * span, HEAD_DIM), dtype),
@@ -720,7 +748,7 @@
         functools.partial(second_kernel, first_row=half * BLOCK, **sizes),
         "attend_second",
         [((n - nh, width), dtype)],
-        [SMEM] * 5 + [VMEM] * 2 + [ANY] * 6,
+        [SMEM] * 2 + [VMEM] * 5 + [ANY] * 6,
         (*in_hbm(fork), *lookup, pk, pv, *rows_in, c_first),
         work(blocks - half),
     )
@@ -749,8 +777,8 @@
         base_kernel,
         "base",
         [((n, model), jnp.float32), ((m, model), jnp.float32)],
-        [VMEM] * 5 + [ANY] * 3,
-        (h_first, s_first, h_second, s_second, home_heads, *in_hbm(out_proj), w_sib, *in_hbm(residual)),
+        [SMEM] + [VMEM] * 5 + [ANY] * 3,
+        (*in_hbm(pairs), h_first, s_first, h_second, s_second, home_heads, *in_hbm(out_proj), w_sib, *in_hbm(residual)),
         [pltpu.VMEM((2 * width, model), dtype), pltpu.VMEM(residual.shape, dtype), dma(3)],
     )
 
@@ -766,20 +794,19 @@
     )(base, got_first)
     return pl.pallas_call(
         functools.partial(finish_second_kernel, moved=moved),
-        in_specs=[SMEM, VMEM, VMEM, VMEM, VMEM, ANY, ANY],
+        in_specs=[SMEM, VMEM, VMEM, VMEM, VMEM, ANY],
         out_specs=ANY,
         out_shape=whole,
-        input_output_aliases={6: 0},
+        input_output_aliases={5: 0},
         scratch_shapes=[
             pltpu.VMEM((moved, steps, model), dtype),
-            pltpu.VMEM((moved, steps, model), dtype),
             pltpu.VMEM(((blocks - half) * BLOCK, steps, model), dtype),
-            dma(moved, 1),
-            dma(1),
+            dma(moved),
+            dma((blocks - half) * BLOCK // 16, 1),
         ],
         compiler_params=params(),
         name="finish_second",
-    )(*in_hbm(pairs), base, got_second, base_moved, got_moved, *in_hbm(residual), out)
+    )(*in_hbm(pairs), base, got_second, base_moved, got_moved, out)
 
 
 def solution(mesh):

time: 66.5 us -> 65.8 us (0.989)
  transfers between devices with their start and end apart: 16 -> 16, of which waited for: 11 -> 10; matrix products, arithmetic and copies ran while one was open for 0% -> 0% of each run, Pallas kernels for 25% -> 26%
where the time goes in v5:
time: 65.8 us; the launch traced here: 65.4 us
  Pallas kernels  25.9 us (39%)
  starting transfers between devices  21.7 us (33%)
  waiting for transfers between devices  17.4 us (26%)
    pallas_call x6, Pallas kernels, call(): pl.pallas_call(kernel, out_shape=[pltpu.VMEM(shape, kind) for shape, kind...  14.3 us
    ppermute x7, starting transfers between devices, body(): lax.ppermute(block, 'replica', [(i, (i + k) % replicas) for i in range(re...  12.6 us
    ppermute x3, waiting for transfers between devices, body(): lax.ppermute(x, 'replica', [(i, i ^ bit) for i in range(replicas)])  6.96 us
    ppermute x7, waiting for transfers between devices, body(): lax.ppermute(block, 'replica', [(i, (i + k) % replicas) for i in range(re...  6.76 us
    pallas_call x1, Pallas kernels, body(): pl.pallas_call(functools.partial(first_kernel, stacked=stacked, replicas=...  6.1 us
    ppermute x3, starting transfers between devices, body(): lax.ppermute(x, 'replica', [(i, i ^ bit) for i in range(replicas)])  4.74 us
    pallas_call x1, Pallas kernels, exchange_pack(): pl.pallas_call(functools.partial(pack_kernel, replicas=replicas, moved=mo...  2.9 us
    ppermute x2, starting transfers between devices, cross(): return (sib, crossed, lax.ppermute(crossed, 'tensor', across))  2.17 us
  transfers between devices with their start and end apart: 16, of which 10 were waited for; matrix products, arithmetic and copies ran while one was open for 0% of the time, Pallas kernels for 26%

profile of v5, /device:TPU:0, one launch (start us, length us, event | category | flops | bytes accessed | tf_op | source)
XLA Modules:
  0.0 65.4 jit_solution(7768323815893301633)
XLA Ops:
  0.5 2.9 %pack.1 = (bf16[288,128]{1,0:T(8,128)(2,1)S(1)}, bf16[288,128]{1,0:T(8,128)(2,1)S(1)}, bf16[288,128]{1,0:T(8,128)(2,1)S(1)}, bf16[288,128]{1,0:T(8,128)(2,1)S(1)...) custom-call(s32[4,8]{1,0:T(4,128)} %bitcast.16, ...), custom_call_target="tpu_custom_call" | custom-call | tf_op jit(solution)/shard_map/pack/pallas_call | solution.py:581
  3.4 2.6 %collective-permute-start.1 = (bf16[288,128]{1,0:T(8,128)(2,1)S(1)}, bf16[288,128]{1,0:T(8,128)(2,1)S(1)}, u32[]{:S(2)}, u32[]{:S(2)}) collective-permute-start(bf16[288,128]{1,0:T(8,128)(2,1)S(1)} %get-tuple-element.26), channel_id=1, source_target_pairs={{0,4},{4,8},{8,12},{12,16},{16,20},{20,24},{24,28},{28,0},{1,5},{5... | collective-permute-start | bytes 221192 | tf_op jit(solution)/shard_map/ppermute | solution.py:672
  5.9 1.6 %collective-permute-start.2 = (bf16[288,128]{1,0:T(8,128)(2,1)S(1)}, bf16[288,128]{1,0:T(8,128)(2,1)S(1)}, u32[]{:S(2)}, u32[]{:S(2)}) collective-permute-start(bf16[288,128]{1,0:T(8,128)(2,1)S(1)} %get-tuple-element.27), channel_id=1, source_target_pairs={{0,8},{4,12},{8,16},{12,20},{16,24},{20,28},{24,0},{28,4},{1,9},{5... | collective-permute-start | bytes 221192 | tf_op jit(solution)/shard_map/ppermute | solution.py:672
  7.5 2.5 %collective-permute-start.3 = (bf16[288,128]{1,0:T(8,128)(2,1)S(1)}, bf16[288,128]{1,0:T(8,128)(2,1)S(1)}, u32[]{:S(2)}, u32[]{:S(2)}) collective-permute-start(bf16[288,128]{1,0:T(8,128)(2,1)S(1)} %get-tuple-element.28), channel_id=1, source_target_pairs={{0,12},{4,16},{8,20},{12,24},{16,28},{20,0},{24,4},{28,8},{1,13},{... | collective-permute-start | bytes 221192 | tf_op jit(solution)/shard_map/ppermute | solution.py:672
  10.1 1.2 %collective-permute-start.4 = (bf16[288,128]{1,0:T(8,128)(2,1)S(1)}, bf16[288,128]{1,0:T(8,128)(2,1)S(1)}, u32[]{:S(2)}, u32[]{:S(2)}) collective-permute-start(bf16[288,128]{1,0:T(8,128)(2,1)S(1)} %get-tuple-element.29), channel_id=1, source_target_pairs={{0,16},{4,20},{8,24},{12,28},{16,0},{20,4},{24,8},{28,12},{1,17},{... | collective-permute-start | bytes 221192 | tf_op jit(solution)/shard_map/ppermute | solution.py:672
  11.3 0.8 %collective-permute-done.1.rest_0_ = bf16[288,128]{1,0:T(8,128)(2,1)S(1)} collective-permute-done((bf16[288,128]{1,0:T(8,128)(2,1)S(1)}, bf16[288,128]{1,0:T(8,128)(2,1)S(1)}, u32[]{:S(2)}, u32[]{:S(2)}) %collective-permute-start.1) | collective-permute-done | bytes 73760 | tf_op jit(solution)/shard_map/ppermute | solution.py:672
  12.1 1.8 %collective-permute-start.5 = (bf16[288,128]{1,0:T(8,128)(2,1)S(1)}, bf16[288,128]{1,0:T(8,128)(2,1)S(1)}, u32[]{:S(2)}, u32[]{:S(2)}) collective-permute-start(bf16[288,128]{1,0:T(8,128)(2,1)S(1)} %get-tuple-element.30), channel_id=1, source_target_pairs={{0,20},{4,24},{8,28},{12,0},{16,4},{20,8},{24,12},{28,16},{1,21},{... | collective-permute-start | bytes 221192 | tf_op jit(solution)/shard_map/ppermute | solution.py:672
  13.9 1.3 %collective-permute-start.6 = (bf16[288,128]{1,0:T(8,128)(2,1)S(1)}, bf16[288,128]{1,0:T(8,128)(2,1)S(1)}, u32[]{:S(2)}, u32[]{:S(2)}) collective-permute-start(bf16[288,128]{1,0:T(8,128)(2,1)S(1)} %get-tuple-element.31), channel_id=1, source_target_pairs={{0,24},{4,28},{8,0},{12,4},{16,8},{20,12},{24,16},{28,20},{1,25},{... | collective-permute-start | bytes 221192 | tf_op jit(solution)/shard_map/ppermute | solution.py:672
  15.3 3.1 %collective-permute-done.3.rest_2_ = bf16[288,128]{1,0:T(8,128)(2,1)S(1)} collective-permute-done((bf16[288,128]{1,0:T(8,128)(2,1)S(1)}, bf16[288,128]{1,0:T(8,128)(2,1)S(1)}, u32[]{:S(2)}, u32[]{:S(2)}) %collective-permute-start.3) | collective-permute-done | bytes 73760 | tf_op jit(solution)/shard_map/ppermute | solution.py:672
  18.4 1.6 %collective-permute-start.7 = (bf16[288,128]{1,0:T(8,128)(2,1)S(1)}, bf16[288,128]{1,0:T(8,128)(2,1)S(1)}, u32[]{:S(2)}, u32[]{:S(2)}) collective-permute-start(bf16[288,128]{1,0:T(8,128)(2,1)S(1)} %get-tuple-element.32), channel_id=1, source_target_pairs={{0,28},{4,0},{8,4},{12,8},{16,12},{20,16},{24,20},{28,24},{1,29},{... | collective-permute-start | bytes 221192 | tf_op jit(solution)/shard_map/ppermute | solution.py:672
  20.0 1.2 %collective-permute-done.5.rest_4_ = bf16[288,128]{1,0:T(8,128)(2,1)S(1)} collective-permute-done((bf16[288,128]{1,0:T(8,128)(2,1)S(1)}, bf16[288,128]{1,0:T(8,128)(2,1)S(1)}, u32[]{:S(2)}, u32[]{:S(2)}) %collective-permute-start.5) | collective-permute-done | bytes 73760 | tf_op jit(solution)/shard_map/ppermute | solution.py:672
  21.8 1.0 %collective-permute-done.7.rest_6_ = bf16[288,128]{1,0:T(8,128)(2,1)S(1)} collective-permute-done((bf16[288,128]{1,0:T(8,128)(2,1)S(1)}, bf16[288,128]{1,0:T(8,128)(2,1)S(1)}, u32[]{:S(2)}, u32[]{:S(2)}) %collective-permute-start.7) | collective-permute-done | bytes 73760 | tf_op jit(solution)/shard_map/ppermute | solution.py:672
  22.8 6.1 %attend_first.1 = (bf16[272,640]{1,0:T(8,128)(2,1)S(1)}, bf16[512,128]{1,0:T(8,128)(2,1)S(1)}, bf16[512,128]{1,0:T(8,128)(2,1)S(1)}, bf16[1280,1280]{1,0:T(8,128)(2,1)S(1)}) custom-call(s32[4,8]{1,0:T(4,128)} %bitcast.17, s32[18]{0:T(128)} %copy-done, s32[32]{0:T(128)} %prompt_lengths.3, s32[8,128]{1,0:T(8,128)} %bitcast.19, s32[8,128]{1,0:T(8,128)} %bitcast.21, ...), custom_call_target="tpu_custom_call" | custom-call | flops 1 | bytes 1 | tf_op jit(solution)/shard_map/attend_first/pallas_call | solution.py:702
  29.0 1.6 %collective-permute-done.8.h_sib.s_first = bf16[272,640]{1,0:T(8,128)(2,1)S(1)} collective-permute-done((bf16[272,640]{1,0:T(8,128)(2,1)S(1)}, bf16[272,640]{1,0:T(8,128)(2,1)S(1)}, u32[]{:S(2)}, u32[]{:S(2)}) %collective-permute-start.8) | collective-permute-done | bytes 348192 | tf_op jit(solution)/shard_map/ppermute | solution.py:733
  30.6 1.0 %project.2.after = bf16[256,1280]{1,0:T(8,128)(2,1)S(1)} custom-call(bf16[272,640]{1,0:T(8,128)(2,1)S(1)} %get-tuple-element.33.h_own.h_first, bf16[272,640]{1,0:T(8,128)(2,1)S(1)} %collective-permute-done.8.h_sib.s_first, bf16[1280,1280]{1,0:T(8,128)(2,1)S(1)} %get-tuple-element.36.weights.w_there), custom_call_target="tpu_custom_call" | custom-call | flops 1 | bytes 1 | tf_op jit(solution)/shard_map/project/pallas_call | solution.py:721
  31.7 1.6 %collective-permute-start.12 = (bf16[256,1280]{1,0:T(8,128)(2,1)S(1)}, bf16[256,1280]{1,0:T(8,128)(2,1)S(1)}, u32[]{:S(2)}, u32[]{:S(2)}) collective-permute-start(bf16[256,1280]{1,0:T(8,128)(2,1)S(1)} %project.2.after), channel_id=1, source_target_pairs={{0,2},{1,3},{2,0},{3,1},{4,6},{5,7},{6,4},{7,5},{8,10},{9,11},{10,... | collective-permute-start | bytes 1966088 | tf_op jit(solution)/shard_map/ppermute | solution.py:735
  33.2 5.1 %attend_second.1.h_own.h_second = bf16[256,640]{1,0:T(8,128)(2,1)S(1)} custom-call(s32[4,8]{1,0:T(4,128)} %bitcast.18, s32[32]{0:T(128)} %prompt_lengths.3, s32[8,128]{1,0:T(8,128)} %bitcast.20, s32[8,128]{1,0:T(8,128)} %bitcast.22, s32[8,128]{1,0:T(8,128)} %bitcast.24, bf16[512,128]{1,0:T(8,128)(2,1)S(1)} %get-tuple-element.34.pk, ...), custom_call_target="tpu_custom_call" | custom-call | flops 1 | bytes 1 | tf_op jit(solution)/shard_map/attend_second/pallas_call | solution.py:721
  38.4 0.7 %moved_send.1 = (bf16[4,4,1280]{2,1,0:T(4,128)(2,1)S(1)}, bf16[4,4,1280]{2,1,0:T(4,128)(2,1)S(1)}) custom-call(s32[18]{0:T(128)} %copy-done, bf16[272,640]{1,0:T(8,128)(2,1)S(1)} %get-tuple-element.33.h_own.h_first, bf16[272,640]{1,0:T(8,128)(2,1)S(1)} %collective-permute-done.8.h_sib.s_first, bf16[256,1280]{1,0:T(8,128)(2,1)S(1)} %project.2.after), custom_call_target="tpu_custom_call" | custom-call | flops 1 | bytes 1 | tf_op jit(solution)/shard_map/moved_send/pallas_call | solution.py:721
  39.1 1.3 %collective-permute-start.10 = (bf16[4,4,1280]{2,1,0:T(4,128)(2,1)S(1)}, bf16[4,4,1280]{2,1,0:T(4,128)(2,1)S(1)}, u32[]{:S(2)}, u32[]{:S(2)}) collective-permute-start(bf16[4,4,1280]{2,1,0:T(4,128)(2,1)S(1)} %get-tuple-element.37), channel_id=1, source_target_pairs={{0,4},{4,0},{8,12},{12,8},{16,20},{20,16},{24,28},{28,24},{1,5},{5... | collective-permute-start | bytes 122888 | tf_op jit(solution)/shard_map/ppermute | solution.py:759
  40.4 1.0 %project.3 = bf16[256,1280]{1,0:T(8,128)(2,1)S(1)} custom-call(bf16[256,640]{1,0:T(8,128)(2,1)S(1)} %attend_second.1.h_own.h_second, bf16[256,640]{1,0:T(8,128)(2,1)S(1)} %collective-permute-done.9.h_sib.s_second, bf16[1280,1280]{1,0:T(8,128)(2,1)S(1)} %get-tuple-element.36.weights.w_there), custom_call_target="tpu_custom_call" | custom-call | flops 1 | bytes 1 | tf_op jit(solution)/shard_map/project/pallas_call | solution.py:721
  41.5 1.7 %collective-permute-done.10.rest_0_ = bf16[4,4,1280]{2,1,0:T(4,128)(2,1)S(1)} collective-permute-done((bf16[4,4,1280]{2,1,0:T(4,128)(2,1)S(1)}, bf16[4,4,1280]{2,1,0:T(4,128)(2,1)S(1)}, u32[]{:S(2)}, u32[]{:S(2)}) %collective-permute-start.10) | collective-permute-done | bytes 40992 | tf_op jit(solution)/shard_map/ppermute | solution.py:759
  43.2 1.9 %collective-permute-start.11 = (bf16[4,4,1280]{2,1,0:T(4,128)(2,1)S(1)}, bf16[4,4,1280]{2,1,0:T(4,128)(2,1)S(1)}, u32[]{:S(2)}, u32[]{:S(2)}) collective-permute-start(bf16[4,4,1280]{2,1,0:T(4,128)(2,1)S(1)} %pad_maximum_fusion), channel_id=1, source_target_pairs={{0,8},{4,12},{8,0},{12,4},{16,24},{20,28},{24,16},{28,20},{1,9},{5... | collective-permute-start | bytes 122888 | tf_op jit(solution)/shard_map/ppermute | solution.py:759
  45.1 0.6 collective-permute-start.14
  45.7 1.6 %collective-permute-done.11.rest_1_ = bf16[4,4,1280]{2,1,0:T(4,128)(2,1)S(1)} collective-permute-done((bf16[4,4,1280]{2,1,0:T(4,128)(2,1)S(1)}, bf16[4,4,1280]{2,1,0:T(4,128)(2,1)S(1)}, u32[]{:S(2)}, u32[]{:S(2)}) %collective-permute-start.11) | collective-permute-done | bytes 40992 | tf_op jit(solution)/shard_map/ppermute | solution.py:759
  47.3 2.0 %collective-permute-done.12.recv = bf16[256,1280]{1,0:T(8,128)(2,1)S(1)} collective-permute-done((bf16[256,1280]{1,0:T(8,128)(2,1)S(1)}, bf16[256,1280]{1,0:T(8,128)(2,1)S(1)}, u32[]{:S(2)}, u32[]{:S(2)}) %collective-permute-start.12) | collective-permute-done | bytes 655392 | tf_op jit(solution)/shard_map/ppermute | solution.py:735
  49.4 1.6 %collective-permute-start.13 = (bf16[4,4,1280]{2,1,0:T(4,128)(2,1)S(1)}, bf16[4,4,1280]{2,1,0:T(4,128)(2,1)S(1)}, u32[]{:S(2)}, u32[]{:S(2)}) collective-permute-start(bf16[4,4,1280]{2,1,0:T(4,128)(2,1)S(1)} %pad_maximum_fusion.1), channel_id=1, source_target_pairs={{0,16},{4,20},{8,24},{12,28},{16,0},{20,4},{24,8},{28,12},{1,17},{... | collective-permute-start | bytes 122888 | tf_op jit(solution)/shard_map/ppermute | solution.py:759
  50.9 3.7 %collective-permute-done.13.rest_2_ = bf16[4,4,1280]{2,1,0:T(4,128)(2,1)S(1)} collective-permute-done((bf16[4,4,1280]{2,1,0:T(4,128)(2,1)S(1)}, bf16[4,4,1280]{2,1,0:T(4,128)(2,1)S(1)}, u32[]{:S(2)}, u32[]{:S(2)}) %collective-permute-start.13) | collective-permute-done | bytes 40992 | tf_op jit(solution)/shard_map/ppermute | solution.py:759
  54.6 1.5 %moved_project.1 = (bf16[16,1280]{1,0:T(8,128)(2,1)S(1)}, bf16[16,1280]{1,0:T(8,128)(2,1)S(1)}) custom-call(s32[18]{0:T(128)} %copy-done, bf16[1280,1280]{1,0:T(8,128)(2,1)S(1)} %get-tuple-element.36.weights.w_there, bf16[4,4,1280]{2,1,0:T(4,128)(2,1)S(1)} %collective-permute-done.10.rest_0_, bf16[4,4,1280]{2,1,0:T(4,128)(2,1)S(1)} %collective-permute-done.11.rest_1_, ...), custom_call_target="tpu_custom_call" | custom-call | flops 1 | bytes 1 | tf_op jit(solution)/shard_map/moved_project/pallas_call | solution.py:721
  56.1 1.5 %collective-permute-start.15 = (bf16[16,1280]{1,0:T(8,128)(2,1)S(1)}, bf16[16,1280]{1,0:T(8,128)(2,1)S(1)}, u32[]{:S(2)}, u32[]{:S(2)}) collective-permute-start(bf16[16,1280]{1,0:T(8,128)(2,1)S(1)} %get-tuple-element.44), channel_id=1, source_target_pairs={{0,2},{1,3},{2,0},{3,1},{4,6},{5,7},{6,4},{7,5},{8,10},{9,11},{10,... | collective-permute-start | bytes 122888 | tf_op jit(solution)/shard_map/ppermute | solution.py:775
  57.7 4.9 %base.1 = (f32[512,1280]{1,0:T(8,128)S(1)}, f32[16,1280]{1,0:T(8,128)S(1)}) custom-call(s32[18]{0:T(128)} %copy-done, bf16[272,640]{1,0:T(8,128)(2,1)S(1)} %get-tuple-element.33.h_own.h_first, bf16[272,640]{1,0:T(8,128)(2,1)S(1)} %collective-permute-done.8.h_sib.s_first, bf16[256,640]{1,0:T(8,128)(2,1)S(1)} %attend_second.1.h_own.h_second, ...), custom_call_target="tpu_custom_call" | custom-call | flops 1 | bytes 1 | tf_op jit(solution)/shard_map/base/pallas_call | solution.py:721
  62.6 0.9 %finish_first.1.earlier = bf16[128,4,1280]{2,1,0:T(4,128)(2,1)} custom-call(f32[512,1280]{1,0:T(8,128)S(1)} %get-tuple-element.42.base, bf16[256,1280]{1,0:T(8,128)(2,1)S(1)} %collective-permute-done.12.recv), custom_call_target="tpu_custom_call" | custom-call | tf_op jit(solution)/shard_map/finish_first/pallas_call | solution.py:786
  63.5 1.7 %finish_second.1 = bf16[128,4,1280]{2,1,0:T(4,128)(2,1)} custom-call(s32[18]{0:T(128)} %copy-done, f32[512,1280]{1,0:T(8,128)S(1)} %get-tuple-element.42.base, bf16[256,1280]{1,0:T(8,128)(2,1)S(1)} %collective-permute-done.14.recv, f32[16,1280]{1,0:T(8,128)S(1)} %get-tuple-element.43.base_moved, ...), custom_call_target="tpu_custom_call", output_to_operand_aliasing={{}: (5, {})} | custom-call | tf_op jit(solution)/shard_map/finish_second/pallas_call | solution.py:795
  (19 shorter events, 1.3 us)
Async XLA Ops:
  0.0 22.8 %collective-permute-start = (bf16[640,5120]{1,0:T(8,128)(2,1)}, bf16[640,5120]{1,0:T(8,128)(2,1)S(1)}, u32[]{:S(2)}, u32[]{:S(2)}) collective-permute-start(bf16[640,5120]{1,0:T(8,128)(2,1)} %w_own.3), channel_id=1, source_target_pairs={{0,1},{1,0},{2,3},{3,2},{4,5},{5,4},{6,7},{7,6},{8,9},{9,8},{10,11... | collective-permute-start | bytes 19660808 | tf_op jit(solution)/shard_map/ppermute | solution.py:657
  3.4 19.4 %copy-start = (s32[18]{0:T(128)}, s32[18]{0:T(128)S(1)}, u32[]{:S(2)}) copy-start(s32[18]{0:T(128)S(1)} %get-tuple-element.25.pairs) | copy-start | bytes 220
  3.4 8.8 %collective-permute-start.1 = (bf16[288,128]{1,0:T(8,128)(2,1)S(1)}, bf16[288,128]{1,0:T(8,128)(2,1)S(1)}, u32[]{:S(2)}, u32[]{:S(2)}) collective-permute-start(bf16[288,128]{1,0:T(8,128)(2,1)S(1)} %get-tuple-element.26), channel_id=1, source_target_pairs={{0,4},{4,8},{8,12},{12,16},{16,20},{20,24},{24,28},{28,0},{1,5},{5... | collective-permute-start | bytes 221192 | tf_op jit(solution)/shard_map/ppermute | solution.py:672
  5.9 8.0 %collective-permute-start.2 = (bf16[288,128]{1,0:T(8,128)(2,1)S(1)}, bf16[288,128]{1,0:T(8,128)(2,1)S(1)}, u32[]{:S(2)}, u32[]{:S(2)}) collective-permute-start(bf16[288,128]{1,0:T(8,128)(2,1)S(1)} %get-tuple-element.27), channel_id=1, source_target_pairs={{0,8},{4,12},{8,16},{12,20},{16,24},{20,28},{24,0},{28,4},{1,9},{5... | collective-permute-start | bytes 221192 | tf_op jit(solution)/shard_map/ppermute | solution.py:672
  7.5 10.9 %collective-permute-start.3 = (bf16[288,128]{1,0:T(8,128)(2,1)S(1)}, bf16[288,128]{1,0:T(8,128)(2,1)S(1)}, u32[]{:S(2)}, u32[]{:S(2)}) collective-permute-start(bf16[288,128]{1,0:T(8,128)(2,1)S(1)} %get-tuple-element.28), channel_id=1, source_target_pairs={{0,12},{4,16},{8,20},{12,24},{16,28},{20,0},{24,4},{28,8},{1,13},{... | collective-permute-start | bytes 221192 | tf_op jit(solution)/shard_map/ppermute | solution.py:672
  10.1 10.0 %collective-permute-start.4 = (bf16[288,128]{1,0:T(8,128)(2,1)S(1)}, bf16[288,128]{1,0:T(8,128)(2,1)S(1)}, u32[]{:S(2)}, u32[]{:S(2)}) collective-permute-start(bf16[288,128]{1,0:T(8,128)(2,1)S(1)} %get-tuple-element.29), channel_id=1, source_target_pairs={{0,16},{4,20},{8,24},{12,28},{16,0},{20,4},{24,8},{28,12},{1,17},{... | collective-permute-start | bytes 221192 | tf_op jit(solution)/shard_map/ppermute | solution.py:672
  12.1 9.1 %collective-permute-start.5 = (bf16[288,128]{1,0:T(8,128)(2,1)S(1)}, bf16[288,128]{1,0:T(8,128)(2,1)S(1)}, u32[]{:S(2)}, u32[]{:S(2)}) collective-permute-start(bf16[288,128]{1,0:T(8,128)(2,1)S(1)} %get-tuple-element.30), channel_id=1, source_target_pairs={{0,20},{4,24},{8,28},{12,0},{16,4},{20,8},{24,12},{28,16},{1,21},{... | collective-permute-start | bytes 221192 | tf_op jit(solution)/shard_map/ppermute | solution.py:672
  13.9 7.8 %collective-permute-start.6 = (bf16[288,128]{1,0:T(8,128)(2,1)S(1)}, bf16[288,128]{1,0:T(8,128)(2,1)S(1)}, u32[]{:S(2)}, u32[]{:S(2)}) collective-permute-start(bf16[288,128]{1,0:T(8,128)(2,1)S(1)} %get-tuple-element.31), channel_id=1, source_target_pairs={{0,24},{4,28},{8,0},{12,4},{16,8},{20,12},{24,16},{28,20},{1,25},{... | collective-permute-start | bytes 221192 | tf_op jit(solution)/shard_map/ppermute | solution.py:672
  18.4 4.4 %collective-permute-start.7 = (bf16[288,128]{1,0:T(8,128)(2,1)S(1)}, bf16[288,128]{1,0:T(8,128)(2,1)S(1)}, u32[]{:S(2)}, u32[]{:S(2)}) collective-permute-start(bf16[288,128]{1,0:T(8,128)(2,1)S(1)} %get-tuple-element.32), channel_id=1, source_target_pairs={{0,28},{4,0},{8,4},{12,8},{16,12},{20,16},{24,20},{28,24},{1,29},{... | collective-permute-start | bytes 221192 | tf_op jit(solution)/shard_map/ppermute | solution.py:672
  28.9 1.7 %collective-permute-start.8 = (bf16[272,640]{1,0:T(8,128)(2,1)S(1)}, bf16[272,640]{1,0:T(8,128)(2,1)S(1)}, u32[]{:S(2)}, u32[]{:S(2)}) collective-permute-start(bf16[272,640]{1,0:T(8,128)(2,1)S(1)} %get-tuple-element.33.h_own.h_first), channel_id=1, source_target_pairs={{0,1},{1,0},{2,3},{3,2},{4,5},{5,4},{6,7},{7,6},{8,9},{9,8},{10,11... | collective-permute-start | bytes 1044488 | tf_op jit(solution)/shard_map/ppermute | solution.py:733
  31.7 17.6 %collective-permute-start.12 = (bf16[256,1280]{1,0:T(8,128)(2,1)S(1)}, bf16[256,1280]{1,0:T(8,128)(2,1)S(1)}, u32[]{:S(2)}, u32[]{:S(2)}) collective-permute-start(bf16[256,1280]{1,0:T(8,128)(2,1)S(1)} %project.2.after), channel_id=1, source_target_pairs={{0,2},{1,3},{2,0},{3,1},{4,6},{5,7},{6,4},{7,5},{8,10},{9,11},{10,... | collective-permute-start | bytes 1966088 | tf_op jit(solution)/shard_map/ppermute | solution.py:735
  38.3 2.1 %collective-permute-start.9 = (bf16[256,640]{1,0:T(8,128)(2,1)S(1)}, bf16[256,640]{1,0:T(8,128)(2,1)S(1)}, u32[]{:S(2)}, u32[]{:S(2)}) collective-permute-start(bf16[256,640]{1,0:T(8,128)(2,1)S(1)} %attend_second.1.h_own.h_second), channel_id=1, source_target_pairs={{0,1},{1,0},{2,3},{3,2},{4,5},{5,4},{6,7},{7,6},{8,9},{9,8},{10,11... | collective-permute-start | bytes 983048 | tf_op jit(solution)/shard_map/ppermute | solution.py:733
  39.1 4.1 %collective-permute-start.10 = (bf16[4,4,1280]{2,1,0:T(4,128)(2,1)S(1)}, bf16[4,4,1280]{2,1,0:T(4,128)(2,1)S(1)}, u32[]{:S(2)}, u32[]{:S(2)}) collective-permute-start(bf16[4,4,1280]{2,1,0:T(4,128)(2,1)S(1)} %get-tuple-element.37), channel_id=1, source_target_pairs={{0,4},{4,0},{8,12},{12,8},{16,20},{20,16},{24,28},{28,24},{1,5},{5... | collective-permute-start | bytes 122888 | tf_op jit(solution)/shard_map/ppermute | solution.py:759
  43.2 4.1 %collective-permute-start.11 = (bf16[4,4,1280]{2,1,0:T(4,128)(2,1)S(1)}, bf16[4,4,1280]{2,1,0:T(4,128)(2,1)S(1)}, u32[]{:S(2)}, u32[]{:S(2)}) collective-permute-start(bf16[4,4,1280]{2,1,0:T(4,128)(2,1)S(1)} %pad_maximum_fusion), channel_id=1, source_target_pairs={{0,8},{4,12},{8,0},{12,4},{16,24},{20,28},{24,16},{28,20},{1,9},{5... | collective-permute-start | bytes 122888 | tf_op jit(solution)/shard_map/ppermute | solution.py:759
  45.1 18.4 %collective-permute-start.14 = (bf16[256,1280]{1,0:T(8,128)(2,1)S(1)}, bf16[256,1280]{1,0:T(8,128)(2,1)S(1)}, u32[]{:S(2)}, u32[]{:S(2)}) collective-permute-start(bf16[256,1280]{1,0:T(8,128)(2,1)S(1)} %project.3), channel_id=1, source_target_pairs={{0,2},{1,3},{2,0},{3,1},{4,6},{5,7},{6,4},{7,5},{8,10},{9,11},{10,... | collective-permute-start | bytes 1966088 | tf_op jit(solution)/shard_map/ppermute | solution.py:735
  49.4 5.3 %collective-permute-start.13 = (bf16[4,4,1280]{2,1,0:T(4,128)(2,1)S(1)}, bf16[4,4,1280]{2,1,0:T(4,128)(2,1)S(1)}, u32[]{:S(2)}, u32[]{:S(2)}) collective-permute-start(bf16[4,4,1280]{2,1,0:T(4,128)(2,1)S(1)} %pad_maximum_fusion.1), channel_id=1, source_target_pairs={{0,16},{4,20},{8,24},{12,28},{16,0},{20,4},{24,8},{28,12},{1,17},{... | collective-permute-start | bytes 122888 | tf_op jit(solution)/shard_map/ppermute | solution.py:759
  56.1 7.4 %collective-permute-start.15 = (bf16[16,1280]{1,0:T(8,128)(2,1)S(1)}, bf16[16,1280]{1,0:T(8,128)(2,1)S(1)}, u32[]{:S(2)}, u32[]{:S(2)}) collective-permute-start(bf16[16,1280]{1,0:T(8,128)(2,1)S(1)} %get-tuple-element.44), channel_id=1, source_target_pairs={{0,2},{1,3},{2,0},{3,1},{4,6},{5,7},{6,4},{7,5},{8,10},{9,11},{10,... | collective-permute-start | bytes 122888 | tf_op jit(solution)/shard_map/ppermute | solution.py:775

commit v6 on v5

--- a/solution.py
+++ b/solution.py
@@ -156,10 +156,12 @@
     return picked
 
 
-def spread_slot(weights, slot, slots):
-    return jnp.concatenate(
-        [jnp.where(slot == s, weights, 0.0).astype(jnp.bfloat16) for s in range(slots)], axis=1
-    )
+def ones_where(mask):
+    return mask.astype(jnp.float32).astype(jnp.bfloat16)
+
+
+def spread_slot(weights, masks):
+    return jnp.concatenate([weights * mask for mask in masks], axis=1)
 
 
 def row_values(slots_of, lengths, finished, fork, prompt_lengths, slots):
@@ -213,6 +215,8 @@
     prompt_mask = lane < meta[1]
     cache_mask = cache_lane < meta[2]
     alive_rows = meta[3].astype(jnp.float32)
+    masks = [ones_where(slot == s) for s in range(slots)]
+    halves = [ones_where(first_half), ones_where(jnp.logical_not(first_half))]
     q_all = jnp.concatenate([q[:, h * HEAD_DIM : (h + 1) * HEAD_DIM] for h in range(groups)], axis=0)
     prompt_all = matmul(q_all, pk[...], NT)
     new_all = matmul(q_all, nk[...], NT)
@@ -222,9 +226,10 @@
         wp, wn, wc = softmax_weights(
             prompt, new_all[part], cache_scores[h], prompt_mask, new_mask, cache_mask
         )
-        cache_weights[h, :, :half] = jnp.where(first_half, wc, 0.0).astype(jnp.bfloat16)
-        cache_weights[h, :, half:] = jnp.where(first_half, 0.0, wc).astype(jnp.bfloat16)
-        weights[part, : slots * prefix] = spread_slot(wp, slot, slots)
+        wc = wc.astype(jnp.bfloat16)
+        cache_weights[h, :, :half] = wc * halves[0]
+        cache_weights[h, :, half:] = wc * halves[1]
+        weights[part, : slots * prefix] = spread_slot(wp.astype(jnp.bfloat16), masks)
         weights[part, slots * prefix :] = wn.astype(jnp.bfloat16)
     mixed[...] = matmul(weights[:, : slots * prefix], pv[...], NN) + matmul(
         weights[:, slots * prefix :], nv[...], NN
@@ -262,7 +267,7 @@
     ).astype(jnp.bfloat16)
     wn = pltpu.roll(wn, steps, 1).astype(jnp.bfloat16)
     mixed = (
-        matmul(spread_slot(wp, slot, slots), pv[...], NN)
+        matmul(spread_slot(wp.astype(jnp.bfloat16), [ones_where(slot == s) for s in range(slots)]), pv[...], NN)
         + matmul(wn, x, NN)
         + matmul(wc, values[...], NN)
     )

time: 65.8 us -> 65.8 us (level)
  waiting for transfers between devices: 17.4 us -> 16.6 us
  starting transfers between devices: 21.7 us -> 22.4 us
    ppermute x7, waiting for transfers between devices: 6.76 us -> 5.95 us  [body(): lax.ppermute(block, 'replica', [(i, (i + k) % replicas) for i in range(re...]
    ppermute x7, starting transfers between devices: 12.6 us -> 13.5 us  [body(): lax.ppermute(block, 'replica', [(i, (i + k) % replicas) for i in range(re...]
where the time goes in v6:
time: 65.8 us; the launch traced here: 65.4 us
  Pallas kernels  25.9 us (39%)
  starting transfers between devices  22.4 us (34%)
  waiting for transfers between devices  16.6 us (25%)
    pallas_call x6, Pallas kernels, call(): pl.pallas_call(kernel, out_shape=[pltpu.VMEM(shape, kind) for shape, kind...  14.3 us
    ppermute x7, starting transfers between devices, body(): lax.ppermute(block, 'replica', [(i, (i + k) % replicas) for i in range(re...  13.5 us
    ppermute x3, waiting for transfers between devices, body(): lax.ppermute(x, 'replica', [(i, i ^ bit) for i in range(replicas)])  6.99 us
    pallas_call x1, Pallas kernels, body(): pl.pallas_call(functools.partial(first_kernel, stacked=stacked, replicas=...  6.09 us
    ppermute x7, waiting for transfers between devices, body(): lax.ppermute(block, 'replica', [(i, (i + k) % replicas) for i in range(re...  5.95 us
    ppermute x3, starting transfers between devices, body(): lax.ppermute(x, 'replica', [(i, i ^ bit) for i in range(replicas)])  4.71 us
    pallas_call x1, Pallas kernels, exchange_pack(): pl.pallas_call(functools.partial(pack_kernel, replicas=replicas, moved=mo...  2.9 us
    ppermute x2, starting transfers between devices, cross(): return (sib, crossed, lax.ppermute(crossed, 'tensor', across))  2.16 us
  transfers between devices with their start and end apart: 16, of which 10 were waited for; matrix products, arithmetic and copies ran while one was open for 0% of the time, Pallas kernels for 26%

profile of v6, /device:TPU:0, one launch (start us, length us, event | category | flops | bytes accessed | tf_op | source)
XLA Modules:
  0.0 65.4 jit_solution(8135160106306155802)
XLA Ops:
  0.5 2.9 %pack.1 = (bf16[288,128]{1,0:T(8,128)(2,1)S(1)}, bf16[288,128]{1,0:T(8,128)(2,1)S(1)}, bf16[288,128]{1,0:T(8,128)(2,1)S(1)}, bf16[288,128]{1,0:T(8,128)(2,1)S(1)...) custom-call(s32[4,8]{1,0:T(4,128)} %bitcast.16, ...), custom_call_target="tpu_custom_call" | custom-call | tf_op jit(solution)/shard_map/pack/pallas_call | solution.py:586
  3.4 2.6 %collective-permute-start.1 = (bf16[288,128]{1,0:T(8,128)(2,1)S(1)}, bf16[288,128]{1,0:T(8,128)(2,1)S(1)}, u32[]{:S(2)}, u32[]{:S(2)}) collective-permute-start(bf16[288,128]{1,0:T(8,128)(2,1)S(1)} %get-tuple-element.26), channel_id=1, source_target_pairs={{0,4},{4,8},{8,12},{12,16},{16,20},{20,24},{24,28},{28,0},{1,5},{5... | collective-permute-start | bytes 221192 | tf_op jit(solution)/shard_map/ppermute | solution.py:677
  5.9 1.6 %collective-permute-start.2 = (bf16[288,128]{1,0:T(8,128)(2,1)S(1)}, bf16[288,128]{1,0:T(8,128)(2,1)S(1)}, u32[]{:S(2)}, u32[]{:S(2)}) collective-permute-start(bf16[288,128]{1,0:T(8,128)(2,1)S(1)} %get-tuple-element.27), channel_id=1, source_target_pairs={{0,8},{4,12},{8,16},{12,20},{16,24},{20,28},{24,0},{28,4},{1,9},{5... | collective-permute-start | bytes 221192 | tf_op jit(solution)/shard_map/ppermute | solution.py:677
  7.5 2.5 %collective-permute-start.3 = (bf16[288,128]{1,0:T(8,128)(2,1)S(1)}, bf16[288,128]{1,0:T(8,128)(2,1)S(1)}, u32[]{:S(2)}, u32[]{:S(2)}) collective-permute-start(bf16[288,128]{1,0:T(8,128)(2,1)S(1)} %get-tuple-element.28), channel_id=1, source_target_pairs={{0,12},{4,16},{8,20},{12,24},{16,28},{20,0},{24,4},{28,8},{1,13},{... | collective-permute-start | bytes 221192 | tf_op jit(solution)/shard_map/ppermute | solution.py:677
  10.0 1.2 %collective-permute-start.4 = (bf16[288,128]{1,0:T(8,128)(2,1)S(1)}, bf16[288,128]{1,0:T(8,128)(2,1)S(1)}, u32[]{:S(2)}, u32[]{:S(2)}) collective-permute-start(bf16[288,128]{1,0:T(8,128)(2,1)S(1)} %get-tuple-element.29), channel_id=1, source_target_pairs={{0,16},{4,20},{8,24},{12,28},{16,0},{20,4},{24,8},{28,12},{1,17},{... | collective-permute-start | bytes 221192 | tf_op jit(solution)/shard_map/ppermute | solution.py:677
  11.3 0.8 %collective-permute-done.1.rest_0_ = bf16[288,128]{1,0:T(8,128)(2,1)S(1)} collective-permute-done((bf16[288,128]{1,0:T(8,128)(2,1)S(1)}, bf16[288,128]{1,0:T(8,128)(2,1)S(1)}, u32[]{:S(2)}, u32[]{:S(2)}) %collective-permute-start.1) | collective-permute-done | bytes 73760 | tf_op jit(solution)/shard_map/ppermute | solution.py:677
  12.1 1.8 %collective-permute-start.5 = (bf16[288,128]{1,0:T(8,128)(2,1)S(1)}, bf16[288,128]{1,0:T(8,128)(2,1)S(1)}, u32[]{:S(2)}, u32[]{:S(2)}) collective-permute-start(bf16[288,128]{1,0:T(8,128)(2,1)S(1)} %get-tuple-element.30), channel_id=1, source_target_pairs={{0,20},{4,24},{8,28},{12,0},{16,4},{20,8},{24,12},{28,16},{1,21},{... | collective-permute-start | bytes 221192 | tf_op jit(solution)/shard_map/ppermute | solution.py:677
  13.9 1.4 %collective-permute-start.6 = (bf16[288,128]{1,0:T(8,128)(2,1)S(1)}, bf16[288,128]{1,0:T(8,128)(2,1)S(1)}, u32[]{:S(2)}, u32[]{:S(2)}) collective-permute-start(bf16[288,128]{1,0:T(8,128)(2,1)S(1)} %get-tuple-element.31), channel_id=1, source_target_pairs={{0,24},{4,28},{8,0},{12,4},{16,8},{20,12},{24,16},{28,20},{1,25},{... | collective-permute-start | bytes 221192 | tf_op jit(solution)/shard_map/ppermute | solution.py:677
  15.3 3.1 %collective-permute-done.3.rest_2_ = bf16[288,128]{1,0:T(8,128)(2,1)S(1)} collective-permute-done((bf16[288,128]{1,0:T(8,128)(2,1)S(1)}, bf16[288,128]{1,0:T(8,128)(2,1)S(1)}, u32[]{:S(2)}, u32[]{:S(2)}) %collective-permute-start.3) | collective-permute-done | bytes 73760 | tf_op jit(solution)/shard_map/ppermute | solution.py:677
  18.4 2.4 %collective-permute-start.7 = (bf16[288,128]{1,0:T(8,128)(2,1)S(1)}, bf16[288,128]{1,0:T(8,128)(2,1)S(1)}, u32[]{:S(2)}, u32[]{:S(2)}) collective-permute-start(bf16[288,128]{1,0:T(8,128)(2,1)S(1)} %get-tuple-element.32), channel_id=1, source_target_pairs={{0,28},{4,0},{8,4},{12,8},{16,12},{20,16},{24,20},{28,24},{1,29},{... | collective-permute-start | bytes 221192 | tf_op jit(solution)/shard_map/ppermute | solution.py:677
  21.2 0.5 collective-permute-done.6.rest_5_
  21.7 1.0 %collective-permute-done.7.rest_6_ = bf16[288,128]{1,0:T(8,128)(2,1)S(1)} collective-permute-done((bf16[288,128]{1,0:T(8,128)(2,1)S(1)}, bf16[288,128]{1,0:T(8,128)(2,1)S(1)}, u32[]{:S(2)}, u32[]{:S(2)}) %collective-permute-start.7) | collective-permute-done | bytes 73760 | tf_op jit(solution)/shard_map/ppermute | solution.py:677
  22.8 6.1 %attend_first.1 = (bf16[272,640]{1,0:T(8,128)(2,1)S(1)}, bf16[512,128]{1,0:T(8,128)(2,1)S(1)}, bf16[512,128]{1,0:T(8,128)(2,1)S(1)}, bf16[1280,1280]{1,0:T(8,128)(2,1)S(1)}) custom-call(s32[4,8]{1,0:T(4,128)} %bitcast.17, s32[18]{0:T(128)} %copy-done, s32[32]{0:T(128)} %prompt_lengths.3, s32[8,128]{1,0:T(8,128)} %bitcast.19, s32[8,128]{1,0:T(8,128)} %bitcast.21, ...), custom_call_target="tpu_custom_call" | custom-call | flops 1 | bytes 1 | tf_op jit(solution)/shard_map/attend_first/pallas_call | solution.py:707
  29.0 1.6 %collective-permute-done.8.h_sib.s_first = bf16[272,640]{1,0:T(8,128)(2,1)S(1)} collective-permute-done((bf16[272,640]{1,0:T(8,128)(2,1)S(1)}, bf16[272,640]{1,0:T(8,128)(2,1)S(1)}, u32[]{:S(2)}, u32[]{:S(2)}) %collective-permute-start.8) | collective-permute-done | bytes 348192 | tf_op jit(solution)/shard_map/ppermute | solution.py:738
  30.6 1.0 %project.2.after = bf16[256,1280]{1,0:T(8,128)(2,1)S(1)} custom-call(bf16[272,640]{1,0:T(8,128)(2,1)S(1)} %get-tuple-element.33.h_own.h_first, bf16[272,640]{1,0:T(8,128)(2,1)S(1)} %collective-permute-done.8.h_sib.s_first, bf16[1280,1280]{1,0:T(8,128)(2,1)S(1)} %get-tuple-element.36.weights.w_there), custom_call_target="tpu_custom_call" | custom-call | flops 1 | bytes 1 | tf_op jit(solution)/shard_map/project/pallas_call | solution.py:726
  31.6 1.6 %collective-permute-start.12 = (bf16[256,1280]{1,0:T(8,128)(2,1)S(1)}, bf16[256,1280]{1,0:T(8,128)(2,1)S(1)}, u32[]{:S(2)}, u32[]{:S(2)}) collective-permute-start(bf16[256,1280]{1,0:T(8,128)(2,1)S(1)} %project.2.after), channel_id=1, source_target_pairs={{0,2},{1,3},{2,0},{3,1},{4,6},{5,7},{6,4},{7,5},{8,10},{9,11},{10,... | collective-permute-start | bytes 1966088 | tf_op jit(solution)/shard_map/ppermute | solution.py:740
  33.2 5.1 %attend_second.1.h_own.h_second = bf16[256,640]{1,0:T(8,128)(2,1)S(1)} custom-call(s32[4,8]{1,0:T(4,128)} %bitcast.18, s32[32]{0:T(128)} %prompt_lengths.3, s32[8,128]{1,0:T(8,128)} %bitcast.20, s32[8,128]{1,0:T(8,128)} %bitcast.22, s32[8,128]{1,0:T(8,128)} %bitcast.24, bf16[512,128]{1,0:T(8,128)(2,1)S(1)} %get-tuple-element.34.pk, ...), custom_call_target="tpu_custom_call" | custom-call | flops 1 | bytes 1 | tf_op jit(solution)/shard_map/attend_second/pallas_call | solution.py:726
  38.3 0.7 %moved_send.1 = (bf16[4,4,1280]{2,1,0:T(4,128)(2,1)S(1)}, bf16[4,4,1280]{2,1,0:T(4,128)(2,1)S(1)}) custom-call(s32[18]{0:T(128)} %copy-done, bf16[272,640]{1,0:T(8,128)(2,1)S(1)} %get-tuple-element.33.h_own.h_first, bf16[272,640]{1,0:T(8,128)(2,1)S(1)} %collective-permute-done.8.h_sib.s_first, bf16[256,1280]{1,0:T(8,128)(2,1)S(1)} %project.2.after), custom_call_target="tpu_custom_call" | custom-call | flops 1 | bytes 1 | tf_op jit(solution)/shard_map/moved_send/pallas_call | solution.py:726
  39.1 1.3 %collective-permute-start.10 = (bf16[4,4,1280]{2,1,0:T(4,128)(2,1)S(1)}, bf16[4,4,1280]{2,1,0:T(4,128)(2,1)S(1)}, u32[]{:S(2)}, u32[]{:S(2)}) collective-permute-start(bf16[4,4,1280]{2,1,0:T(4,128)(2,1)S(1)} %get-tuple-element.37), channel_id=1, source_target_pairs={{0,4},{4,0},{8,12},{12,8},{16,20},{20,16},{24,28},{28,24},{1,5},{5... | collective-permute-start | bytes 122888 | tf_op jit(solution)/shard_map/ppermute | solution.py:764
  40.4 1.0 %project.3 = bf16[256,1280]{1,0:T(8,128)(2,1)S(1)} custom-call(bf16[256,640]{1,0:T(8,128)(2,1)S(1)} %attend_second.1.h_own.h_second, bf16[256,640]{1,0:T(8,128)(2,1)S(1)} %collective-permute-done.9.h_sib.s_second, bf16[1280,1280]{1,0:T(8,128)(2,1)S(1)} %get-tuple-element.36.weights.w_there), custom_call_target="tpu_custom_call" | custom-call | flops 1 | bytes 1 | tf_op jit(solution)/shard_map/project/pallas_call | solution.py:726
  41.4 1.7 %collective-permute-done.10.rest_0_ = bf16[4,4,1280]{2,1,0:T(4,128)(2,1)S(1)} collective-permute-done((bf16[4,4,1280]{2,1,0:T(4,128)(2,1)S(1)}, bf16[4,4,1280]{2,1,0:T(4,128)(2,1)S(1)}, u32[]{:S(2)}, u32[]{:S(2)}) %collective-permute-start.10) | collective-permute-done | bytes 40992 | tf_op jit(solution)/shard_map/ppermute | solution.py:764
  43.2 1.9 %collective-permute-start.11 = (bf16[4,4,1280]{2,1,0:T(4,128)(2,1)S(1)}, bf16[4,4,1280]{2,1,0:T(4,128)(2,1)S(1)}, u32[]{:S(2)}, u32[]{:S(2)}) collective-permute-start(bf16[4,4,1280]{2,1,0:T(4,128)(2,1)S(1)} %pad_maximum_fusion), channel_id=1, source_target_pairs={{0,8},{4,12},{8,0},{12,4},{16,24},{20,28},{24,16},{28,20},{1,9},{5... | collective-permute-start | bytes 122888 | tf_op jit(solution)/shard_map/ppermute | solution.py:764
  45.1 0.6 collective-permute-start.14
  45.7 1.6 %collective-permute-done.11.rest_1_ = bf16[4,4,1280]{2,1,0:T(4,128)(2,1)S(1)} collective-permute-done((bf16[4,4,1280]{2,1,0:T(4,128)(2,1)S(1)}, bf16[4,4,1280]{2,1,0:T(4,128)(2,1)S(1)}, u32[]{:S(2)}, u32[]{:S(2)}) %collective-permute-start.11) | collective-permute-done | bytes 40992 | tf_op jit(solution)/shard_map/ppermute | solution.py:764
  47.3 2.0 %collective-permute-done.12.recv = bf16[256,1280]{1,0:T(8,128)(2,1)S(1)} collective-permute-done((bf16[256,1280]{1,0:T(8,128)(2,1)S(1)}, bf16[256,1280]{1,0:T(8,128)(2,1)S(1)}, u32[]{:S(2)}, u32[]{:S(2)}) %collective-permute-start.12) | collective-permute-done | bytes 655392 | tf_op jit(solution)/shard_map/ppermute | solution.py:740
  49.3 1.6 %collective-permute-start.13 = (bf16[4,4,1280]{2,1,0:T(4,128)(2,1)S(1)}, bf16[4,4,1280]{2,1,0:T(4,128)(2,1)S(1)}, u32[]{:S(2)}, u32[]{:S(2)}) collective-permute-start(bf16[4,4,1280]{2,1,0:T(4,128)(2,1)S(1)} %pad_maximum_fusion.1), channel_id=1, source_target_pairs={{0,16},{4,20},{8,24},{12,28},{16,0},{20,4},{24,8},{28,12},{1,17},{... | collective-permute-start | bytes 122888 | tf_op jit(solution)/shard_map/ppermute | solution.py:764
  50.9 3.7 %collective-permute-done.13.rest_2_ = bf16[4,4,1280]{2,1,0:T(4,128)(2,1)S(1)} collective-permute-done((bf16[4,4,1280]{2,1,0:T(4,128)(2,1)S(1)}, bf16[4,4,1280]{2,1,0:T(4,128)(2,1)S(1)}, u32[]{:S(2)}, u32[]{:S(2)}) %collective-permute-start.13) | collective-permute-done | bytes 40992 | tf_op jit(solution)/shard_map/ppermute | solution.py:764
  54.6 1.5 %moved_project.1 = (bf16[16,1280]{1,0:T(8,128)(2,1)S(1)}, bf16[16,1280]{1,0:T(8,128)(2,1)S(1)}) custom-call(s32[18]{0:T(128)} %copy-done, bf16[1280,1280]{1,0:T(8,128)(2,1)S(1)} %get-tuple-element.36.weights.w_there, bf16[4,4,1280]{2,1,0:T(4,128)(2,1)S(1)} %collective-permute-done.10.rest_0_, bf16[4,4,1280]{2,1,0:T(4,128)(2,1)S(1)} %collective-permute-done.11.rest_1_, ...), custom_call_target="tpu_custom_call" | custom-call | flops 1 | bytes 1 | tf_op jit(solution)/shard_map/moved_project/pallas_call | solution.py:726
  56.1 1.5 %collective-permute-start.15 = (bf16[16,1280]{1,0:T(8,128)(2,1)S(1)}, bf16[16,1280]{1,0:T(8,128)(2,1)S(1)}, u32[]{:S(2)}, u32[]{:S(2)}) collective-permute-start(bf16[16,1280]{1,0:T(8,128)(2,1)S(1)} %get-tuple-element.44), channel_id=1, source_target_pairs={{0,2},{1,3},{2,0},{3,1},{4,6},{5,7},{6,4},{7,5},{8,10},{9,11},{10,... | collective-permute-start | bytes 122888 | tf_op jit(solution)/shard_map/ppermute | solution.py:780
  57.6 4.9 %base.1 = (f32[512,1280]{1,0:T(8,128)S(1)}, f32[16,1280]{1,0:T(8,128)S(1)}) custom-call(s32[18]{0:T(128)} %copy-done, bf16[272,640]{1,0:T(8,128)(2,1)S(1)} %get-tuple-element.33.h_own.h_first, bf16[272,640]{1,0:T(8,128)(2,1)S(1)} %collective-permute-done.8.h_sib.s_first, bf16[256,640]{1,0:T(8,128)(2,1)S(1)} %attend_second.1.h_own.h_second, ...), custom_call_target="tpu_custom_call" | custom-call | flops 1 | bytes 1 | tf_op jit(solution)/shard_map/base/pallas_call | solution.py:726
  62.6 0.9 %finish_first.1.earlier = bf16[128,4,1280]{2,1,0:T(4,128)(2,1)} custom-call(f32[512,1280]{1,0:T(8,128)S(1)} %get-tuple-element.42.base, bf16[256,1280]{1,0:T(8,128)(2,1)S(1)} %collective-permute-done.12.recv), custom_call_target="tpu_custom_call" | custom-call | tf_op jit(solution)/shard_map/finish_first/pallas_call | solution.py:791
  63.5 1.7 %finish_second.1 = bf16[128,4,1280]{2,1,0:T(4,128)(2,1)} custom-call(s32[18]{0:T(128)} %copy-done, f32[512,1280]{1,0:T(8,128)S(1)} %get-tuple-element.42.base, bf16[256,1280]{1,0:T(8,128)(2,1)S(1)} %collective-permute-done.14.recv, f32[16,1280]{1,0:T(8,128)S(1)} %get-tuple-element.43.base_moved, ...), custom_call_target="tpu_custom_call", output_to_operand_aliasing={{}: (5, {})} | custom-call | tf_op jit(solution)/shard_map/finish_second/pallas_call | solution.py:800
  (19 shorter events, 1.1 us)
Async XLA Ops:
  0.0 22.8 %collective-permute-start = (bf16[640,5120]{1,0:T(8,128)(2,1)}, bf16[640,5120]{1,0:T(8,128)(2,1)S(1)}, u32[]{:S(2)}, u32[]{:S(2)}) collective-permute-start(bf16[640,5120]{1,0:T(8,128)(2,1)} %w_own.3), channel_id=1, source_target_pairs={{0,1},{1,0},{2,3},{3,2},{4,5},{5,4},{6,7},{7,6},{8,9},{9,8},{10,11... | collective-permute-start | bytes 19660808 | tf_op jit(solution)/shard_map/ppermute | solution.py:662
  3.4 19.4 %copy-start = (s32[18]{0:T(128)}, s32[18]{0:T(128)S(1)}, u32[]{:S(2)}) copy-start(s32[18]{0:T(128)S(1)} %get-tuple-element.25.pairs) | copy-start | bytes 220
  3.4 8.7 %collective-permute-start.1 = (bf16[288,128]{1,0:T(8,128)(2,1)S(1)}, bf16[288,128]{1,0:T(8,128)(2,1)S(1)}, u32[]{:S(2)}, u32[]{:S(2)}) collective-permute-start(bf16[288,128]{1,0:T(8,128)(2,1)S(1)} %get-tuple-element.26), channel_id=1, source_target_pairs={{0,4},{4,8},{8,12},{12,16},{16,20},{20,24},{24,28},{28,0},{1,5},{5... | collective-permute-start | bytes 221192 | tf_op jit(solution)/shard_map/ppermute | solution.py:677
  5.9 8.0 %collective-permute-start.2 = (bf16[288,128]{1,0:T(8,128)(2,1)S(1)}, bf16[288,128]{1,0:T(8,128)(2,1)S(1)}, u32[]{:S(2)}, u32[]{:S(2)}) collective-permute-start(bf16[288,128]{1,0:T(8,128)(2,1)S(1)} %get-tuple-element.27), channel_id=1, source_target_pairs={{0,8},{4,12},{8,16},{12,20},{16,24},{20,28},{24,0},{28,4},{1,9},{5... | collective-permute-start | bytes 221192 | tf_op jit(solution)/shard_map/ppermute | solution.py:677
  7.5 10.9 %collective-permute-start.3 = (bf16[288,128]{1,0:T(8,128)(2,1)S(1)}, bf16[288,128]{1,0:T(8,128)(2,1)S(1)}, u32[]{:S(2)}, u32[]{:S(2)}) collective-permute-start(bf16[288,128]{1,0:T(8,128)(2,1)S(1)} %get-tuple-element.28), channel_id=1, source_target_pairs={{0,12},{4,16},{8,20},{12,24},{16,28},{20,0},{24,4},{28,8},{1,13},{... | collective-permute-start | bytes 221192 | tf_op jit(solution)/shard_map/ppermute | solution.py:677
  10.0 10.7 %collective-permute-start.4 = (bf16[288,128]{1,0:T(8,128)(2,1)S(1)}, bf16[288,128]{1,0:T(8,128)(2,1)S(1)}, u32[]{:S(2)}, u32[]{:S(2)}) collective-permute-start(bf16[288,128]{1,0:T(8,128)(2,1)S(1)} %get-tuple-element.29), channel_id=1, source_target_pairs={{0,16},{4,20},{8,24},{12,28},{16,0},{20,4},{24,8},{28,12},{1,17},{... | collective-permute-start | bytes 221192 | tf_op jit(solution)/shard_map/ppermute | solution.py:677
  12.1 9.1 %collective-permute-start.5 = (bf16[288,128]{1,0:T(8,128)(2,1)S(1)}, bf16[288,128]{1,0:T(8,128)(2,1)S(1)}, u32[]{:S(2)}, u32[]{:S(2)}) collective-permute-start(bf16[288,128]{1,0:T(8,128)(2,1)S(1)} %get-tuple-element.30), channel_id=1, source_target_pairs={{0,20},{4,24},{8,28},{12,0},{16,4},{20,8},{24,12},{28,16},{1,21},{... | collective-permute-start | bytes 221192 | tf_op jit(solution)/shard_map/ppermute | solution.py:677
  13.9 7.8 %collective-permute-start.6 = (bf16[288,128]{1,0:T(8,128)(2,1)S(1)}, bf16[288,128]{1,0:T(8,128)(2,1)S(1)}, u32[]{:S(2)}, u32[]{:S(2)}) collective-permute-start(bf16[288,128]{1,0:T(8,128)(2,1)S(1)} %get-tuple-element.31), channel_id=1, source_target_pairs={{0,24},{4,28},{8,0},{12,4},{16,8},{20,12},{24,16},{28,20},{1,25},{... | collective-permute-start | bytes 221192 | tf_op jit(solution)/shard_map/ppermute | solution.py:677
  18.4 4.4 %collective-permute-start.7 = (bf16[288,128]{1,0:T(8,128)(2,1)S(1)}, bf16[288,128]{1,0:T(8,128)(2,1)S(1)}, u32[]{:S(2)}, u32[]{:S(2)}) collective-permute-start(bf16[288,128]{1,0:T(8,128)(2,1)S(1)} %get-tuple-element.32), channel_id=1, source_target_pairs={{0,28},{4,0},{8,4},{12,8},{16,12},{20,16},{24,20},{28,24},{1,29},{... | collective-permute-start | bytes 221192 | tf_op jit(solution)/shard_map/ppermute | solution.py:677
  28.9 1.7 %collective-permute-start.8 = (bf16[272,640]{1,0:T(8,128)(2,1)S(1)}, bf16[272,640]{1,0:T(8,128)(2,1)S(1)}, u32[]{:S(2)}, u32[]{:S(2)}) collective-permute-start(bf16[272,640]{1,0:T(8,128)(2,1)S(1)} %get-tuple-element.33.h_own.h_first), channel_id=1, source_target_pairs={{0,1},{1,0},{2,3},{3,2},{4,5},{5,4},{6,7},{7,6},{8,9},{9,8},{10,11... | collective-permute-start | bytes 1044488 | tf_op jit(solution)/shard_map/ppermute | solution.py:738
  31.6 17.6 %collective-permute-start.12 = (bf16[256,1280]{1,0:T(8,128)(2,1)S(1)}, bf16[256,1280]{1,0:T(8,128)(2,1)S(1)}, u32[]{:S(2)}, u32[]{:S(2)}) collective-permute-start(bf16[256,1280]{1,0:T(8,128)(2,1)S(1)} %project.2.after), channel_id=1, source_target_pairs={{0,2},{1,3},{2,0},{3,1},{4,6},{5,7},{6,4},{7,5},{8,10},{9,11},{10,... | collective-permute-start | bytes 1966088 | tf_op jit(solution)/shard_map/ppermute | solution.py:740
  38.2 2.1 %collective-permute-start.9 = (bf16[256,640]{1,0:T(8,128)(2,1)S(1)}, bf16[256,640]{1,0:T(8,128)(2,1)S(1)}, u32[]{:S(2)}, u32[]{:S(2)}) collective-permute-start(bf16[256,640]{1,0:T(8,128)(2,1)S(1)} %attend_second.1.h_own.h_second), channel_id=1, source_target_pairs={{0,1},{1,0},{2,3},{3,2},{4,5},{5,4},{6,7},{7,6},{8,9},{9,8},{10,11... | collective-permute-start | bytes 983048 | tf_op jit(solution)/shard_map/ppermute | solution.py:738
  39.1 4.1 %collective-permute-start.10 = (bf16[4,4,1280]{2,1,0:T(4,128)(2,1)S(1)}, bf16[4,4,1280]{2,1,0:T(4,128)(2,1)S(1)}, u32[]{:S(2)}, u32[]{:S(2)}) collective-permute-start(bf16[4,4,1280]{2,1,0:T(4,128)(2,1)S(1)} %get-tuple-element.37), channel_id=1, source_target_pairs={{0,4},{4,0},{8,12},{12,8},{16,20},{20,16},{24,28},{28,24},{1,5},{5... | collective-permute-start | bytes 122888 | tf_op jit(solution)/shard_map/ppermute | solution.py:764
  43.2 4.1 %collective-permute-start.11 = (bf16[4,4,1280]{2,1,0:T(4,128)(2,1)S(1)}, bf16[4,4,1280]{2,1,0:T(4,128)(2,1)S(1)}, u32[]{:S(2)}, u32[]{:S(2)}) collective-permute-start(bf16[4,4,1280]{2,1,0:T(4,128)(2,1)S(1)} %pad_maximum_fusion), channel_id=1, source_target_pairs={{0,8},{4,12},{8,0},{12,4},{16,24},{20,28},{24,16},{28,20},{1,9},{5... | collective-permute-start | bytes 122888 | tf_op jit(solution)/shard_map/ppermute | solution.py:764
  45.1 18.4 %collective-permute-start.14 = (bf16[256,1280]{1,0:T(8,128)(2,1)S(1)}, bf16[256,1280]{1,0:T(8,128)(2,1)S(1)}, u32[]{:S(2)}, u32[]{:S(2)}) collective-permute-start(bf16[256,1280]{1,0:T(8,128)(2,1)S(1)} %project.3), channel_id=1, source_target_pairs={{0,2},{1,3},{2,0},{3,1},{4,6},{5,7},{6,4},{7,5},{8,10},{9,11},{10,... | collective-permute-start | bytes 1966088 | tf_op jit(solution)/shard_map/ppermute | solution.py:740
  49.3 5.3 %collective-permute-start.13 = (bf16[4,4,1280]{2,1,0:T(4,128)(2,1)S(1)}, bf16[4,4,1280]{2,1,0:T(4,128)(2,1)S(1)}, u32[]{:S(2)}, u32[]{:S(2)}) collective-permute-start(bf16[4,4,1280]{2,1,0:T(4,128)(2,1)S(1)} %pad_maximum_fusion.1), channel_id=1, source_target_pairs={{0,16},{4,20},{8,24},{12,28},{16,0},{20,4},{24,8},{28,12},{1,17},{... | collective-permute-start | bytes 122888 | tf_op jit(solution)/shard_map/ppermute | solution.py:764
  56.1 7.4 %collective-permute-start.15 = (bf16[16,1280]{1,0:T(8,128)(2,1)S(1)}, bf16[16,1280]{1,0:T(8,128)(2,1)S(1)}, u32[]{:S(2)}, u32[]{:S(2)}) collective-permute-start(bf16[16,1280]{1,0:T(8,128)(2,1)S(1)} %get-tuple-element.44), channel_id=1, source_target_pairs={{0,2},{1,3},{2,0},{3,1},{4,6},{5,7},{6,4},{7,5},{8,10},{9,11},{10,... | collective-permute-start | bytes 122888 | tf_op jit(solution)/shard_map/ppermute | solution.py:780

commit v7 on v5

--- a/solution.py
+++ b/solution.py
@@ -440,7 +440,7 @@
 
 
 def base_kernel(
-    pairs, h_first, s_first, h_second, s_second, h_moved, w_own, w_sib, residual, out, moved_out, weights, before, sems
+    pairs, h_first, s_first, h_second, s_second, w_own, w_sib, residual, out, weights, moved_out, before, sems
 ):
     rows, model = out.shape
     width = w_own.shape[0]
@@ -455,10 +455,8 @@
         sems,
     )
     ready()
-    moved_total = matmul(h_moved[...], weights[...], NN)
-    for i in range(h_moved.shape[0] // steps):
-        part = slice(i * steps, (i + 1) * steps)
-        moved_out[part, :] = moved_total[part] + before[pairs[i]].astype(jnp.float32)
+    for i in range(moved_out.shape[0] // steps):
+        moved_out[i * steps : (i + 1) * steps, :] = before[pairs[i]].astype(jnp.float32)
     low = 0
     for h_own, h_sib, size in ((h_first, s_first, rows - h_second.shape[0]), (h_second, s_second, h_second.shape[0])):
         part = pl.ds(0, size)
@@ -491,8 +489,8 @@
             outs[0][peer] = value
 
 
-def moved_project_kernel(pairs, w_there, *rest, moved, steps, split):
-    backs, (cross, both_out, heads) = rest[:-3], rest[-3:]
+def moved_project_kernel(pairs, w_here, w_there, before, *rest, moved, steps, split):
+    backs, (cross, base, heads) = rest[:-3], rest[-3:]
     me = lax.axis_index("replica")
     for i in range(moved):
         peer = pairs[moved + 1 + i]
@@ -509,8 +507,8 @@
         else:
             heads[part, :] = backs[0][peer].astype(jnp.float32)
     both = heads[...].astype(cross.dtype)
-    both_out[...] = both
     cross[...] = matmul(both, w_there[...], NN).astype(cross.dtype)
+    base[...] = matmul(both, w_here[...], NN) + before[...]
 
 
 def add_rows(total, out, first, steps):
@@ -764,23 +762,23 @@
         two, *_ = lax.optimization_barrier((two, got_first))
         four = flip(jnp.concatenate([kept[1:2], one[1:2], two[1:2], two[3:4]]), 4)
         backs = [one, two, four]
-    crossed_moved, home_heads = call(
+    base, w_here, before = call(
+        base_kernel,
+        "base",
+        [((n, model), jnp.float32), ((2 * width, model), dtype), ((m, model), jnp.float32)],
+        [SMEM] + [VMEM] * 4 + [ANY] * 3,
+        (*in_hbm(pairs), h_first, s_first, h_second, s_second, *in_hbm(out_proj), w_sib, *in_hbm(residual)),
+        [pltpu.VMEM(residual.shape, dtype), dma(3)],
+    )
+    crossed_moved, base_moved = call(
         functools.partial(moved_project_kernel, **options),
         "moved_project",
-        [((m, model), dtype), ((m, 2 * width), dtype)],
-        [SMEM] + [VMEM] * (1 + len(backs)),
-        (*in_hbm(pairs), w_there, *backs),
+        [((m, model), dtype), ((m, model), jnp.float32)],
+        [SMEM] + [VMEM] * (3 + len(backs)),
+        (*in_hbm(pairs), w_here, w_there, before, *backs),
         [pltpu.VMEM((m, 2 * width), jnp.float32)],
     )
     got_moved = lax.ppermute(crossed_moved, "tensor", across)
-    base, base_moved = call(
-        base_kernel,
-        "base",
-        [((n, model), jnp.float32), ((m, model), jnp.float32)],
-        [SMEM] + [VMEM] * 5 + [ANY] * 3,
-        (*in_hbm(pairs), h_first, s_first, h_second, s_second, home_heads, *in_hbm(out_proj), w_sib, *in_hbm(residual)),
-        [pltpu.VMEM((2 * width, model), dtype), pltpu.VMEM(residual.shape, dtype), dma(3)],
-    )
 
     whole = jax.ShapeDtypeStruct(residual.shape, residual.dtype)
     out = pl.pallas_call(

time: 65.8 us -> 65.5 us (level)
    ppermute x1, waiting for transfers between devices: 0.01 us -> 4.6 us  [body(): got_moved = lax.ppermute(crossed_moved, 'tensor', across)]
    ppermute x3, waiting for transfers between devices: 6.96 us -> 3.27 us  [body(): lax.ppermute(x, 'replica', [(i, i ^ bit) for i in range(replicas)])]
    ppermute x1, starting transfers between devices: 1.51 us -> 0.6 us  [body(): got_moved = lax.ppermute(crossed_moved, 'tensor', across)]
    ppermute x7, waiting for transfers between devices: 6.76 us -> 5.93 us  [body(): lax.ppermute(block, 'replica', [(i, (i + k) % replicas) for i in range(re...]
    ppermute x7, starting transfers between devices: 12.6 us -> 13.5 us  [body(): lax.ppermute(block, 'replica', [(i, (i + k) % replicas) for i in range(re...]
where the time goes in v7:
time: 65.5 us; the launch traced here: 65.1 us
  Pallas kernels  25.8 us (39%)
  starting transfers between devices  21.5 us (33%)
  waiting for transfers between devices  17.5 us (27%)
    pallas_call x6, Pallas kernels, call(): pl.pallas_call(kernel, out_shape=[pltpu.VMEM(shape, kind) for shape, kind...  14.2 us
    ppermute x7, starting transfers between devices, body(): lax.ppermute(block, 'replica', [(i, (i + k) % replicas) for i in range(re...  13.5 us
    pallas_call x1, Pallas kernels, body(): pl.pallas_call(functools.partial(first_kernel, stacked=stacked, replicas=...  6.1 us
    ppermute x7, waiting for transfers between devices, body(): lax.ppermute(block, 'replica', [(i, (i + k) % replicas) for i in range(re...  5.93 us
    ppermute x3, starting transfers between devices, body(): lax.ppermute(x, 'replica', [(i, i ^ bit) for i in range(replicas)])  4.73 us
    ppermute x1, waiting for transfers between devices, body(): got_moved = lax.ppermute(crossed_moved, 'tensor', across)  4.6 us
    ppermute x3, waiting for transfers between devices, body(): lax.ppermute(x, 'replica', [(i, i ^ bit) for i in range(replicas)])  3.27 us
    pallas_call x1, Pallas kernels, exchange_pack(): pl.pallas_call(functools.partial(pack_kernel, replicas=replicas, moved=mo...  2.91 us
  transfers between devices with their start and end apart: 16, of which 10 were waited for; matrix products, arithmetic and copies ran while one was open for 0% of the time, Pallas kernels for 26%

profile of v7, /device:TPU:0, one launch (start us, length us, event | category | flops | bytes accessed | tf_op | source)
XLA Modules:
  0.0 65.1 jit_solution(14314187959358436087)
XLA Ops:
  0.5 2.9 %pack.1 = (bf16[288,128]{1,0:T(8,128)(2,1)S(1)}, bf16[288,128]{1,0:T(8,128)(2,1)S(1)}, bf16[288,128]{1,0:T(8,128)(2,1)S(1)}, bf16[288,128]{1,0:T(8,128)(2,1)S(1)...) custom-call(s32[4,8]{1,0:T(4,128)} %bitcast.16, ...), custom_call_target="tpu_custom_call" | custom-call | tf_op jit(solution)/shard_map/pack/pallas_call | solution.py:579
  3.4 2.6 %collective-permute-start.1 = (bf16[288,128]{1,0:T(8,128)(2,1)S(1)}, bf16[288,128]{1,0:T(8,128)(2,1)S(1)}, u32[]{:S(2)}, u32[]{:S(2)}) collective-permute-start(bf16[288,128]{1,0:T(8,128)(2,1)S(1)} %get-tuple-element.27), channel_id=1, source_target_pairs={{0,4},{4,8},{8,12},{12,16},{16,20},{20,24},{24,28},{28,0},{1,5},{5... | collective-permute-start | bytes 221192 | tf_op jit(solution)/shard_map/ppermute | solution.py:670
  5.9 1.6 %collective-permute-start.2 = (bf16[288,128]{1,0:T(8,128)(2,1)S(1)}, bf16[288,128]{1,0:T(8,128)(2,1)S(1)}, u32[]{:S(2)}, u32[]{:S(2)}) collective-permute-start(bf16[288,128]{1,0:T(8,128)(2,1)S(1)} %get-tuple-element.28), channel_id=1, source_target_pairs={{0,8},{4,12},{8,16},{12,20},{16,24},{20,28},{24,0},{28,4},{1,9},{5... | collective-permute-start | bytes 221192 | tf_op jit(solution)/shard_map/ppermute | solution.py:670
  7.5 2.5 %collective-permute-start.3 = (bf16[288,128]{1,0:T(8,128)(2,1)S(1)}, bf16[288,128]{1,0:T(8,128)(2,1)S(1)}, u32[]{:S(2)}, u32[]{:S(2)}) collective-permute-start(bf16[288,128]{1,0:T(8,128)(2,1)S(1)} %get-tuple-element.29), channel_id=1, source_target_pairs={{0,12},{4,16},{8,20},{12,24},{16,28},{20,0},{24,4},{28,8},{1,13},{... | collective-permute-start | bytes 221192 | tf_op jit(solution)/shard_map/ppermute | solution.py:670
  10.1 1.2 %collective-permute-start.4 = (bf16[288,128]{1,0:T(8,128)(2,1)S(1)}, bf16[288,128]{1,0:T(8,128)(2,1)S(1)}, u32[]{:S(2)}, u32[]{:S(2)}) collective-permute-start(bf16[288,128]{1,0:T(8,128)(2,1)S(1)} %get-tuple-element.30), channel_id=1, source_target_pairs={{0,16},{4,20},{8,24},{12,28},{16,0},{20,4},{24,8},{28,12},{1,17},{... | collective-permute-start | bytes 221192 | tf_op jit(solution)/shard_map/ppermute | solution.py:670
  11.3 0.8 %collective-permute-done.1.rest_0_ = bf16[288,128]{1,0:T(8,128)(2,1)S(1)} collective-permute-done((bf16[288,128]{1,0:T(8,128)(2,1)S(1)}, bf16[288,128]{1,0:T(8,128)(2,1)S(1)}, u32[]{:S(2)}, u32[]{:S(2)}) %collective-permute-start.1) | collective-permute-done | bytes 73760 | tf_op jit(solution)/shard_map/ppermute | solution.py:670
  12.1 1.8 %collective-permute-start.5 = (bf16[288,128]{1,0:T(8,128)(2,1)S(1)}, bf16[288,128]{1,0:T(8,128)(2,1)S(1)}, u32[]{:S(2)}, u32[]{:S(2)}) collective-permute-start(bf16[288,128]{1,0:T(8,128)(2,1)S(1)} %get-tuple-element.31), channel_id=1, source_target_pairs={{0,20},{4,24},{8,28},{12,0},{16,4},{20,8},{24,12},{28,16},{1,21},{... | collective-permute-start | bytes 221192 | tf_op jit(solution)/shard_map/ppermute | solution.py:670
  13.9 1.4 %collective-permute-start.6 = (bf16[288,128]{1,0:T(8,128)(2,1)S(1)}, bf16[288,128]{1,0:T(8,128)(2,1)S(1)}, u32[]{:S(2)}, u32[]{:S(2)}) collective-permute-start(bf16[288,128]{1,0:T(8,128)(2,1)S(1)} %get-tuple-element.32), channel_id=1, source_target_pairs={{0,24},{4,28},{8,0},{12,4},{16,8},{20,12},{24,16},{28,20},{1,25},{... | collective-permute-start | bytes 221192 | tf_op jit(solution)/shard_map/ppermute | solution.py:670
  15.3 3.1 %collective-permute-done.3.rest_2_ = bf16[288,128]{1,0:T(8,128)(2,1)S(1)} collective-permute-done((bf16[288,128]{1,0:T(8,128)(2,1)S(1)}, bf16[288,128]{1,0:T(8,128)(2,1)S(1)}, u32[]{:S(2)}, u32[]{:S(2)}) %collective-permute-start.3) | collective-permute-done | bytes 73760 | tf_op jit(solution)/shard_map/ppermute | solution.py:670
  18.4 2.4 %collective-permute-start.7 = (bf16[288,128]{1,0:T(8,128)(2,1)S(1)}, bf16[288,128]{1,0:T(8,128)(2,1)S(1)}, u32[]{:S(2)}, u32[]{:S(2)}) collective-permute-start(bf16[288,128]{1,0:T(8,128)(2,1)S(1)} %get-tuple-element.33), channel_id=1, source_target_pairs={{0,28},{4,0},{8,4},{12,8},{16,12},{20,16},{24,20},{28,24},{1,29},{... | collective-permute-start | bytes 221192 | tf_op jit(solution)/shard_map/ppermute | solution.py:670
  21.2 0.5 collective-permute-done.6.rest_5_
  21.7 1.0 %collective-permute-done.7.rest_6_ = bf16[288,128]{1,0:T(8,128)(2,1)S(1)} collective-permute-done((bf16[288,128]{1,0:T(8,128)(2,1)S(1)}, bf16[288,128]{1,0:T(8,128)(2,1)S(1)}, u32[]{:S(2)}, u32[]{:S(2)}) %collective-permute-start.7) | collective-permute-done | bytes 73760 | tf_op jit(solution)/shard_map/ppermute | solution.py:670
  22.8 6.1 %attend_first.1 = (bf16[272,640]{1,0:T(8,128)(2,1)S(1)}, bf16[512,128]{1,0:T(8,128)(2,1)S(1)}, bf16[512,128]{1,0:T(8,128)(2,1)S(1)}, bf16[1280,1280]{1,0:T(8,128)(2,1)S(1)}) custom-call(s32[4,8]{1,0:T(4,128)} %bitcast.17, s32[18]{0:T(128)} %copy-done, s32[32]{0:T(128)} %prompt_lengths.3, s32[8,128]{1,0:T(8,128)} %bitcast.19, s32[8,128]{1,0:T(8,128)} %bitcast.21, ...), custom_call_target="tpu_custom_call" | custom-call | flops 1 | bytes 1 | tf_op jit(solution)/shard_map/attend_first/pallas_call | solution.py:700
  29.0 1.6 %collective-permute-done.8.h_sib.s_first = bf16[272,640]{1,0:T(8,128)(2,1)S(1)} collective-permute-done((bf16[272,640]{1,0:T(8,128)(2,1)S(1)}, bf16[272,640]{1,0:T(8,128)(2,1)S(1)}, u32[]{:S(2)}, u32[]{:S(2)}) %collective-permute-start.8) | collective-permute-done | bytes 348192 | tf_op jit(solution)/shard_map/ppermute | solution.py:731
  30.6 1.0 %project.2.after = bf16[256,1280]{1,0:T(8,128)(2,1)S(1)} custom-call(bf16[272,640]{1,0:T(8,128)(2,1)S(1)} %get-tuple-element.34.h_own.h_first, bf16[272,640]{1,0:T(8,128)(2,1)S(1)} %collective-permute-done.8.h_sib.s_first, bf16[1280,1280]{1,0:T(8,128)(2,1)S(1)} %get-tuple-element.37.weights.w_there), custom_call_target="tpu_custom_call" | custom-call | flops 1 | bytes 1 | tf_op jit(solution)/shard_map/project/pallas_call | solution.py:719
  31.6 1.6 %collective-permute-start.13 = (bf16[256,1280]{1,0:T(8,128)(2,1)S(1)}, bf16[256,1280]{1,0:T(8,128)(2,1)S(1)}, u32[]{:S(2)}, u32[]{:S(2)}) collective-permute-start(bf16[256,1280]{1,0:T(8,128)(2,1)S(1)} %project.2.after), channel_id=1, source_target_pairs={{0,2},{1,3},{2,0},{3,1},{4,6},{5,7},{6,4},{7,5},{8,10},{9,11},{10,... | collective-permute-start | bytes 1966088 | tf_op jit(solution)/shard_map/ppermute | solution.py:733
  33.2 5.1 %attend_second.1.h_second.h_own = bf16[256,640]{1,0:T(8,128)(2,1)S(1)} custom-call(s32[4,8]{1,0:T(4,128)} %bitcast.18, s32[32]{0:T(128)} %prompt_lengths.3, s32[8,128]{1,0:T(8,128)} %bitcast.20, s32[8,128]{1,0:T(8,128)} %bitcast.22, s32[8,128]{1,0:T(8,128)} %bitcast.24, bf16[512,128]{1,0:T(8,128)(2,1)S(1)} %get-tuple-element.35.pk, ...), custom_call_target="tpu_custom_call" | custom-call | flops 1 | bytes 1 | tf_op jit(solution)/shard_map/attend_second/pallas_call | solution.py:719
  38.3 0.7 %moved_send.1 = (bf16[4,4,1280]{2,1,0:T(4,128)(2,1)S(1)}, bf16[4,4,1280]{2,1,0:T(4,128)(2,1)S(1)}) custom-call(s32[18]{0:T(128)} %copy-done, bf16[272,640]{1,0:T(8,128)(2,1)S(1)} %get-tuple-element.34.h_own.h_first, bf16[272,640]{1,0:T(8,128)(2,1)S(1)} %collective-permute-done.8.h_sib.s_first, bf16[256,1280]{1,0:T(8,128)(2,1)S(1)} %project.2.after), custom_call_target="tpu_custom_call" | custom-call | flops 1 | bytes 1 | tf_op jit(solution)/shard_map/moved_send/pallas_call | solution.py:719
  39.1 1.3 %collective-permute-start.11 = (bf16[4,4,1280]{2,1,0:T(4,128)(2,1)S(1)}, bf16[4,4,1280]{2,1,0:T(4,128)(2,1)S(1)}, u32[]{:S(2)}, u32[]{:S(2)}) collective-permute-start(bf16[4,4,1280]{2,1,0:T(4,128)(2,1)S(1)} %get-tuple-element.41), channel_id=1, source_target_pairs={{0,4},{4,0},{8,12},{12,8},{16,20},{20,16},{24,28},{28,24},{1,5},{5... | collective-permute-start | bytes 122888 | tf_op jit(solution)/shard_map/ppermute | solution.py:757
  40.4 1.1 %project.3 = bf16[256,1280]{1,0:T(8,128)(2,1)S(1)} custom-call(bf16[256,640]{1,0:T(8,128)(2,1)S(1)} %attend_second.1.h_second.h_own, bf16[256,640]{1,0:T(8,128)(2,1)S(1)} %collective-permute-done.9.s_second.h_sib, bf16[1280,1280]{1,0:T(8,128)(2,1)S(1)} %get-tuple-element.37.weights.w_there), custom_call_target="tpu_custom_call" | custom-call | flops 1 | bytes 1 | tf_op jit(solution)/shard_map/project/pallas_call | solution.py:719
  41.4 1.7 %collective-permute-done.11.rest_0_ = bf16[4,4,1280]{2,1,0:T(4,128)(2,1)S(1)} collective-permute-done((bf16[4,4,1280]{2,1,0:T(4,128)(2,1)S(1)}, bf16[4,4,1280]{2,1,0:T(4,128)(2,1)S(1)}, u32[]{:S(2)}, u32[]{:S(2)}) %collective-permute-start.11) | collective-permute-done | bytes 40992 | tf_op jit(solution)/shard_map/ppermute | solution.py:757
  43.2 1.9 %collective-permute-start.12 = (bf16[4,4,1280]{2,1,0:T(4,128)(2,1)S(1)}, bf16[4,4,1280]{2,1,0:T(4,128)(2,1)S(1)}, u32[]{:S(2)}, u32[]{:S(2)}) collective-permute-start(bf16[4,4,1280]{2,1,0:T(4,128)(2,1)S(1)} %pad_maximum_fusion), channel_id=1, source_target_pairs={{0,8},{4,12},{8,0},{12,4},{16,24},{20,28},{24,16},{28,20},{1,9},{5... | collective-permute-start | bytes 122888 | tf_op jit(solution)/shard_map/ppermute | solution.py:757
  45.1 0.6 collective-permute-start.10
  45.7 1.6 %collective-permute-done.12.rest_1_ = bf16[4,4,1280]{2,1,0:T(4,128)(2,1)S(1)} collective-permute-done((bf16[4,4,1280]{2,1,0:T(4,128)(2,1)S(1)}, bf16[4,4,1280]{2,1,0:T(4,128)(2,1)S(1)}, u32[]{:S(2)}, u32[]{:S(2)}) %collective-permute-start.12) | collective-permute-done | bytes 40992 | tf_op jit(solution)/shard_map/ppermute | solution.py:757
  47.3 2.0 %collective-permute-done.13.recv = bf16[256,1280]{1,0:T(8,128)(2,1)S(1)} collective-permute-done((bf16[256,1280]{1,0:T(8,128)(2,1)S(1)}, bf16[256,1280]{1,0:T(8,128)(2,1)S(1)}, u32[]{:S(2)}, u32[]{:S(2)}) %collective-permute-start.13) | collective-permute-done | bytes 655392 | tf_op jit(solution)/shard_map/ppermute | solution.py:733
  49.3 1.6 %collective-permute-start.14 = (bf16[4,4,1280]{2,1,0:T(4,128)(2,1)S(1)}, bf16[4,4,1280]{2,1,0:T(4,128)(2,1)S(1)}, u32[]{:S(2)}, u32[]{:S(2)}) collective-permute-start(bf16[4,4,1280]{2,1,0:T(4,128)(2,1)S(1)} %pad_maximum_fusion.1), channel_id=1, source_target_pairs={{0,16},{4,20},{8,24},{12,28},{16,0},{20,4},{24,8},{28,12},{1,17},{... | collective-permute-start | bytes 122888 | tf_op jit(solution)/shard_map/ppermute | solution.py:757
  50.9 4.6 %base.1 = (f32[512,1280]{1,0:T(8,128)S(1)}, bf16[1280,1280]{1,0:T(8,128)(2,1)S(1)}, f32[16,1280]{1,0:T(8,128)S(1)}) custom-call(s32[18]{0:T(128)} %copy-done, bf16[272,640]{1,0:T(8,128)(2,1)S(1)} %get-tuple-element.34.h_own.h_first, bf16[272,640]{1,0:T(8,128)(2,1)S(1)} %collective-permute-done.8.h_sib.s_first, ...), custom_call_target="tpu_custom_call" | custom-call | flops 1 | bytes 1 | tf_op jit(solution)/shard_map/base/pallas_call | solution.py:719
  55.5 1.8 %moved_project.1 = (bf16[16,1280]{1,0:T(8,128)(2,1)S(1)}, f32[16,1280]{1,0:T(8,128)S(1)}) custom-call(s32[18]{0:T(128)} %copy-done, bf16[1280,1280]{1,0:T(8,128)(2,1)S(1)} %get-tuple-element.39.w_here, bf16[1280,1280]{1,0:T(8,128)(2,1)S(1)} %get-tuple-element.37.weights.w_there, f32[16,1280]{1,0:T(8,128)S(1)} %get-tuple-element.40.before, ...), custom_call_target="tpu_custom_call" | custom-call | flops 1 | bytes 1 | tf_op jit(solution)/shard_map/moved_project/pallas_call | solution.py:719
  57.3 0.6 collective-permute-start.15
  57.9 0.9 %finish_first.1.earlier = bf16[128,4,1280]{2,1,0:T(4,128)(2,1)} custom-call(f32[512,1280]{1,0:T(8,128)S(1)} %get-tuple-element.38.base, bf16[256,1280]{1,0:T(8,128)(2,1)S(1)} %collective-permute-done.13.recv), custom_call_target="tpu_custom_call" | custom-call | tf_op jit(solution)/shard_map/finish_first/pallas_call | solution.py:784
  58.8 4.6 %collective-permute-done.15.recv_moved = bf16[16,1280]{1,0:T(8,128)(2,1)S(1)} collective-permute-done((bf16[16,1280]{1,0:T(8,128)(2,1)S(1)}, bf16[16,1280]{1,0:T(8,128)(2,1)S(1)}, u32[]{:S(2)}, u32[]{:S(2)}) %collective-permute-start.15) | collective-permute-done | bytes 40992 | tf_op jit(solution)/shard_map/ppermute | solution.py:781
  63.4 1.7 %finish_second.1 = bf16[128,4,1280]{2,1,0:T(4,128)(2,1)} custom-call(s32[18]{0:T(128)} %copy-done, f32[512,1280]{1,0:T(8,128)S(1)} %get-tuple-element.38.base, bf16[256,1280]{1,0:T(8,128)(2,1)S(1)} %collective-permute-done.10.recv, f32[16,1280]{1,0:T(8,128)S(1)} %get-tuple-element.45.base_moved, ...), custom_call_target="tpu_custom_call", output_to_operand_aliasing={{}: (5, {})} | custom-call | tf_op jit(solution)/shard_map/finish_second/pallas_call | solution.py:793
  (19 shorter events, 1.1 us)
Async XLA Ops:
  0.0 22.8 %collective-permute-start = (bf16[640,5120]{1,0:T(8,128)(2,1)}, bf16[640,5120]{1,0:T(8,128)(2,1)S(1)}, u32[]{:S(2)}, u32[]{:S(2)}) collective-permute-start(bf16[640,5120]{1,0:T(8,128)(2,1)} %w_own.3), channel_id=1, source_target_pairs={{0,1},{1,0},{2,3},{3,2},{4,5},{5,4},{6,7},{7,6},{8,9},{9,8},{10,11... | collective-permute-start | bytes 19660808 | tf_op jit(solution)/shard_map/ppermute | solution.py:655
  3.4 6.7 %copy-start = (s32[18]{0:T(128)}, s32[18]{0:T(128)S(1)}, u32[]{:S(2)}) copy-start(s32[18]{0:T(128)S(1)} %get-tuple-element.26.pairs) | copy-start | bytes 220
  3.4 8.7 %collective-permute-start.1 = (bf16[288,128]{1,0:T(8,128)(2,1)S(1)}, bf16[288,128]{1,0:T(8,128)(2,1)S(1)}, u32[]{:S(2)}, u32[]{:S(2)}) collective-permute-start(bf16[288,128]{1,0:T(8,128)(2,1)S(1)} %get-tuple-element.27), channel_id=1, source_target_pairs={{0,4},{4,8},{8,12},{12,16},{16,20},{20,24},{24,28},{28,0},{1,5},{5... | collective-permute-start | bytes 221192 | tf_op jit(solution)/shard_map/ppermute | solution.py:670
  5.9 8.0 %collective-permute-start.2 = (bf16[288,128]{1,0:T(8,128)(2,1)S(1)}, bf16[288,128]{1,0:T(8,128)(2,1)S(1)}, u32[]{:S(2)}, u32[]{:S(2)}) collective-permute-start(bf16[288,128]{1,0:T(8,128)(2,1)S(1)} %get-tuple-element.28), channel_id=1, source_target_pairs={{0,8},{4,12},{8,16},{12,20},{16,24},{20,28},{24,0},{28,4},{1,9},{5... | collective-permute-start | bytes 221192 | tf_op jit(solution)/shard_map/ppermute | solution.py:670
  7.5 10.9 %collective-permute-start.3 = (bf16[288,128]{1,0:T(8,128)(2,1)S(1)}, bf16[288,128]{1,0:T(8,128)(2,1)S(1)}, u32[]{:S(2)}, u32[]{:S(2)}) collective-permute-start(bf16[288,128]{1,0:T(8,128)(2,1)S(1)} %get-tuple-element.29), channel_id=1, source_target_pairs={{0,12},{4,16},{8,20},{12,24},{16,28},{20,0},{24,4},{28,8},{1,13},{... | collective-permute-start | bytes 221192 | tf_op jit(solution)/shard_map/ppermute | solution.py:670
  10.1 10.7 %collective-permute-start.4 = (bf16[288,128]{1,0:T(8,128)(2,1)S(1)}, bf16[288,128]{1,0:T(8,128)(2,1)S(1)}, u32[]{:S(2)}, u32[]{:S(2)}) collective-permute-start(bf16[288,128]{1,0:T(8,128)(2,1)S(1)} %get-tuple-element.30), channel_id=1, source_target_pairs={{0,16},{4,20},{8,24},{12,28},{16,0},{20,4},{24,8},{28,12},{1,17},{... | collective-permute-start | bytes 221192 | tf_op jit(solution)/shard_map/ppermute | solution.py:670
  12.1 9.1 %collective-permute-start.5 = (bf16[288,128]{1,0:T(8,128)(2,1)S(1)}, bf16[288,128]{1,0:T(8,128)(2,1)S(1)}, u32[]{:S(2)}, u32[]{:S(2)}) collective-permute-start(bf16[288,128]{1,0:T(8,128)(2,1)S(1)} %get-tuple-element.31), channel_id=1, source_target_pairs={{0,20},{4,24},{8,28},{12,0},{16,4},{20,8},{24,12},{28,16},{1,21},{... | collective-permute-start | bytes 221192 | tf_op jit(solution)/shard_map/ppermute | solution.py:670
  13.9 7.8 %collective-permute-start.6 = (bf16[288,128]{1,0:T(8,128)(2,1)S(1)}, bf16[288,128]{1,0:T(8,128)(2,1)S(1)}, u32[]{:S(2)}, u32[]{:S(2)}) collective-permute-start(bf16[288,128]{1,0:T(8,128)(2,1)S(1)} %get-tuple-element.32), channel_id=1, source_target_pairs={{0,24},{4,28},{8,0},{12,4},{16,8},{20,12},{24,16},{28,20},{1,25},{... | collective-permute-start | bytes 221192 | tf_op jit(solution)/shard_map/ppermute | solution.py:670
  18.4 4.4 %collective-permute-start.7 = (bf16[288,128]{1,0:T(8,128)(2,1)S(1)}, bf16[288,128]{1,0:T(8,128)(2,1)S(1)}, u32[]{:S(2)}, u32[]{:S(2)}) collective-permute-start(bf16[288,128]{1,0:T(8,128)(2,1)S(1)} %get-tuple-element.33), channel_id=1, source_target_pairs={{0,28},{4,0},{8,4},{12,8},{16,12},{20,16},{24,20},{28,24},{1,29},{... | collective-permute-start | bytes 221192 | tf_op jit(solution)/shard_map/ppermute | solution.py:670
  28.9 1.7 %collective-permute-start.8 = (bf16[272,640]{1,0:T(8,128)(2,1)S(1)}, bf16[272,640]{1,0:T(8,128)(2,1)S(1)}, u32[]{:S(2)}, u32[]{:S(2)}) collective-permute-start(bf16[272,640]{1,0:T(8,128)(2,1)S(1)} %get-tuple-element.34.h_own.h_first), channel_id=1, source_target_pairs={{0,1},{1,0},{2,3},{3,2},{4,5},{5,4},{6,7},{7,6},{8,9},{9,8},{10,11... | collective-permute-start | bytes 1044488 | tf_op jit(solution)/shard_map/ppermute | solution.py:731
  31.6 17.6 %collective-permute-start.13 = (bf16[256,1280]{1,0:T(8,128)(2,1)S(1)}, bf16[256,1280]{1,0:T(8,128)(2,1)S(1)}, u32[]{:S(2)}, u32[]{:S(2)}) collective-permute-start(bf16[256,1280]{1,0:T(8,128)(2,1)S(1)} %project.2.after), channel_id=1, source_target_pairs={{0,2},{1,3},{2,0},{3,1},{4,6},{5,7},{6,4},{7,5},{8,10},{9,11},{10,... | collective-permute-start | bytes 1966088 | tf_op jit(solution)/shard_map/ppermute | solution.py:733
  38.3 2.1 %collective-permute-start.9 = (bf16[256,640]{1,0:T(8,128)(2,1)S(1)}, bf16[256,640]{1,0:T(8,128)(2,1)S(1)}, u32[]{:S(2)}, u32[]{:S(2)}) collective-permute-start(bf16[256,640]{1,0:T(8,128)(2,1)S(1)} %attend_second.1.h_second.h_own), channel_id=1, source_target_pairs={{0,1},{1,0},{2,3},{3,2},{4,5},{5,4},{6,7},{7,6},{8,9},{9,8},{10,11... | collective-permute-start | bytes 983048 | tf_op jit(solution)/shard_map/ppermute | solution.py:731
  39.1 4.1 %collective-permute-start.11 = (bf16[4,4,1280]{2,1,0:T(4,128)(2,1)S(1)}, bf16[4,4,1280]{2,1,0:T(4,128)(2,1)S(1)}, u32[]{:S(2)}, u32[]{:S(2)}) collective-permute-start(bf16[4,4,1280]{2,1,0:T(4,128)(2,1)S(1)} %get-tuple-element.41), channel_id=1, source_target_pairs={{0,4},{4,0},{8,12},{12,8},{16,20},{20,16},{24,28},{28,24},{1,5},{5... | collective-permute-start | bytes 122888 | tf_op jit(solution)/shard_map/ppermute | solution.py:757
  43.2 4.1 %collective-permute-start.12 = (bf16[4,4,1280]{2,1,0:T(4,128)(2,1)S(1)}, bf16[4,4,1280]{2,1,0:T(4,128)(2,1)S(1)}, u32[]{:S(2)}, u32[]{:S(2)}) collective-permute-start(bf16[4,4,1280]{2,1,0:T(4,128)(2,1)S(1)} %pad_maximum_fusion), channel_id=1, source_target_pairs={{0,8},{4,12},{8,0},{12,4},{16,24},{20,28},{24,16},{28,20},{1,9},{5... | collective-permute-start | bytes 122888 | tf_op jit(solution)/shard_map/ppermute | solution.py:757
  45.1 18.3 %collective-permute-start.10 = (bf16[256,1280]{1,0:T(8,128)(2,1)S(1)}, bf16[256,1280]{1,0:T(8,128)(2,1)S(1)}, u32[]{:S(2)}, u32[]{:S(2)}) collective-permute-start(bf16[256,1280]{1,0:T(8,128)(2,1)S(1)} %project.3), channel_id=1, source_target_pairs={{0,2},{1,3},{2,0},{3,1},{4,6},{5,7},{6,4},{7,5},{8,10},{9,11},{10,... | collective-permute-start | bytes 1966088 | tf_op jit(solution)/shard_map/ppermute | solution.py:733
  49.3 6.1 %collective-permute-start.14 = (bf16[4,4,1280]{2,1,0:T(4,128)(2,1)S(1)}, bf16[4,4,1280]{2,1,0:T(4,128)(2,1)S(1)}, u32[]{:S(2)}, u32[]{:S(2)}) collective-permute-start(bf16[4,4,1280]{2,1,0:T(4,128)(2,1)S(1)} %pad_maximum_fusion.1), channel_id=1, source_target_pairs={{0,16},{4,20},{8,24},{12,28},{16,0},{20,4},{24,8},{28,12},{1,17},{... | collective-permute-start | bytes 122888 | tf_op jit(solution)/shard_map/ppermute | solution.py:757
  57.3 6.1 %collective-permute-start.15 = (bf16[16,1280]{1,0:T(8,128)(2,1)S(1)}, bf16[16,1280]{1,0:T(8,128)(2,1)S(1)}, u32[]{:S(2)}, u32[]{:S(2)}) collective-permute-start(bf16[16,1280]{1,0:T(8,128)(2,1)S(1)} %get-tuple-element.46), channel_id=1, source_target_pairs={{0,2},{1,3},{2,0},{3,1},{4,6},{5,7},{6,4},{7,5},{8,10},{9,11},{10,... | collective-permute-start | bytes 122888 | tf_op jit(solution)/shard_map/ppermute | solution.py:781
